TPU v7x, 32 devices: a whole 2x2x4 slice. The times are simulated.
32 devices in a mesh: parts: 2 (over x), ep: 2 (over core), shadow: 8 (over z, y).
Axes of the slice: x: 2, y: 2, z: 4, core: 2. Of those that a mesh axis runs over, the one named last changes fastest.
Arguments:
- hot_root: int32 [4], P('parts'), parts along dimension 0, may hold values from 0 to 7
- res_rows: bfloat16 [24576, 2048], P(('parts', 'ep', 'shadow')), parts along dimension 0, may hold values from -6 to 6
- res_weight: float32 [24576], P(('parts', 'ep', 'shadow')), parts along dimension 0, may hold values from 0.2 to 1
- cold_rows: bfloat16 [2048, 2048], P(('parts', 'ep', 'shadow')), parts along dimension 0, may hold values from -6 to 6
- cold_experts: int32 [2048, 2], P(('parts', 'ep', 'shadow')), parts along dimension 0, may hold values from 0 to 15, all different within a row; in each aligned block of 64 rows (0 to 63, 64 to 127, ...) at most 16 rows name the same one
- cold_weights: float32 [2048, 2], P(('parts', 'ep', 'shadow')), parts along dimension 0, may hold values from 0.2 to 1
- w_gate_up: bfloat16 [16, 2048, 1024], P(('ep', 'shadow')), may hold values from -0.125 to 0.125
- w_down: bfloat16 [16, 512, 2048], P(('ep', 'shadow')), may hold values from -0.25 to 0.25
Outputs:
- hot_out: bfloat16 [24576, 2048], P(('parts', 'ep', 'shadow')), parts along dimension 0
- cold_out: bfloat16 [2048, 2048], P(('parts', 'ep', 'shadow')), parts along dimension 0
There are 2 independent parts, one for each index of `parts`. A program takes and returns all parts, laid end to end along the dimension named above; an argument that names none is the same for every part. Nothing has to cross between parts.
Inputs may be any that keep to these rules, and one draw needn't show every extreme that they name: `cold_experts`: within the rows of one device no expert is named by more than 16 routes, a bound that some block reaches; the 2 experts of a row differ; every expert is named somewhere in a part.
All inputs are finite; a program needn't handle non-finite values.
Results may differ from a plain program's by a relative error of at most 0.0058.
Values may be sent and summed in bfloat16 or wider, within the bound.
No kernel may reach another device: no remote copies, remote signals or barrier semaphores. Data moves between devices by JAX's collectives and lax.ppermute only.
A program may use at most 64 MiB of HBM per device.

v0:
```python
import jax
import jax.numpy as jnp
from jax import lax
from jax.sharding import PartitionSpec as P


def broadcast(value, axis, source):
    kept = jnp.where(lax.axis_index(axis) == source, value, 0).astype(value.dtype)
    return lax.psum(kept, axis)


def expert_apply(group_rows, gate_up, down_proj):
    hidden_units = down_proj.shape[0]
    pre_act = jnp.dot(group_rows, gate_up, preferred_element_type=jnp.float32)
    hidden = (jax.nn.silu(pre_act[:, :hidden_units]) * pre_act[:, hidden_units:]).astype(
        jnp.bfloat16
    )
    return jnp.dot(hidden, down_proj, preferred_element_type=jnp.float32)


def body(hot_root, res_rows, res_weight, cold_rows, cold_experts, cold_weights, w_gate_up, w_down):
    own_gate_up = w_gate_up[0]
    own_down = w_down[0]
    group_index = lax.axis_index("ep")
    root_index = hot_root[group_index]
    n_groups = lax.axis_size("ep")
    n_shadows = lax.axis_size("shadow")
    n_owners = n_groups * n_shadows
    per_device = cold_rows.shape[0]
    fan_out = cold_experts.shape[1]
    width = cold_rows.shape[1]
    capacity = max(2, 2 * per_device * fan_out // n_owners)
    flat_routes = cold_experts.reshape(-1)
    onehot = (flat_routes[:, None] == jnp.arange(n_owners, dtype=jnp.int32)[None, :]).astype(
        jnp.int32
    )
    route_rank = jnp.sum((jnp.cumsum(onehot, axis=0) - 1) * onehot, axis=1)
    slot_ids = flat_routes * capacity + route_rank
    sources = jnp.repeat(cold_rows, fan_out, axis=0)
    outgoing = jnp.zeros((n_owners * capacity, width), jnp.bfloat16).at[slot_ids].set(sources)
    sectioned = outgoing.reshape(n_groups, n_shadows, capacity, width)
    arrived = lax.all_to_all(
        lax.all_to_all(sectioned, "ep", split_axis=0, concat_axis=0, tiled=True),
        "shadow",
        split_axis=1,
        concat_axis=1,
        tiled=True,
    )
    shape_now = arrived.shape
    served = expert_apply(arrived.reshape(-1, width), own_gate_up, own_down).astype(jnp.bfloat16)
    answered = served.reshape(shape_now)
    returned = lax.all_to_all(
        lax.all_to_all(answered, "ep", split_axis=0, concat_axis=0, tiled=True),
        "shadow",
        split_axis=1,
        concat_axis=1,
        tiled=True,
    )
    returned = returned.reshape(n_owners * capacity, width)
    picked = returned[slot_ids].astype(jnp.float32) * cold_weights.reshape(-1)[:, None]
    cold_out = jnp.sum(picked.reshape(per_device, fan_out, width), axis=1).astype(jnp.bfloat16)
    hot_gate_up = broadcast(own_gate_up, "shadow", root_index)
    hot_down = broadcast(own_down, "shadow", root_index)
    hot_total = expert_apply(res_rows, hot_gate_up, hot_down)
    hot_out = (hot_total * res_weight[:, None]).astype(jnp.bfloat16)
    return (hot_out, cold_out)


def solution(mesh):
    in_specs = (
        P("parts"),
        P(("parts", "ep", "shadow"), None),
        P(("parts", "ep", "shadow")),
        P(("parts", "ep", "shadow"), None),
        P(("parts", "ep", "shadow"), None),
        P(("parts", "ep", "shadow"), None),
        P(("ep", "shadow"), None, None),
        P(("ep", "shadow"), None, None),
    )
    out_specs = (P(("parts", "ep", "shadow"), None), P(("parts", "ep", "shadow"), None))
    return jax.shard_map(body, mesh=mesh, in_specs=in_specs, out_specs=out_specs, check_vma=False)
```

profile of v0, /device:TPU:0, one launch (start us, length us, event | category | flops | bytes accessed | tf_op | source)
XLA Modules:
  0.0 287.0 jit_solution(9341460776118302856)
XLA Ops:
  7.2 0.0 copy-start
  7.2 0.0 all-reduce.3.cloned.1.call-start
  7.2 1.4 dynamic_slice.3
  9.3 0.0 copy-start.2
  9.3 4.6 %bitcast_select_fusion = bf16[2048,1024]{1,0:T(8,128)(2,1)} fusion(bf16[1,2048,1024]{2,1,0:T(8,128)(2,1)} %param.14, pred[]{:T(512)S(6)} %eq.19), kind=kLoop, calls=%fused_computation.5 | loop fusion | flops 2097152 | bytes 8388609 | tf_op jit(solution)/shard_map/jit(_where)/select_n | solution.py:8
  13.9 0.0 copy-done.2
  13.9 1.5 bitcast_select_fusion.1
  15.3 0.0 copy-start.5
  15.3 0.0 copy-start.4
  15.3 0.0 all-reduce.3.cloned.1.call-update
  15.4 0.7 copy-done.5
  16.0 0.1 copy.29
  16.1 0.1 eq.20
  16.2 0.1 fusion.11
  16.3 0.2 reduce_window_sum.11
  16.5 0.1 copy.28
  16.6 0.1 mul.56
  16.8 0.0 copy-done.4
  16.8 1.1 broadcast_in_dim.21
  17.9 2.1 reshape.78
  19.9 0.2 select_reduce_fusion
  20.1 3.0 %scatter_custom_fusion = bf16[256,2048]{1,0:T(8,128)(2,1)} fusion(s32[128]{0:T(128)S(1)} %fusion.12, bf16[128,2048]{1,0:T(8,128)(2,1)} %reshape.78, bf16[]{:T(256)} %constant.29.clone.1), kind=kCustom, calls=%fused_computation.16 | custom fusion | bytes 1049088 | tf_op jit(solution)/shard_map/scatter | solution.py:40
  23.1 5.7 %all_to_all.20 = bf16[2,8,16,2048]{3,2,1,0:T(8,128)(2,1)S(1)} all-to-all(bf16[2,8,16,2048]{3,2,1,0:T(8,128)(2,1)} %bitcast.26), channel_id=1, replica_groups=mesh['parts'=2,'ep'=2,'shadow'=8] {'ep'}, dimensions={0} | all-to-all | bytes 2097152 | tf_op jit(solution)/shard_map/all_to_all | solution.py:43
  28.8 0.0 copy-start.1
  28.8 0.1 copy.30
  28.8 59.8 %all_to_all.21 = bf16[2,8,16,2048]{3,2,0,1:T(8,128)(2,1)S(1)} all-to-all(bf16[2,8,16,2048]{3,2,0,1:T(8,128)(2,1)S(1)} %copy.30), channel_id=1, replica_groups=mesh['parts'=2,'ep'=2,'shadow'=8] {'shadow'}, dimensions={1} | all-to-all | bytes 2097152 | tf_op jit(solution)/shard_map/all_to_all | solution.py:42
  88.6 0.1 copy.31
  88.7 0.0 copy-done.1
  88.7 0.0 copy-start.3
  88.7 1.3 fusion
  90.0 0.3 copy-done.3
  90.3 0.8 convolution_convert_fusion
  91.1 0.0 copy-start.6
  91.1 4.6 %all_to_all.22 = bf16[2,8,16,2048]{3,2,1,0:T(8,128)(2,1)S(1)} all-to-all(bf16[2,8,16,2048]{3,2,1,0:T(8,128)(2,1)S(1)} %bitcast.28), channel_id=1, replica_groups=mesh['parts'=2,'ep'=2,'shadow'=8] {'ep'}, dimensions={0} | all-to-all | bytes 2097152 | tf_op jit(solution)/shard_map/all_to_all | solution.py:53
  95.6 1.0 copy.32
  96.7 4.4 %all-to-all-start.3 = ((bf16[2,8,16,2048]{3,2,0,1:T(8,128)(2,1)}), bf16[2,8,16,2048]{3,2,0,1:T(8,128)(2,1)}, u32[]{:S(2)}, u32[]{:S(2)}) async-start(bf16[2,8,16,2048]{3,2,0,1:T(8,128)(2,1)} %copy.32), calls=%async_computation.3 | async-start | bytes 2097152 | tf_op jit(solution)/shard_map/all_to_all | solution.py:52
  101.1 0.0 copy-done.6
  101.1 0.1 copy.34
  101.2 38.2 %all-to-all-done.3 = bf16[2,8,16,2048]{3,2,0,1:T(8,128)(2,1)} async-done(((bf16[2,8,16,2048]{3,2,0,1:T(8,128)(2,1)}), bf16[2,8,16,2048]{3,2,0,1:T(8,128)(2,1)}, u32[]{:S(2)}, u32[]{:S(2)}) %all-to-all-start.3) | async-done | bytes 1048608 | tf_op jit(solution)/shard_map/all_to_all | solution.py:52
  139.5 2.4 copy.33
  141.8 3.6 %gather_fusion = bf16[128,2048]{1,0:T(8,128)(2,1)} fusion(bf16[256,2048]{1,0:T(8,128)(2,1)} %bitcast.25, s32[1024]{0:T(1024)S(1)} %pad_clamp_fusion), kind=kCustom, calls=%fused_computation | custom fusion | bytes 1049088 | tf_op jit(solution)/shard_map/gather | solution.py:60
  145.5 2.7 reshape.65
  148.1 3.5 %multiply_reduce_fusion = bf16[64,2048]{1,0:T(8,128)(2,1)} fusion(f32[64,2,2048]{2,1,0:T(2,128)} %reshape.65, f32[64,2]{1,0:T(8,128)S(1)} %copy.34), kind=kLoop, calls=%fused_computation.12 | loop fusion | flops 393216 | bytes 1311232 | tf_op jit(solution)/shard_map/reduce_sum | solution.py:61
  151.6 119.4 %all-reduce.3.cloned.1.call-done = (bf16[512,2048]{1,0:T(8,128)(2,1)}, bf16[2048,1024]{1,0:T(8,128)(2,1)}) async-done(((bf16[512,2048]{1,0:T(8,128)(2,1)}, bf16[2048,1024]{1,0:T(8,128)(2,1)}), (bf16[512,2048]{1,0:T(8,128)(2,1)}, bf16[2048,1024]{1,0:T(8,128)(2,1)})) %all-reduce.3.cloned.1.call-update) | async-done | bytes 6291472 | tf_op jit(solution)/shard_map/psum | solution.py:9
  271.0 0.0 copy-done
  271.1 0.0 copy-start.7
  271.1 0.0 copy-start.8
  271.1 5.4 %convolution_bitcast_fusion = f32[768,1024]{0,1:T(8,128)S(1)} fusion(bf16[2048,1024]{1,0:T(8,128)(2,1)} %get-tuple-element.3, bf16[768,2048]{1,0:T(8,128)(2,1)S(1)} %copy-done), kind=kOutput, calls=%fused_computation.9 | convolution fusion | flops 3221225472 | bytes 10485760 | tf_op jit(solution)/shard_map/dot_general | solution.py:14
  276.5 0.0 copy-done.7
  276.5 0.0 copy-done.8
  276.5 3.6 %multiply_convert_fusion = bf16[768,2048]{1,0:T(8,128)(2,1)} fusion(bf16[512,2048]{1,0:T(8,128)(2,1)S(1)} %copy-done.7, f32[768]{0:T(1024)S(1)} %copy-done.8, f32[768,1024]{0,1:T(8,128)S(1)} %convolution_bitcast_fusion), kind=kOutput, calls=%fused_computation.2 | convolution fusion | flops 1616117760 | bytes 8391680 | tf_op jit(solution)/shard_map/dot_general | solution.py:18
  (3 shorter events, 0.0 us)
Async XLA Ops:
  7.2 263.9 %copy-start = (bf16[768,2048]{1,0:T(8,128)(2,1)S(1)}, bf16[768,2048]{1,0:T(8,128)(2,1)}, u32[]{:S(2)}) copy-start(bf16[768,2048]{1,0:T(8,128)(2,1)} %param.9) | copy-start | bytes 9437188
  7.2 263.9 %all-reduce.3.cloned.1.call-start = ((), (), s32[]{:S(2)}) async-start(), calls=%async_computation.4 | async-start | bytes 12582912 | tf_op jit(solution)/shard_map/psum | solution.py:9
  9.3 4.6 %copy-start.2 = (bf16[1,512,2048]{2,1,0:T(8,128)(2,1)S(1)}, bf16[1,512,2048]{2,1,0:T(8,128)(2,1)}, u32[]{:S(2)}) copy-start(bf16[1,512,2048]{2,1,0:T(8,128)(2,1)} %param.15) | copy-start | bytes 6291460
  15.3 0.7 copy-start.5
  15.3 1.4 copy-start.4
  28.8 59.9 %copy-start.1 = (bf16[1,2048,1024]{2,1,0:T(8,128)(2,1)S(1)}, bf16[1,2048,1024]{2,1,0:T(8,128)(2,1)}, u32[]{:S(2)}) copy-start(bf16[1,2048,1024]{2,1,0:T(8,128)(2,1)} %param.14) | copy-start | bytes 12582916
  88.7 1.6 copy-start.3
  91.1 10.1 %copy-start.6 = (f32[64,2]{0,1:T(2,128)S(1)}, f32[64,2]{0,1:T(2,128)}, u32[]{:S(2)}) copy-start(f32[64,2]{0,1:T(2,128)} %param.13) | copy-start | bytes 1540
  96.7 42.8 %all-to-all-start.3 = ((bf16[2,8,16,2048]{3,2,0,1:T(8,128)(2,1)}), bf16[2,8,16,2048]{3,2,0,1:T(8,128)(2,1)}, u32[]{:S(2)}, u32[]{:S(2)}) async-start(bf16[2,8,16,2048]{3,2,0,1:T(8,128)(2,1)} %copy.32), calls=%async_computation.3 | async-start | bytes 2097152 | tf_op jit(solution)/shard_map/all_to_all | solution.py:52
  271.1 5.5 %copy-start.7 = (bf16[512,2048]{1,0:T(8,128)(2,1)S(1)}, bf16[512,2048]{1,0:T(8,128)(2,1)}, u32[]{:S(2)}) copy-start(bf16[512,2048]{1,0:T(8,128)(2,1)} %get-tuple-element.2) | copy-start | bytes 6291460
  271.1 5.5 %copy-start.8 = (f32[768]{0:T(1024)S(1)}, f32[768]{0:T(1024)}, u32[]{:S(2)}) copy-start(f32[768]{0:T(1024)} %param.10) | copy-start | bytes 9220
Sparse Core Ops, SparseCore 0:
  15.5 255.5 all-reduce.2
where the time goes:
time: 288 us; the launch traced here: 287 us
  waiting for transfers between devices  158 us (55%)
  blocking collectives  70 us (24%)
  local copies, waits for them, and re-layouts  18.9 us (7%)
  between operations  14.8 us (5%)
  matrix products  11 us (4%)
  other arithmetic  9.98 us (3%)
  starting transfers between devices  4.48 us (2%)
    psum x1, waiting for transfers between devices, broadcast(): return lax.psum(kept, axis)  119 us
    all_to_all x1, blocking collectives, body(): lax.all_to_all(lax.all_to_all(sectioned, 'ep', split_axis=0, concat_axis=...  59.8 us
    all_to_all x1, waiting for transfers between devices, body(): lax.all_to_all(lax.all_to_all(answered, 'ep', split_axis=0, concat_axis=0...  38.2 us
    dot_general x2, matrix products, expert_apply(): pre_act = jnp.dot(group_rows, gate_up, preferred_element_type=jnp.float32)  6.7 us
    select_n x2, other arithmetic, broadcast(): jnp.where(lax.axis_index(axis) == source, value, 0).astype(value.dtype)  6.04 us
  transfers between devices with their start and end apart: 2, of which 2 were waited for; matrix products, arithmetic and copies ran while one was open for 8% of the time, Pallas kernels for 0%

commit v1 on v0

v1 whole, which is shorter than its diff:
```python
import jax
import jax.numpy as jnp
from jax import lax
from jax.sharding import PartitionSpec as P

LAG = 2
CHUNKS = 16


def ring_order(mesh):
    n = mesh.shape["shadow"]
    axis = mesh.axis_names.index("shadow")
    index = [0] * mesh.devices.ndim
    spots = []
    for s in range(n):
        index[axis] = s
        spots.append(tuple(getattr(mesh.devices[tuple(index)], "coords", (s,))))
    varying = [a for a in range(len(spots[0])) if len({p[a] for p in spots}) > 1]
    if len(varying) == 2:
        sizes = [len({p[a] for p in spots}) for a in varying]
        if 2 in sizes:
            short = varying[sizes.index(2)]
            long = varying[1 - sizes.index(2)]
            low = min(p[short] for p in spots)
            one = sorted((s for s in range(n) if spots[s][short] == low), key=lambda s: spots[s][long])
            two = sorted((s for s in range(n) if spots[s][short] != low), key=lambda s: -spots[s][long])
            return one + two
    return list(range(n))


def swiglu(pre, hidden_units):
    return (jax.nn.silu(pre[:, :hidden_units]) * pre[:, hidden_units:]).astype(jnp.bfloat16)


def ring_broadcast(order, own, root):
    n = len(order)
    chunks = len(own[0])
    place = jnp.array([order.index(s) for s in range(n)], jnp.int32)
    me = lax.axis_index("shadow")
    ahead = (place[me] - place[root]) % n
    hops = (ahead, (n - ahead) % n)
    ways = (
        [(order[i], order[(i + 1) % n]) for i in range(n)],
        [(order[(i + 1) % n], order[i]) for i in range(n)],
    )
    is_root = me == root
    held = [jnp.zeros((chunks, *own[0][0].shape), own[0][0].dtype) for _ in ways]
    came, last = {}, None
    for t in range(chunks + (n - 1) * LAG):
        mine = [own[i][min(t, chunks - 1)] for i in range(2)]
        if t >= LAG:
            got = came.pop(t - LAG)
            if last is not None:
                got, _ = lax.optimization_barrier((got, last))
            mine = [jnp.where(is_root, mine[i], got[i]) for i in range(2)]
        mine = list(lax.optimization_barrier(tuple(mine)))
        last = mine
        for i in range(2):
            at = jnp.clip(t - LAG * hops[i], 0, chunks - 1)
            held[i] = lax.dynamic_update_slice(held[i], mine[i][None], (at, 0, 0))
        if t < chunks + (n - 2) * LAG:
            came[t] = [lax.ppermute(mine[i], "shadow", ways[i]) for i in range(2)]
    return held


def cut(parts, start, size):
    out = []
    for part in parts:
        rows = part.shape[0]
        low, high = max(start, 0), min(start + size, rows)
        if low < high:
            out.append(part[low:high])
        start -= rows
    return out[0] if len(out) == 1 else jnp.concatenate(out, 0)


def body(order, hot_root, res_rows, res_weight, cold_rows, cold_experts, cold_weights, w_gate_up, w_down):
    gate_up, down = w_gate_up[0], w_down[0]
    hidden_units, width = down.shape
    n_owners = lax.axis_size("ep") * lax.axis_size("shadow")
    per_device, fan_out = cold_experts.shape
    capacity = max(2, 2 * per_device * fan_out // n_owners)

    slot = lax.broadcasted_iota(jnp.int32, (per_device, n_owners * capacity), 1)
    named = [cold_experts[:, k : k + 1] == slot // capacity for k in range(fan_out)]
    count = sum(m.astype(jnp.bfloat16) for m in named)
    before = (
        lax.broadcasted_iota(jnp.int32, (per_device, per_device), 0)
        > lax.broadcasted_iota(jnp.int32, (per_device, per_device), 1)
    ).astype(jnp.bfloat16)
    rank = jnp.dot(before, count, preferred_element_type=jnp.float32)
    here = rank == (slot % capacity).astype(jnp.float32)
    chosen = [m & here for m in named]
    placed = sum(m.astype(jnp.bfloat16) for m in chosen)
    outgoing = lax.dot_general(
        placed, cold_rows, (((0,), (0,)), ((), ())), preferred_element_type=jnp.float32
    ).astype(jnp.bfloat16)
    arrived = lax.all_to_all(outgoing, ("ep", "shadow"), 0, 0, tiled=True)
    pre = jnp.dot(arrived, gate_up, preferred_element_type=jnp.float32)
    served = jnp.dot(swiglu(pre, hidden_units), down, preferred_element_type=jnp.float32)
    returned = lax.all_to_all(served.astype(jnp.bfloat16), ("ep", "shadow"), 0, 0, tiled=True)
    scale = sum(jnp.where(chosen[k], cold_weights[:, k : k + 1], 0.0) for k in range(fan_out))
    high = scale.astype(jnp.bfloat16)
    low = (scale - high.astype(jnp.float32)).astype(jnp.bfloat16)
    cold_out = (
        jnp.dot(high, returned, preferred_element_type=jnp.float32)
        + jnp.dot(low, returned, preferred_element_type=jnp.float32)
    ).astype(jnp.bfloat16)

    root = hot_root[lax.axis_index("ep")]
    half, middle = width // 2, gate_up.shape[0] // 2
    lanes = ([gate_up[:middle], down[:, :half]], [gate_up[middle:], down[:, half:]])
    rows = (middle + hidden_units) // CHUNKS
    own = [[cut(lane, c * rows, rows) for c in range(CHUNKS)] for lane in lanes]
    held = [h.reshape(middle + hidden_units, half) for h in ring_broadcast(order, own, root)]
    pre = jnp.dot(res_rows[:, :middle], held[0][:middle], preferred_element_type=jnp.float32) + jnp.dot(
        res_rows[:, middle:], held[1][:middle], preferred_element_type=jnp.float32
    )
    hidden = swiglu(pre, hidden_units)
    hot_out = jnp.concatenate(
        [
            (jnp.dot(hidden, h[middle:], preferred_element_type=jnp.float32) * res_weight[:, None]).astype(jnp.bfloat16)
            for h in held
        ],
        axis=1,
    )
    return hot_out, cold_out


def solution(mesh):
    order = ring_order(mesh)
    rows = P(("parts", "ep", "shadow"), None)
    owners = P(("ep", "shadow"), None, None)
    in_specs = (P("parts"), rows, P(("parts", "ep", "shadow")), rows, rows, rows, owners, owners)
    return jax.shard_map(
        lambda *args: body(order, *args), mesh=mesh, in_specs=in_specs, out_specs=(rows, rows), check_vma=False
    )
```

time: 288 us -> 204 us (0.71)
  waiting for transfers between devices: 158 us -> 28.7 us
  starting transfers between devices: 4.48 us -> 80 us
  blocking collectives: 70 us -> 0 us
  local copies, waits for them, and re-layouts: 18.9 us -> 60.4 us
  between operations: 14.8 us -> 4.92 us
  matrix products: 11 us -> 19.7 us
    psum x1 -> x0, waiting for transfers between devices: 119 us -> none  [broadcast(): return lax.psum(kept, axis)]
    all_to_all x3 -> x0, blocking collectives: 70 us -> none  [the longest x1 59.8 us: body(): lax.all_to_all(lax.all_to_all(sectioned, 'ep', split_axis=0, concat_axis=...]
    ppermute x0 -> x56, starting transfers between devices: none -> 69.2 us  [ring_broadcast(): came[t] = [lax.ppermute(mine[i], 'shadow', ways[i]) for i in range(2)]]
    dynamic_update_slice x0 -> x60, local copies, waits for them, and re-layouts: none -> 48.9 us  [ring_broadcast(): held[i] = lax.dynamic_update_slice(held[i], mine[i][None], (at, 0, 0))]
    all_to_all x1 -> x2, waiting for transfers between devices: 38.2 us -> 0.01 us  [the longest x1 0.01 us: body(): arrived = lax.all_to_all(outgoing, ('ep', 'shadow'), 0, 0, tiled=True)]
    ppermute x0 -> x56, waiting for transfers between devices: none -> 28.7 us  [ring_broadcast(): came[t] = [lax.ppermute(mine[i], 'shadow', ways[i]) for i in range(2)]]
    dot_general x4 -> x10, matrix products: 11 us -> 19.7 us  [the longest x2 4.49 us: body(): jnp.dot(hidden, h[middle:], preferred_element_type=jnp.float32)]
    all_to_all x1 -> x2, starting transfers between devices: 4.44 us -> 10.8 us  [the longest x1 6.39 us: body(): arrived = lax.all_to_all(outgoing, ('ep', 'shadow'), 0, 0, tiled=True)]
  transfers between devices with their start and end apart: 2 -> 58, of which waited for: 2 -> 28; matrix products, arithmetic and copies ran while one was open for 8% -> 42% of each run, Pallas kernels for 0% -> 0%
where the time goes in v1:
time: 204 us
  starting transfers between devices  80 us (39%)
  local copies, waits for them, and re-layouts  60.4 us (30%)
  waiting for transfers between devices  28.7 us (14%)
  matrix products  19.7 us (10%)
  other arithmetic  9.74 us (5%)
  between operations  4.92 us (2%)
    ppermute x56, starting transfers between devices, ring_broadcast(): came[t] = [lax.ppermute(mine[i], 'shadow', ways[i]) for i in range(2)]  69.2 us
    dynamic_update_slice x60, local copies, waits for them, and re-layouts, ring_broadcast(): held[i] = lax.dynamic_update_slice(held[i], mine[i][None], (at, 0, 0))  48.9 us
    ppermute x56, waiting for transfers between devices, ring_broadcast(): came[t] = [lax.ppermute(mine[i], 'shadow', ways[i]) for i in range(2)]  28.7 us
    select_n x28, other arithmetic, ring_broadcast(): mine = [jnp.where(is_root, mine[i], got[i]) for i in range(2)]  7.27 us
    all_to_all x1, starting transfers between devices, body(): arrived = lax.all_to_all(outgoing, ('ep', 'shadow'), 0, 0, tiled=True)  6.39 us
    slice x3, local copies, waits for them, and re-layouts, cut(): out.append(part[low:high])  4.53 us
    dot_general x2, matrix products, body(): jnp.dot(hidden, h[middle:], preferred_element_type=jnp.float32)  4.49 us
    all_to_all x1, starting transfers between devices, body(): lax.all_to_all(served.astype(jnp.bfloat16), ('ep', 'shadow'), 0, 0, tiled...  4.4 us
  transfers between devices with their start and end apart: 58, of which 28 were waited for; matrix products, arithmetic and copies ran while one was open for 42% of the time, Pallas kernels for 0%

profile of v1, /device:TPU:0, one launch (start us, length us, event | category | flops | bytes accessed | tf_op | source)
XLA Modules:
  0.0 203.6 jit_solution(4143516397695233655)
XLA Ops:
  0.7 2.2 %slice_bitcast_fusion = (bf16[96,1024]{1,0:T(8,128)(2,1)}, bf16[96,1024]{1,0:T(8,128)(2,1)}, bf16[96,1024]{1,0:T(8,128)(2,1)}, bf16[96,1024]{1,0:T(8,128)(2,1)}) fusion(bf16[1,2048,1024]{2,1,0:T(8,128)(2,1)} %param.15), kind=kLoop, calls=%fused_computation.110 | loop fusion | bytes 1572864 | tf_op jit(solution)/shard_map/slice | solution.py:72
  2.9 3.0 %collective-permute-start = (bf16[96,1024]{1,0:T(8,128)(2,1)}, bf16[96,1024]{1,0:T(8,128)(2,1)}, u32[]{:S(2)}, u32[]{:S(2)}) collective-permute-start(bf16[96,1024]{1,0:T(8,128)(2,1)} %get-tuple-element.118), channel_id=1, source_target_pairs={{0,2},{2,4},{4,6},{6,7},{7,5},{5,3},{3,1},{1,0},{8,10},{10,12},{12... | collective-permute-start | bytes 589832 | tf_op jit(solution)/shard_map/ppermute | solution.py:62
  5.9 2.0 collective-permute-start.2
  9.0 1.5 convolution_convert_fusion.1
  10.6 6.4 %all-to-all-start = ((bf16[16,16,2048]{2,1,0:T(8,128)(2,1)}), bf16[16,16,2048]{2,1,0:T(8,128)(2,1)S(1)}, u32[]{:S(2)}, u32[]{:S(2)}) async-start(bf16[16,16,2048]{2,1,0:T(8,128)(2,1)} %bitcast.92), calls=%async_computation | async-start | bytes 2097152 | tf_op jit(solution)/shard_map/all_to_all | solution.py:98
  22.1 1.6 slice_bitcast_fusion.4
  24.4 2.1 %broadcast.48.clone.1 = bf16[16,96,1024]{2,1,0:T(8,128)(2,1)} broadcast(bf16[]{:T(256)} %constant.145.clone.1), dimensions={} | broadcast | bytes 3145730 | tf_op jit(solution)/shard_map/broadcast.7
  26.4 1.8 bitcast_dynamic-update-slice_fusion.59
  28.2 1.6 bitcast_dynamic-update-slice_fusion.58
  29.8 2.1 %broadcast.48.clone = bf16[16,96,1024]{2,1,0:T(8,128)(2,1)} broadcast(bf16[]{:T(256)} %constant.145.clone.1), dimensions={} | broadcast | bytes 3145730 | tf_op jit(solution)/shard_map/broadcast.7
  31.9 1.6 bitcast_dynamic-update-slice_fusion.29
  33.5 1.6 bitcast_dynamic-update-slice_fusion.28
  35.6 1.1 bitcast_select_fusion.14
  36.7 2.0 collective-permute-start.4
  38.8 1.1 bitcast_select_fusion.12
  39.9 2.0 collective-permute-start.6
  44.7 1.4 collective-permute-done.4
  46.7 2.2 %collective-permute-start.8 = (bf16[96,1024]{1,0:T(8,128)(2,1)S(1)}, bf16[96,1024]{1,0:T(8,128)(2,1)S(1)}, u32[]{:S(2)}, u32[]{:S(2)}) collective-permute-start(bf16[96,1024]{1,0:T(8,128)(2,1)S(1)} %get-tuple-element.132), channel_id=1, source_target_pairs={{0,2},{2,4},{4,6},{6,7},{7,5},{5,3},{3,1},{1,0},{8,10},{10,12},{12... | collective-permute-start | bytes 589832 | tf_op jit(solution)/shard_map/ppermute | solution.py:62
  48.8 1.5 collective-permute-done.6
  50.7 2.4 %collective-permute-start.10 = (bf16[96,1024]{1,0:T(8,128)(2,1)S(1)}, bf16[96,1024]{1,0:T(8,128)(2,1)S(1)}, u32[]{:S(2)}, u32[]{:S(2)}) collective-permute-start(bf16[96,1024]{1,0:T(8,128)(2,1)S(1)} %get-tuple-element.136), channel_id=1, source_target_pairs={{0,2},{2,4},{4,6},{6,7},{7,5},{5,3},{3,1},{1,0},{8,10},{10,12},{12... | collective-permute-start | bytes 589832 | tf_op jit(solution)/shard_map/ppermute | solution.py:62
  55.9 2.1 %collective-permute-start.12 = (bf16[96,1024]{1,0:T(8,128)(2,1)S(1)}, bf16[96,1024]{1,0:T(8,128)(2,1)S(1)}, u32[]{:S(2)}, u32[]{:S(2)}) collective-permute-start(bf16[96,1024]{1,0:T(8,128)(2,1)S(1)} %get-tuple-element.140), channel_id=1, source_target_pairs={{0,2},{2,4},{4,6},{6,7},{7,5},{5,3},{3,1},{1,0},{8,10},{10,12},{12... | collective-permute-start | bytes 589832 | tf_op jit(solution)/shard_map/ppermute | solution.py:62
  59.0 2.7 %collective-permute-start.14 = (bf16[96,1024]{1,0:T(8,128)(2,1)S(1)}, bf16[96,1024]{1,0:T(8,128)(2,1)S(1)}, u32[]{:S(2)}, u32[]{:S(2)}) collective-permute-start(bf16[96,1024]{1,0:T(8,128)(2,1)S(1)} %get-tuple-element.144), channel_id=1, source_target_pairs={{0,2},{2,4},{4,6},{6,7},{7,5},{5,3},{3,1},{1,0},{8,10},{10,12},{12... | collective-permute-start | bytes 589832 | tf_op jit(solution)/shard_map/ppermute | solution.py:62
  64.5 2.0 %collective-permute-start.16 = (bf16[96,1024]{1,0:T(8,128)(2,1)S(1)}, bf16[96,1024]{1,0:T(8,128)(2,1)S(1)}, u32[]{:S(2)}, u32[]{:S(2)}) collective-permute-start(bf16[96,1024]{1,0:T(8,128)(2,1)S(1)} %get-tuple-element.148), channel_id=1, source_target_pairs={{0,2},{2,4},{4,6},{6,7},{7,5},{5,3},{3,1},{1,0},{8,10},{10,12},{12... | collective-permute-start | bytes 589832 | tf_op jit(solution)/shard_map/ppermute | solution.py:62
  66.6 1.4 collective-permute-done.14
  68.6 2.0 collective-permute-start.18
  74.0 1.6 collective-permute-start.20
  76.6 1.2 collective-permute-done.19
  77.9 1.6 collective-permute-start.22
  82.9 1.4 collective-permute-start.24
  85.2 2.0 %collective-permute-done.23 = bf16[96,1024]{1,0:T(8,128)(2,1)S(1)} collective-permute-done((bf16[96,1024]{1,0:T(8,128)(2,1)S(1)}, bf16[96,1024]{1,0:T(8,128)(2,1)S(1)}, u32[]{:S(2)}, u32[]{:S(2)}) %collective-permute-start.23) | collective-permute-done | bytes 196640 | tf_op jit(solution)/shard_map/ppermute | solution.py:62
  87.2 1.2 collective-permute-start.26
  92.1 1.2 collective-permute-start.28
  95.0 1.2 collective-permute-done.27
  97.0 1.4 collective-permute-start.31
  101.9 1.4 collective-permute-start.33
  104.8 1.1 collective-permute-start.34
  109.7 1.0 collective-permute-start.36
  113.8 1.1 collective-permute-start.38
  119.5 1.0 collective-permute-start.40
  122.6 1.1 collective-permute-start.42
  124.6 3.4 %fusion = f32[256,1024]{1,0:T(8,128)S(1)} fusion(bf16[256,2048]{1,0:T(8,128)(2,1)S(1)} %bitcast.216, bf16[1,2048,1024]{2,1,0:T(8,128)(2,1)} %param.15), kind=kOutput, calls=%fused_computation | convolution fusion | flops 1073741824 | bytes 6291456 | tf_op jit(solution)/shard_map/dot_general | solution.py:99
  128.0 1.8 convolution_convert_fusion
  129.8 4.4 %all-to-all-start.1 = ((bf16[16,16,2048]{2,1,0:T(8,128)(2,1)}), bf16[16,16,2048]{2,1,0:T(8,128)(2,1)S(1)}, u32[]{:S(2)}, u32[]{:S(2)}) async-start(bf16[16,16,2048]{2,1,0:T(8,128)(2,1)} %bitcast.217), calls=%async_computation.1 | async-start | bytes 2097152 | tf_op jit(solution)/shard_map/all_to_all | solution.py:101
  134.2 1.6 bitcast_dynamic-update-slice_fusion.39
  135.8 1.6 bitcast_dynamic-update-slice_fusion.38
  137.5 1.6 bitcast_dynamic-update-slice_fusion.9
  139.1 1.6 bitcast_dynamic-update-slice_fusion.8
  140.7 1.1 broadcast_select_fusion.14
  141.8 2.0 collective-permute-start.44
  143.9 1.1 broadcast_select_fusion.12
  145.0 1.9 collective-permute-start.46
  149.8 7.0 %collective-permute-done.44 = bf16[96,1024]{1,0:T(8,128)(2,1)S(1)} collective-permute-done((bf16[96,1024]{1,0:T(8,128)(2,1)S(1)}, bf16[96,1024]{1,0:T(8,128)(2,1)S(1)}, u32[]{:S(2)}, u32[]{:S(2)}) %collective-permute-start.44) | collective-permute-done | bytes 196640 | tf_op jit(solution)/shard_map/ppermute | solution.py:62
  157.4 8.7 %collective-permute-start.48 = (bf16[96,1024]{1,0:T(8,128)(2,1)S(1)}, bf16[96,1024]{1,0:T(8,128)(2,1)S(1)}, u32[]{:S(2)}, u32[]{:S(2)}) collective-permute-start(bf16[96,1024]{1,0:T(8,128)(2,1)S(1)} %get-tuple-element.212), channel_id=1, source_target_pairs={{0,2},{2,4},{4,6},{6,7},{7,5},{5,3},{3,1},{1,0},{8,10},{10,12},{12... | collective-permute-start | bytes 589832 | tf_op jit(solution)/shard_map/ppermute | solution.py:62
  166.2 4.1 %collective-permute-start.50 = (bf16[96,1024]{1,0:T(8,128)(2,1)S(1)}, bf16[96,1024]{1,0:T(8,128)(2,1)S(1)}, u32[]{:S(2)}, u32[]{:S(2)}) collective-permute-start(bf16[96,1024]{1,0:T(8,128)(2,1)S(1)} %get-tuple-element.216), channel_id=1, source_target_pairs={{0,2},{2,4},{4,6},{6,7},{7,5},{5,3},{3,1},{1,0},{8,10},{10,12},{12... | collective-permute-start | bytes 589832 | tf_op jit(solution)/shard_map/ppermute | solution.py:62
  173.2 2.1 %collective-permute-start.52 = (bf16[96,1024]{1,0:T(8,128)(2,1)S(1)}, bf16[96,1024]{1,0:T(8,128)(2,1)S(1)}, u32[]{:S(2)}, u32[]{:S(2)}) collective-permute-start(bf16[96,1024]{1,0:T(8,128)(2,1)S(1)} %get-tuple-element.220), channel_id=1, source_target_pairs={{0,2},{2,4},{4,6},{6,7},{7,5},{5,3},{3,1},{1,0},{8,10},{10,12},{12... | collective-permute-start | bytes 589832 | tf_op jit(solution)/shard_map/ppermute | solution.py:62
  176.1 2.7 %collective-permute-start.54 = (bf16[96,1024]{1,0:T(8,128)(2,1)S(1)}, bf16[96,1024]{1,0:T(8,128)(2,1)S(1)}, u32[]{:S(2)}, u32[]{:S(2)}) collective-permute-start(bf16[96,1024]{1,0:T(8,128)(2,1)S(1)} %get-tuple-element.224), channel_id=1, source_target_pairs={{0,2},{2,4},{4,6},{6,7},{7,5},{5,3},{3,1},{1,0},{8,10},{10,12},{12... | collective-permute-start | bytes 589832 | tf_op jit(solution)/shard_map/ppermute | solution.py:62
  181.6 1.5 collective-permute-done.54
  183.1 2.0 collective-permute-done.55
  187.3 3.5 %fusion.3 = f32[1024,768]{1,0:T(8,128)S(1)} fusion(bf16[1536,1024]{1,0:T(8,128)(2,1)} %bitcast.86, bf16[768,2048]{1,0:T(8,128)(2,1)S(1)} %copy-done.20), kind=kOutput, calls=%fused_computation.10 | convolution fusion | flops 1610612736 | bytes 6815744 | tf_op jit(solution)/shard_map/dot_general | solution.py:116
  191.4 3.5 %add_bitcast_fusion = f32[768,1024]{0,1:T(8,128)S(1)} fusion(f32[1024,768]{1,0:T(8,128)S(1)} %fusion.3, bf16[1536,1024]{1,0:T(8,128)(2,1)} %bitcast.55, bf16[768,2048]{1,0:T(8,128)(2,1)S(1)} %copy-done.20), kind=kOutput, calls=%fused_computation.5 | convolution fusion | flops 1611399168 | bytes 9961472 | tf_op jit(solution)/shard_map/dot_general | solution.py:116
  195.6 2.2 %multiply_convert_fusion.1 = bf16[768,1024]{1,0:T(8,128)(2,1)S(1)} fusion(bf16[768,512]{0,1:T(8,128)(2,1)S(1)} %fusion.9, f32[768]{0:T(1024)S(1)} %copy-done.21, bf16[1536,1024]{1,0:T(8,128)(2,1)} %bitcast.55), kind=kOutput, calls=%fused_computation.4 | convolution fusion | flops 806879232 | bytes 3410944 | tf_op jit(solution)/shard_map/dot_general | solution.py:122
  197.9 2.2 %multiply_convert_fusion = bf16[768,1024]{1,0:T(8,128)(2,1)S(1)} fusion(bf16[768,512]{0,1:T(8,128)(2,1)S(1)} %fusion.9, f32[768]{0:T(1024)S(1)} %copy-done.21, bf16[1536,1024]{1,0:T(8,128)(2,1)} %bitcast.86), kind=kOutput, calls=%fused_computation.3 | convolution fusion | flops 806879232 | bytes 3410944 | tf_op jit(solution)/shard_map/dot_general | solution.py:122
  200.2 2.0 pad_maximum_fusion
  202.6 1.1 fusion.2
  (210 shorter events, 63.5 us)
Async XLA Ops:
  0.6 18.9 %copy-start.18 = (s32[8]{0:T(128)S(1)}, s32[8]{0:T(128)}, u32[]{:S(2)}) copy-start(s32[8]{0:T(128)} %constant.182.clone) | copy-start | bytes 100
  0.7 16.3 %copy-start.22 = (s32[2]{0:T(128)S(1)}, s32[2]{0:T(128)}, u32[]{:S(2)}) copy-start(s32[2]{0:T(128)} %param.9) | copy-start | bytes 28
  0.7 23.0 %copy-start.1 = (bf16[1,512,2048]{2,1,0:T(8,128)(2,1)S(1)}, bf16[1,512,2048]{2,1,0:T(8,128)(2,1)}, u32[]{:S(2)}) copy-start(bf16[1,512,2048]{2,1,0:T(8,128)(2,1)} %param.16) | copy-start | bytes 6291460
  2.9 32.7 %collective-permute-start = (bf16[96,1024]{1,0:T(8,128)(2,1)}, bf16[96,1024]{1,0:T(8,128)(2,1)}, u32[]{:S(2)}, u32[]{:S(2)}) collective-permute-start(bf16[96,1024]{1,0:T(8,128)(2,1)} %get-tuple-element.118), channel_id=1, source_target_pairs={{0,2},{2,4},{4,6},{6,7},{7,5},{5,3},{3,1},{1,0},{8,10},{10,12},{12... | collective-permute-start | bytes 589832 | tf_op jit(solution)/shard_map/ppermute | solution.py:62
  5.9 29.7 %collective-permute-start.1 = (bf16[96,1024]{1,0:T(8,128)(2,1)}, bf16[96,1024]{1,0:T(8,128)(2,1)}, u32[]{:S(2)}, u32[]{:S(2)}) collective-permute-start(bf16[96,1024]{1,0:T(8,128)(2,1)} %get-tuple-element.120), channel_id=1, source_target_pairs={{2,0},{4,2},{6,4},{7,6},{5,7},{3,5},{1,3},{0,1},{10,8},{12,10},{14... | collective-permute-start | bytes 589832 | tf_op jit(solution)/shard_map/ppermute | solution.py:62
  5.9 32.9 %collective-permute-start.2 = (bf16[96,1024]{1,0:T(8,128)(2,1)}, bf16[96,1024]{1,0:T(8,128)(2,1)}, u32[]{:S(2)}, u32[]{:S(2)}) collective-permute-start(bf16[96,1024]{1,0:T(8,128)(2,1)} %get-tuple-element.119), channel_id=1, source_target_pairs={{0,2},{2,4},{4,6},{6,7},{7,5},{5,3},{3,1},{1,0},{8,10},{10,12},{12... | collective-permute-start | bytes 589832 | tf_op jit(solution)/shard_map/ppermute | solution.py:62
  8.0 30.8 %collective-permute-start.3 = (bf16[96,1024]{1,0:T(8,128)(2,1)}, bf16[96,1024]{1,0:T(8,128)(2,1)}, u32[]{:S(2)}, u32[]{:S(2)}) collective-permute-start(bf16[96,1024]{1,0:T(8,128)(2,1)} %get-tuple-element.121), channel_id=1, source_target_pairs={{2,0},{4,2},{6,4},{7,6},{5,7},{3,5},{1,3},{0,1},{10,8},{12,10},{14... | collective-permute-start | bytes 589832 | tf_op jit(solution)/shard_map/ppermute | solution.py:62
  10.6 114.0 %all-to-all-start = ((bf16[16,16,2048]{2,1,0:T(8,128)(2,1)}), bf16[16,16,2048]{2,1,0:T(8,128)(2,1)S(1)}, u32[]{:S(2)}, u32[]{:S(2)}) async-start(bf16[16,16,2048]{2,1,0:T(8,128)(2,1)} %bitcast.92), calls=%async_computation | async-start | bytes 2097152 | tf_op jit(solution)/shard_map/all_to_all | solution.py:98
  36.7 9.4 %collective-permute-start.4 = (bf16[96,1024]{1,0:T(8,128)(2,1)S(1)}, bf16[96,1024]{1,0:T(8,128)(2,1)S(1)}, u32[]{:S(2)}, u32[]{:S(2)}) collective-permute-start(bf16[96,1024]{1,0:T(8,128)(2,1)S(1)} %get-tuple-element.124), channel_id=1, source_target_pairs={{0,2},{2,4},{4,6},{6,7},{7,5},{5,3},{3,1},{1,0},{8,10},{10,12},{12... | collective-permute-start | bytes 589832 | tf_op jit(solution)/shard_map/ppermute | solution.py:62
  38.7 7.9 %collective-permute-start.5 = (bf16[96,1024]{1,0:T(8,128)(2,1)S(1)}, bf16[96,1024]{1,0:T(8,128)(2,1)S(1)}, u32[]{:S(2)}, u32[]{:S(2)}) collective-permute-start(bf16[96,1024]{1,0:T(8,128)(2,1)S(1)} %get-tuple-element.125), channel_id=1, source_target_pairs={{2,0},{4,2},{6,4},{7,6},{5,7},{3,5},{1,3},{0,1},{10,8},{12,10},{14... | collective-permute-start | bytes 589832 | tf_op jit(solution)/shard_map/ppermute | solution.py:62
  39.9 10.4 %collective-permute-start.6 = (bf16[96,1024]{1,0:T(8,128)(2,1)S(1)}, bf16[96,1024]{1,0:T(8,128)(2,1)S(1)}, u32[]{:S(2)}, u32[]{:S(2)}) collective-permute-start(bf16[96,1024]{1,0:T(8,128)(2,1)S(1)} %get-tuple-element.128), channel_id=1, source_target_pairs={{0,2},{2,4},{4,6},{6,7},{7,5},{5,3},{3,1},{1,0},{8,10},{10,12},{12... | collective-permute-start | bytes 589832 | tf_op jit(solution)/shard_map/ppermute | solution.py:62
  41.9 8.7 %collective-permute-start.7 = (bf16[96,1024]{1,0:T(8,128)(2,1)S(1)}, bf16[96,1024]{1,0:T(8,128)(2,1)S(1)}, u32[]{:S(2)}, u32[]{:S(2)}) collective-permute-start(bf16[96,1024]{1,0:T(8,128)(2,1)S(1)} %get-tuple-element.129), channel_id=1, source_target_pairs={{2,0},{4,2},{6,4},{7,6},{5,7},{3,5},{1,3},{0,1},{10,8},{12,10},{14... | collective-permute-start | bytes 589832 | tf_op jit(solution)/shard_map/ppermute | solution.py:62
  46.7 9.1 %collective-permute-start.8 = (bf16[96,1024]{1,0:T(8,128)(2,1)S(1)}, bf16[96,1024]{1,0:T(8,128)(2,1)S(1)}, u32[]{:S(2)}, u32[]{:S(2)}) collective-permute-start(bf16[96,1024]{1,0:T(8,128)(2,1)S(1)} %get-tuple-element.132), channel_id=1, source_target_pairs={{0,2},{2,4},{4,6},{6,7},{7,5},{5,3},{3,1},{1,0},{8,10},{10,12},{12... | collective-permute-start | bytes 589832 | tf_op jit(solution)/shard_map/ppermute | solution.py:62
  48.8 7.0 %collective-permute-start.9 = (bf16[96,1024]{1,0:T(8,128)(2,1)S(1)}, bf16[96,1024]{1,0:T(8,128)(2,1)S(1)}, u32[]{:S(2)}, u32[]{:S(2)}) collective-permute-start(bf16[96,1024]{1,0:T(8,128)(2,1)S(1)} %get-tuple-element.133), channel_id=1, source_target_pairs={{2,0},{4,2},{6,4},{7,6},{5,7},{3,5},{1,3},{0,1},{10,8},{12,10},{14... | collective-permute-start | bytes 589832 | tf_op jit(solution)/shard_map/ppermute | solution.py:62
  50.7 8.1 %collective-permute-start.10 = (bf16[96,1024]{1,0:T(8,128)(2,1)S(1)}, bf16[96,1024]{1,0:T(8,128)(2,1)S(1)}, u32[]{:S(2)}, u32[]{:S(2)}) collective-permute-start(bf16[96,1024]{1,0:T(8,128)(2,1)S(1)} %get-tuple-element.136), channel_id=1, source_target_pairs={{0,2},{2,4},{4,6},{6,7},{7,5},{5,3},{3,1},{1,0},{8,10},{10,12},{12... | collective-permute-start | bytes 589832 | tf_op jit(solution)/shard_map/ppermute | solution.py:62
  53.0 5.9 %collective-permute-start.11 = (bf16[96,1024]{1,0:T(8,128)(2,1)S(1)}, bf16[96,1024]{1,0:T(8,128)(2,1)S(1)}, u32[]{:S(2)}, u32[]{:S(2)}) collective-permute-start(bf16[96,1024]{1,0:T(8,128)(2,1)S(1)} %get-tuple-element.137), channel_id=1, source_target_pairs={{2,0},{4,2},{6,4},{7,6},{5,7},{3,5},{1,3},{0,1},{10,8},{12,10},{14... | collective-permute-start | bytes 589832 | tf_op jit(solution)/shard_map/ppermute | solution.py:62
  55.9 18.0 %copy-start.3 = (bf16[64,1024]{1,0:T(8,128)(2,1)S(1)}, bf16[64,1024]{1,0:T(8,128)(2,1)}, u32[]{:S(2)}) copy-start(bf16[64,1024]{1,0:T(8,128)(2,1)} %get-tuple-element.235) | copy-start | bytes 393220
  55.9 18.0 %copy-start.4 = (bf16[32,1024]{1,0:T(8,128)(2,1)S(1)}, bf16[32,1024]{1,0:T(8,128)(2,1)}, u32[]{:S(2)}) copy-start(bf16[32,1024]{1,0:T(8,128)(2,1)} %get-tuple-element.294) | copy-start | bytes 196612
  55.9 18.0 %copy-start.5 = (bf16[32,1024]{1,0:T(8,128)(2,1)S(1)}, bf16[32,1024]{1,0:T(8,128)(2,1)}, u32[]{:S(2)}) copy-start(bf16[32,1024]{1,0:T(8,128)(2,1)} %get-tuple-element.295) | copy-start | bytes 196612
  55.9 8.5 %collective-permute-start.12 = (bf16[96,1024]{1,0:T(8,128)(2,1)S(1)}, bf16[96,1024]{1,0:T(8,128)(2,1)S(1)}, u32[]{:S(2)}, u32[]{:S(2)}) collective-permute-start(bf16[96,1024]{1,0:T(8,128)(2,1)S(1)} %get-tuple-element.140), channel_id=1, source_target_pairs={{0,2},{2,4},{4,6},{6,7},{7,5},{5,3},{3,1},{1,0},{8,10},{10,12},{12... | collective-permute-start | bytes 589832 | tf_op jit(solution)/shard_map/ppermute | solution.py:62
  57.9 6.5 %collective-permute-start.13 = (bf16[96,1024]{1,0:T(8,128)(2,1)S(1)}, bf16[96,1024]{1,0:T(8,128)(2,1)S(1)}, u32[]{:S(2)}, u32[]{:S(2)}) collective-permute-start(bf16[96,1024]{1,0:T(8,128)(2,1)S(1)} %get-tuple-element.141), channel_id=1, source_target_pairs={{2,0},{4,2},{6,4},{7,6},{5,7},{3,5},{1,3},{0,1},{10,8},{12,10},{14... | collective-permute-start | bytes 589832 | tf_op jit(solution)/shard_map/ppermute | solution.py:62
  59.0 9.0 %collective-permute-start.14 = (bf16[96,1024]{1,0:T(8,128)(2,1)S(1)}, bf16[96,1024]{1,0:T(8,128)(2,1)S(1)}, u32[]{:S(2)}, u32[]{:S(2)}) collective-permute-start(bf16[96,1024]{1,0:T(8,128)(2,1)S(1)} %get-tuple-element.144), channel_id=1, source_target_pairs={{0,2},{2,4},{4,6},{6,7},{7,5},{5,3},{3,1},{1,0},{8,10},{10,12},{12... | collective-permute-start | bytes 589832 | tf_op jit(solution)/shard_map/ppermute | solution.py:62
  61.7 6.9 %collective-permute-start.15 = (bf16[96,1024]{1,0:T(8,128)(2,1)S(1)}, bf16[96,1024]{1,0:T(8,128)(2,1)S(1)}, u32[]{:S(2)}, u32[]{:S(2)}) collective-permute-start(bf16[96,1024]{1,0:T(8,128)(2,1)S(1)} %get-tuple-element.145), channel_id=1, source_target_pairs={{2,0},{4,2},{6,4},{7,6},{5,7},{3,5},{1,3},{0,1},{10,8},{12,10},{14... | collective-permute-start | bytes 589832 | tf_op jit(solution)/shard_map/ppermute | solution.py:62
  64.5 8.9 %collective-permute-start.16 = (bf16[96,1024]{1,0:T(8,128)(2,1)S(1)}, bf16[96,1024]{1,0:T(8,128)(2,1)S(1)}, u32[]{:S(2)}, u32[]{:S(2)}) collective-permute-start(bf16[96,1024]{1,0:T(8,128)(2,1)S(1)} %get-tuple-element.148), channel_id=1, source_target_pairs={{0,2},{2,4},{4,6},{6,7},{7,5},{5,3},{3,1},{1,0},{8,10},{10,12},{12... | collective-permute-start | bytes 589832 | tf_op jit(solution)/shard_map/ppermute | solution.py:62
  66.6 7.3 %collective-permute-start.17 = (bf16[96,1024]{1,0:T(8,128)(2,1)S(1)}, bf16[96,1024]{1,0:T(8,128)(2,1)S(1)}, u32[]{:S(2)}, u32[]{:S(2)}) collective-permute-start(bf16[96,1024]{1,0:T(8,128)(2,1)S(1)} %get-tuple-element.149), channel_id=1, source_target_pairs={{2,0},{4,2},{6,4},{7,6},{5,7},{3,5},{1,3},{0,1},{10,8},{12,10},{14... | collective-permute-start | bytes 589832 | tf_op jit(solution)/shard_map/ppermute | solution.py:62
  68.6 8.0 %collective-permute-start.18 = (bf16[96,1024]{1,0:T(8,128)(2,1)S(1)}, bf16[96,1024]{1,0:T(8,128)(2,1)S(1)}, u32[]{:S(2)}, u32[]{:S(2)}) collective-permute-start(bf16[96,1024]{1,0:T(8,128)(2,1)S(1)} %get-tuple-element.152), channel_id=1, source_target_pairs={{0,2},{2,4},{4,6},{6,7},{7,5},{5,3},{3,1},{1,0},{8,10},{10,12},{12... | collective-permute-start | bytes 589832 | tf_op jit(solution)/shard_map/ppermute | solution.py:62
  70.6 7.2 %collective-permute-start.19 = (bf16[96,1024]{1,0:T(8,128)(2,1)S(1)}, bf16[96,1024]{1,0:T(8,128)(2,1)S(1)}, u32[]{:S(2)}, u32[]{:S(2)}) collective-permute-start(bf16[96,1024]{1,0:T(8,128)(2,1)S(1)} %get-tuple-element.153), channel_id=1, source_target_pairs={{2,0},{4,2},{6,4},{7,6},{5,7},{3,5},{1,3},{0,1},{10,8},{12,10},{14... | collective-permute-start | bytes 589832 | tf_op jit(solution)/shard_map/ppermute | solution.py:62
  74.0 8.7 %collective-permute-start.20 = (bf16[96,1024]{1,0:T(8,128)(2,1)S(1)}, bf16[96,1024]{1,0:T(8,128)(2,1)S(1)}, u32[]{:S(2)}, u32[]{:S(2)}) collective-permute-start(bf16[96,1024]{1,0:T(8,128)(2,1)S(1)} %get-tuple-element.156), channel_id=1, source_target_pairs={{0,2},{2,4},{4,6},{6,7},{7,5},{5,3},{3,1},{1,0},{8,10},{10,12},{12... | collective-permute-start | bytes 589832 | tf_op jit(solution)/shard_map/ppermute | solution.py:62
  75.6 7.3 %collective-permute-start.21 = (bf16[96,1024]{1,0:T(8,128)(2,1)S(1)}, bf16[96,1024]{1,0:T(8,128)(2,1)S(1)}, u32[]{:S(2)}, u32[]{:S(2)}) collective-permute-start(bf16[96,1024]{1,0:T(8,128)(2,1)S(1)} %get-tuple-element.157), channel_id=1, source_target_pairs={{2,0},{4,2},{6,4},{7,6},{5,7},{3,5},{1,3},{0,1},{10,8},{12,10},{14... | collective-permute-start | bytes 589832 | tf_op jit(solution)/shard_map/ppermute | solution.py:62
  77.9 7.3 %collective-permute-start.22 = (bf16[96,1024]{1,0:T(8,128)(2,1)S(1)}, bf16[96,1024]{1,0:T(8,128)(2,1)S(1)}, u32[]{:S(2)}, u32[]{:S(2)}) collective-permute-start(bf16[96,1024]{1,0:T(8,128)(2,1)S(1)} %get-tuple-element.160), channel_id=1, source_target_pairs={{0,2},{2,4},{4,6},{6,7},{7,5},{5,3},{3,1},{1,0},{8,10},{10,12},{12... | collective-permute-start | bytes 589832 | tf_op jit(solution)/shard_map/ppermute | solution.py:62
  79.4 7.8 %collective-permute-start.23 = (bf16[96,1024]{1,0:T(8,128)(2,1)S(1)}, bf16[96,1024]{1,0:T(8,128)(2,1)S(1)}, u32[]{:S(2)}, u32[]{:S(2)}) collective-permute-start(bf16[96,1024]{1,0:T(8,128)(2,1)S(1)} %get-tuple-element.161), channel_id=1, source_target_pairs={{2,0},{4,2},{6,4},{7,6},{5,7},{3,5},{1,3},{0,1},{10,8},{12,10},{14... | collective-permute-start | bytes 589832 | tf_op jit(solution)/shard_map/ppermute | solution.py:62
  82.9 9.1 %collective-permute-start.24 = (bf16[96,1024]{1,0:T(8,128)(2,1)S(1)}, bf16[96,1024]{1,0:T(8,128)(2,1)S(1)}, u32[]{:S(2)}, u32[]{:S(2)}) collective-permute-start(bf16[96,1024]{1,0:T(8,128)(2,1)S(1)} %get-tuple-element.164), channel_id=1, source_target_pairs={{0,2},{2,4},{4,6},{6,7},{7,5},{5,3},{3,1},{1,0},{8,10},{10,12},{12... | collective-permute-start | bytes 589832 | tf_op jit(solution)/shard_map/ppermute | solution.py:62
  84.3 7.8 %collective-permute-start.25 = (bf16[96,1024]{1,0:T(8,128)(2,1)S(1)}, bf16[96,1024]{1,0:T(8,128)(2,1)S(1)}, u32[]{:S(2)}, u32[]{:S(2)}) collective-permute-start(bf16[96,1024]{1,0:T(8,128)(2,1)S(1)} %get-tuple-element.165), channel_id=1, source_target_pairs={{2,0},{4,2},{6,4},{7,6},{5,7},{3,5},{1,3},{0,1},{10,8},{12,10},{14... | collective-permute-start | bytes 589832 | tf_op jit(solution)/shard_map/ppermute | solution.py:62
  87.2 7.8 %collective-permute-start.26 = (bf16[96,1024]{1,0:T(8,128)(2,1)S(1)}, bf16[96,1024]{1,0:T(8,128)(2,1)S(1)}, u32[]{:S(2)}, u32[]{:S(2)}) collective-permute-start(bf16[96,1024]{1,0:T(8,128)(2,1)S(1)} %get-tuple-element.168), channel_id=1, source_target_pairs={{0,2},{2,4},{4,6},{6,7},{7,5},{5,3},{3,1},{1,0},{8,10},{10,12},{12... | collective-permute-start | bytes 589832 | tf_op jit(solution)/shard_map/ppermute | solution.py:62
  88.4 7.8 %collective-permute-start.27 = (bf16[96,1024]{1,0:T(8,128)(2,1)S(1)}, bf16[96,1024]{1,0:T(8,128)(2,1)S(1)}, u32[]{:S(2)}, u32[]{:S(2)}) collective-permute-start(bf16[96,1024]{1,0:T(8,128)(2,1)S(1)} %get-tuple-element.169), channel_id=1, source_target_pairs={{2,0},{4,2},{6,4},{7,6},{5,7},{3,5},{1,3},{0,1},{10,8},{12,10},{14... | collective-permute-start | bytes 589832 | tf_op jit(solution)/shard_map/ppermute | solution.py:62
  92.1 9.0 %collective-permute-start.28 = (bf16[96,1024]{1,0:T(8,128)(2,1)S(1)}, bf16[96,1024]{1,0:T(8,128)(2,1)S(1)}, u32[]{:S(2)}, u32[]{:S(2)}) collective-permute-start(bf16[96,1024]{1,0:T(8,128)(2,1)S(1)} %get-tuple-element.172), channel_id=1, source_target_pairs={{0,2},{2,4},{4,6},{6,7},{7,5},{5,3},{3,1},{1,0},{8,10},{10,12},{12... | collective-permute-start | bytes 589832 | tf_op jit(solution)/shard_map/ppermute | solution.py:62
  93.3 7.8 %collective-permute-start.29 = (bf16[96,1024]{1,0:T(8,128)(2,1)S(1)}, bf16[96,1024]{1,0:T(8,128)(2,1)S(1)}, u32[]{:S(2)}, u32[]{:S(2)}) collective-permute-start(bf16[96,1024]{1,0:T(8,128)(2,1)S(1)} %get-tuple-element.173), channel_id=1, source_target_pairs={{2,0},{4,2},{6,4},{7,6},{5,7},{3,5},{1,3},{0,1},{10,8},{12,10},{14... | collective-permute-start | bytes 589832 | tf_op jit(solution)/shard_map/ppermute | solution.py:62
  96.3 7.8 %collective-permute-start.30 = (bf16[96,1024]{1,0:T(8,128)(2,1)S(1)}, bf16[96,1024]{1,0:T(8,128)(2,1)S(1)}, u32[]{:S(2)}, u32[]{:S(2)}) collective-permute-start(bf16[96,1024]{1,0:T(8,128)(2,1)S(1)} %get-tuple-element.176), channel_id=1, source_target_pairs={{0,2},{2,4},{4,6},{6,7},{7,5},{5,3},{3,1},{1,0},{8,10},{10,12},{12... | collective-permute-start | bytes 589832 | tf_op jit(solution)/shard_map/ppermute | solution.py:62
  97.0 7.8 %collective-permute-start.31 = (bf16[96,1024]{1,0:T(8,128)(2,1)S(1)}, bf16[96,1024]{1,0:T(8,128)(2,1)S(1)}, u32[]{:S(2)}, u32[]{:S(2)}) collective-permute-start(bf16[96,1024]{1,0:T(8,128)(2,1)S(1)} %get-tuple-element.177), channel_id=1, source_target_pairs={{2,0},{4,2},{6,4},{7,6},{5,7},{3,5},{1,3},{0,1},{10,8},{12,10},{14... | collective-permute-start | bytes 589832 | tf_op jit(solution)/shard_map/ppermute | solution.py:62
  101.2 8.5 %collective-permute-start.32 = (bf16[96,1024]{1,0:T(8,128)(2,1)S(1)}, bf16[96,1024]{1,0:T(8,128)(2,1)S(1)}, u32[]{:S(2)}, u32[]{:S(2)}) collective-permute-start(bf16[96,1024]{1,0:T(8,128)(2,1)S(1)} %get-tuple-element.180), channel_id=1, source_target_pairs={{0,2},{2,4},{4,6},{6,7},{7,5},{5,3},{3,1},{1,0},{8,10},{10,12},{12... | collective-permute-start | bytes 589832 | tf_op jit(solution)/shard_map/ppermute | solution.py:62
  101.9 7.8 %collective-permute-start.33 = (bf16[96,1024]{1,0:T(8,128)(2,1)S(1)}, bf16[96,1024]{1,0:T(8,128)(2,1)S(1)}, u32[]{:S(2)}, u32[]{:S(2)}) collective-permute-start(bf16[96,1024]{1,0:T(8,128)(2,1)S(1)} %get-tuple-element.181), channel_id=1, source_target_pairs={{2,0},{4,2},{6,4},{7,6},{5,7},{3,5},{1,3},{0,1},{10,8},{12,10},{14... | collective-permute-start | bytes 589832 | tf_op jit(solution)/shard_map/ppermute | solution.py:62
  104.8 7.9 %collective-permute-start.34 = (bf16[96,1024]{1,0:T(8,128)(2,1)S(1)}, bf16[96,1024]{1,0:T(8,128)(2,1)S(1)}, u32[]{:S(2)}, u32[]{:S(2)}) collective-permute-start(bf16[96,1024]{1,0:T(8,128)(2,1)S(1)} %get-tuple-element.184), channel_id=1, source_target_pairs={{0,2},{2,4},{4,6},{6,7},{7,5},{5,3},{3,1},{1,0},{8,10},{10,12},{12... | collective-permute-start | bytes 589832 | tf_op jit(solution)/shard_map/ppermute | solution.py:62
  105.9 7.8 %collective-permute-start.35 = (bf16[96,1024]{1,0:T(8,128)(2,1)S(1)}, bf16[96,1024]{1,0:T(8,128)(2,1)S(1)}, u32[]{:S(2)}, u32[]{:S(2)}) collective-permute-start(bf16[96,1024]{1,0:T(8,128)(2,1)S(1)} %get-tuple-element.185), channel_id=1, source_target_pairs={{2,0},{4,2},{6,4},{7,6},{5,7},{3,5},{1,3},{0,1},{10,8},{12,10},{14... | collective-permute-start | bytes 589832 | tf_op jit(solution)/shard_map/ppermute | solution.py:62
  109.7 8.9 %collective-permute-start.36 = (bf16[96,1024]{1,0:T(8,128)(2,1)S(1)}, bf16[96,1024]{1,0:T(8,128)(2,1)S(1)}, u32[]{:S(2)}, u32[]{:S(2)}) collective-permute-start(bf16[96,1024]{1,0:T(8,128)(2,1)S(1)} %get-tuple-element.188), channel_id=1, source_target_pairs={{0,2},{2,4},{4,6},{6,7},{7,5},{5,3},{3,1},{1,0},{8,10},{10,12},{12... | collective-permute-start | bytes 589832 | tf_op jit(solution)/shard_map/ppermute | solution.py:62
  110.8 7.9 %collective-permute-start.37 = (bf16[96,1024]{1,0:T(8,128)(2,1)S(1)}, bf16[96,1024]{1,0:T(8,128)(2,1)S(1)}, u32[]{:S(2)}, u32[]{:S(2)}) collective-permute-start(bf16[96,1024]{1,0:T(8,128)(2,1)S(1)} %get-tuple-element.189), channel_id=1, source_target_pairs={{2,0},{4,2},{6,4},{7,6},{5,7},{3,5},{1,3},{0,1},{10,8},{12,10},{14... | collective-permute-start | bytes 589832 | tf_op jit(solution)/shard_map/ppermute | solution.py:62
  113.8 7.7 %collective-permute-start.38 = (bf16[96,1024]{1,0:T(8,128)(2,1)S(1)}, bf16[96,1024]{1,0:T(8,128)(2,1)S(1)}, u32[]{:S(2)}, u32[]{:S(2)}) collective-permute-start(bf16[96,1024]{1,0:T(8,128)(2,1)S(1)} %get-tuple-element.192), channel_id=1, source_target_pairs={{0,2},{2,4},{4,6},{6,7},{7,5},{5,3},{3,1},{1,0},{8,10},{10,12},{12... | collective-permute-start | bytes 589832 | tf_op jit(solution)/shard_map/ppermute | solution.py:62
  114.9 6.9 %collective-permute-start.39 = (bf16[96,1024]{1,0:T(8,128)(2,1)S(1)}, bf16[96,1024]{1,0:T(8,128)(2,1)S(1)}, u32[]{:S(2)}, u32[]{:S(2)}) collective-permute-start(bf16[96,1024]{1,0:T(8,128)(2,1)S(1)} %get-tuple-element.193), channel_id=1, source_target_pairs={{2,0},{4,2},{6,4},{7,6},{5,7},{3,5},{1,3},{0,1},{10,8},{12,10},{14... | collective-permute-start | bytes 589832 | tf_op jit(solution)/shard_map/ppermute | solution.py:62
  119.5 21.2 %collective-permute-start.40 = (bf16[96,1024]{1,0:T(8,128)(2,1)}, bf16[96,1024]{1,0:T(8,128)(2,1)}, u32[]{:S(2)}, u32[]{:S(2)}) collective-permute-start(bf16[96,1024]{1,0:T(8,128)(2,1)} %get-tuple-element.196), channel_id=1, source_target_pairs={{0,2},{2,4},{4,6},{6,7},{7,5},{5,3},{3,1},{1,0},{8,10},{10,12},{12... | collective-permute-start | bytes 589832 | tf_op jit(solution)/shard_map/ppermute | solution.py:62
  120.5 20.2 %collective-permute-start.41 = (bf16[96,1024]{1,0:T(8,128)(2,1)}, bf16[96,1024]{1,0:T(8,128)(2,1)}, u32[]{:S(2)}, u32[]{:S(2)}) collective-permute-start(bf16[96,1024]{1,0:T(8,128)(2,1)} %get-tuple-element.197), channel_id=1, source_target_pairs={{2,0},{4,2},{6,4},{7,6},{5,7},{3,5},{1,3},{0,1},{10,8},{12,10},{14... | collective-permute-start | bytes 589832 | tf_op jit(solution)/shard_map/ppermute | solution.py:62
  122.6 21.3 %collective-permute-start.42 = (bf16[96,1024]{1,0:T(8,128)(2,1)}, bf16[96,1024]{1,0:T(8,128)(2,1)}, u32[]{:S(2)}, u32[]{:S(2)}) collective-permute-start(bf16[96,1024]{1,0:T(8,128)(2,1)} %get-tuple-element.200), channel_id=1, source_target_pairs={{0,2},{2,4},{4,6},{6,7},{7,5},{5,3},{3,1},{1,0},{8,10},{10,12},{12... | collective-permute-start | bytes 589832 | tf_op jit(solution)/shard_map/ppermute | solution.py:62
  123.6 20.3 %collective-permute-start.43 = (bf16[96,1024]{1,0:T(8,128)(2,1)}, bf16[96,1024]{1,0:T(8,128)(2,1)}, u32[]{:S(2)}, u32[]{:S(2)}) collective-permute-start(bf16[96,1024]{1,0:T(8,128)(2,1)} %get-tuple-element.201), channel_id=1, source_target_pairs={{2,0},{4,2},{6,4},{7,6},{5,7},{3,5},{1,3},{0,1},{10,8},{12,10},{14... | collective-permute-start | bytes 589832 | tf_op jit(solution)/shard_map/ppermute | solution.py:62
  129.8 72.4 %all-to-all-start.1 = ((bf16[16,16,2048]{2,1,0:T(8,128)(2,1)}), bf16[16,16,2048]{2,1,0:T(8,128)(2,1)S(1)}, u32[]{:S(2)}, u32[]{:S(2)}) async-start(bf16[16,16,2048]{2,1,0:T(8,128)(2,1)} %bitcast.217), calls=%async_computation.1 | async-start | bytes 2097152 | tf_op jit(solution)/shard_map/all_to_all | solution.py:101
  141.8 15.1 %collective-permute-start.44 = (bf16[96,1024]{1,0:T(8,128)(2,1)S(1)}, bf16[96,1024]{1,0:T(8,128)(2,1)S(1)}, u32[]{:S(2)}, u32[]{:S(2)}) collective-permute-start(bf16[96,1024]{1,0:T(8,128)(2,1)S(1)} %get-tuple-element.204), channel_id=1, source_target_pairs={{0,2},{2,4},{4,6},{6,7},{7,5},{5,3},{3,1},{1,0},{8,10},{10,12},{12... | collective-permute-start | bytes 589832 | tf_op jit(solution)/shard_map/ppermute | solution.py:62
  143.7 13.6 %collective-permute-start.45 = (bf16[96,1024]{1,0:T(8,128)(2,1)S(1)}, bf16[96,1024]{1,0:T(8,128)(2,1)S(1)}, u32[]{:S(2)}, u32[]{:S(2)}) collective-permute-start(bf16[96,1024]{1,0:T(8,128)(2,1)S(1)} %get-tuple-element.205), channel_id=1, source_target_pairs={{2,0},{4,2},{6,4},{7,6},{5,7},{3,5},{1,3},{0,1},{10,8},{12,10},{14... | collective-permute-start | bytes 589832 | tf_op jit(solution)/shard_map/ppermute | solution.py:62
  145.0 21.1 %collective-permute-start.46 = (bf16[96,1024]{1,0:T(8,128)(2,1)S(1)}, bf16[96,1024]{1,0:T(8,128)(2,1)S(1)}, u32[]{:S(2)}, u32[]{:S(2)}) collective-permute-start(bf16[96,1024]{1,0:T(8,128)(2,1)S(1)} %get-tuple-element.208), channel_id=1, source_target_pairs={{0,2},{2,4},{4,6},{6,7},{7,5},{5,3},{3,1},{1,0},{8,10},{10,12},{12... | collective-permute-start | bytes 589832 | tf_op jit(solution)/shard_map/ppermute | solution.py:62
  146.9 19.2 %collective-permute-start.47 = (bf16[96,1024]{1,0:T(8,128)(2,1)S(1)}, bf16[96,1024]{1,0:T(8,128)(2,1)S(1)}, u32[]{:S(2)}, u32[]{:S(2)}) collective-permute-start(bf16[96,1024]{1,0:T(8,128)(2,1)S(1)} %get-tuple-element.209), channel_id=1, source_target_pairs={{2,0},{4,2},{6,4},{7,6},{5,7},{3,5},{1,3},{0,1},{10,8},{12,10},{14... | collective-permute-start | bytes 589832 | tf_op jit(solution)/shard_map/ppermute | solution.py:62
  157.4 15.7 %collective-permute-start.48 = (bf16[96,1024]{1,0:T(8,128)(2,1)S(1)}, bf16[96,1024]{1,0:T(8,128)(2,1)S(1)}, u32[]{:S(2)}, u32[]{:S(2)}) collective-permute-start(bf16[96,1024]{1,0:T(8,128)(2,1)S(1)} %get-tuple-element.212), channel_id=1, source_target_pairs={{0,2},{2,4},{4,6},{6,7},{7,5},{5,3},{3,1},{1,0},{8,10},{10,12},{12... | collective-permute-start | bytes 589832 | tf_op jit(solution)/shard_map/ppermute | solution.py:62
  166.1 7.0 %collective-permute-start.49 = (bf16[96,1024]{1,0:T(8,128)(2,1)S(1)}, bf16[96,1024]{1,0:T(8,128)(2,1)S(1)}, u32[]{:S(2)}, u32[]{:S(2)}) collective-permute-start(bf16[96,1024]{1,0:T(8,128)(2,1)S(1)} %get-tuple-element.213), channel_id=1, source_target_pairs={{2,0},{4,2},{6,4},{7,6},{5,7},{3,5},{1,3},{0,1},{10,8},{12,10},{14... | collective-permute-start | bytes 589832 | tf_op jit(solution)/shard_map/ppermute | solution.py:62
  166.2 9.1 %collective-permute-start.50 = (bf16[96,1024]{1,0:T(8,128)(2,1)S(1)}, bf16[96,1024]{1,0:T(8,128)(2,1)S(1)}, u32[]{:S(2)}, u32[]{:S(2)}) collective-permute-start(bf16[96,1024]{1,0:T(8,128)(2,1)S(1)} %get-tuple-element.216), channel_id=1, source_target_pairs={{0,2},{2,4},{4,6},{6,7},{7,5},{5,3},{3,1},{1,0},{8,10},{10,12},{12... | collective-permute-start | bytes 589832 | tf_op jit(solution)/shard_map/ppermute | solution.py:62
  170.3 5.7 %collective-permute-start.51 = (bf16[96,1024]{1,0:T(8,128)(2,1)S(1)}, bf16[96,1024]{1,0:T(8,128)(2,1)S(1)}, u32[]{:S(2)}, u32[]{:S(2)}) collective-permute-start(bf16[96,1024]{1,0:T(8,128)(2,1)S(1)} %get-tuple-element.217), channel_id=1, source_target_pairs={{2,0},{4,2},{6,4},{7,6},{5,7},{3,5},{1,3},{0,1},{10,8},{12,10},{14... | collective-permute-start | bytes 589832 | tf_op jit(solution)/shard_map/ppermute | solution.py:62
  173.2 8.3 %collective-permute-start.52 = (bf16[96,1024]{1,0:T(8,128)(2,1)S(1)}, bf16[96,1024]{1,0:T(8,128)(2,1)S(1)}, u32[]{:S(2)}, u32[]{:S(2)}) collective-permute-start(bf16[96,1024]{1,0:T(8,128)(2,1)S(1)} %get-tuple-element.220), channel_id=1, source_target_pairs={{0,2},{2,4},{4,6},{6,7},{7,5},{5,3},{3,1},{1,0},{8,10},{10,12},{12... | collective-permute-start | bytes 589832 | tf_op jit(solution)/shard_map/ppermute | solution.py:62
  175.2 6.3 %collective-permute-start.53 = (bf16[96,1024]{1,0:T(8,128)(2,1)S(1)}, bf16[96,1024]{1,0:T(8,128)(2,1)S(1)}, u32[]{:S(2)}, u32[]{:S(2)}) collective-permute-start(bf16[96,1024]{1,0:T(8,128)(2,1)S(1)} %get-tuple-element.221), channel_id=1, source_target_pairs={{2,0},{4,2},{6,4},{7,6},{5,7},{3,5},{1,3},{0,1},{10,8},{12,10},{14... | collective-permute-start | bytes 589832 | tf_op jit(solution)/shard_map/ppermute | solution.py:62
  176.1 7.1 %collective-permute-start.54 = (bf16[96,1024]{1,0:T(8,128)(2,1)S(1)}, bf16[96,1024]{1,0:T(8,128)(2,1)S(1)}, u32[]{:S(2)}, u32[]{:S(2)}) collective-permute-start(bf16[96,1024]{1,0:T(8,128)(2,1)S(1)} %get-tuple-element.224), channel_id=1, source_target_pairs={{0,2},{2,4},{4,6},{6,7},{7,5},{5,3},{3,1},{1,0},{8,10},{10,12},{12... | collective-permute-start | bytes 589832 | tf_op jit(solution)/shard_map/ppermute | solution.py:62
  178.7 6.4 %collective-permute-start.55 = (bf16[96,1024]{1,0:T(8,128)(2,1)S(1)}, bf16[96,1024]{1,0:T(8,128)(2,1)S(1)}, u32[]{:S(2)}, u32[]{:S(2)}) collective-permute-start(bf16[96,1024]{1,0:T(8,128)(2,1)S(1)} %get-tuple-element.225), channel_id=1, source_target_pairs={{2,0},{4,2},{6,4},{7,6},{5,7},{3,5},{1,3},{0,1},{10,8},{12,10},{14... | collective-permute-start | bytes 589832 | tf_op jit(solution)/shard_map/ppermute | solution.py:62
  (17 other events, 66.6 us)

commit v2 on v1

v2 whole, which is shorter than its diff:
```python
import functools

import jax
import jax.numpy as jnp
from jax import lax
from jax.experimental import pallas as pl
from jax.experimental.pallas import tpu as pltpu
from jax.sharding import PartitionSpec as P

CHUNKS = 16
BLOCKS = 2


def ring_order(mesh):
    n = mesh.shape["shadow"]
    axis = mesh.axis_names.index("shadow")
    index = [0] * mesh.devices.ndim
    spots = []
    for s in range(n):
        index[axis] = s
        spots.append(tuple(getattr(mesh.devices[tuple(index)], "coords", (s,))))
    varying = [a for a in range(len(spots[0])) if len({p[a] for p in spots}) > 1]
    if len(varying) == 2:
        sizes = [len({p[a] for p in spots}) for a in varying]
        if 2 in sizes:
            short = varying[sizes.index(2)]
            long = varying[1 - sizes.index(2)]
            low = min(p[short] for p in spots)
            one = sorted((s for s in range(n) if spots[s][short] == low), key=lambda s: spots[s][long])
            two = sorted((s for s in range(n) if spots[s][short] != low), key=lambda s: -spots[s][long])
            return one + two
    return list(range(n))


def swiglu(pre, hidden_units):
    return (jax.nn.silu(pre[:, :hidden_units]) * pre[:, hidden_units:]).astype(jnp.bfloat16)


def hot_kernel(n, chunks, lag, hops, x, weight, gate_up, down, *rest):
    came = rest[:-5]
    out, gate_all, down_all, gate_sem, down_sem = rest[-5:]
    middle, half = gate_all.shape[0] // 2, down_all.shape[1] // 2
    rows = (middle + down_all.shape[0]) // chunks

    @pl.when(pl.program_id(0) == 0)
    def _():
        @pl.when(hops[0] == 0)
        def _():
            pltpu.make_async_copy(gate_up, gate_all, gate_sem).start()
            pltpu.make_async_copy(down, down_all, down_sem).start()

        for way in range(2):
            for h in range(1, n):

                @pl.when(hops[way] == h)
                def _(way=way, h=h):
                    for c in range(chunks):
                        source = came[2 * (c + lag * (h - 1)) + way]
                        at = c * rows
                        gate = min(max(middle - at, 0), rows)
                        if gate:
                            target = gate_all.at[pl.ds(way * middle + at, gate), :]
                            pltpu.make_async_copy(source.at[pl.ds(0, gate), :], target, gate_sem).start()
                        if gate < rows:
                            target = down_all.at[pl.ds(at + gate - middle, rows - gate), pl.ds(way * half, half)]
                            pltpu.make_async_copy(source.at[pl.ds(gate, rows - gate), :], target, down_sem).start()

        pltpu.make_async_copy(gate_all, gate_all, gate_sem).wait()

    pre = jnp.dot(x[...], gate_all[...], preferred_element_type=jnp.float32)
    hidden = swiglu(pre, down_all.shape[0])

    @pl.when(pl.program_id(0) == 0)
    def _():
        pltpu.make_async_copy(down_all, down_all, down_sem).wait()

    total = jnp.dot(hidden, down_all[...], preferred_element_type=jnp.float32)
    out[...] = (total * weight[...]).astype(out.dtype)


def hot_expert(n, lag, hops, x, weight, gate_up, down, came):
    tokens, width = x.shape
    block = tokens // BLOCKS
    whole = pl.BlockSpec(memory_space=pl.ANY)
    return pl.pallas_call(
        functools.partial(hot_kernel, n, CHUNKS, lag),
        grid=(BLOCKS,),
        out_shape=jax.ShapeDtypeStruct((tokens, width), jnp.bfloat16),
        in_specs=[
            pl.BlockSpec(memory_space=pltpu.SMEM),
            pl.BlockSpec((block, width), lambda i: (i, 0)),
            pl.BlockSpec((block, 1), lambda i: (i, 0)),
            whole,
            whole,
            *[whole for _ in came],
        ],
        out_specs=pl.BlockSpec((block, width), lambda i: (i, 0)),
        scratch_shapes=[
            pltpu.VMEM(gate_up.shape, gate_up.dtype),
            pltpu.VMEM(down.shape, down.dtype),
            pltpu.SemaphoreType.DMA,
            pltpu.SemaphoreType.DMA,
        ],
        compiler_params=pltpu.CompilerParams(vmem_limit_bytes=60 * 2**20),
        cost_estimate=pl.CostEstimate(
            flops=2 * tokens * (gate_up.size + down.size), bytes_accessed=20 * 2**20, transcendentals=0
        ),
    )(hops, x, weight, gate_up, down, *came)


def cut(parts, start, size):
    out = []
    for part in parts:
        low, high = max(start, 0), min(start + size, part.shape[0])
        if low < high:
            out.append(part[low:high])
        start -= part.shape[0]
    return out[0] if len(out) == 1 else jnp.concatenate(out, 0)


def join(*values):
    return lax.optimization_barrier(values)


def body(order, hot_root, res_rows, res_weight, cold_rows, cold_experts, cold_weights, w_gate_up, w_down):
    gate_up, down = w_gate_up[0], w_down[0]
    hidden_units, width = down.shape
    n = len(order)
    lag = 2 if n < CHUNKS else 1
    n_owners = lax.axis_size("ep") * n
    per_device, fan_out = cold_experts.shape
    capacity = max(2, 2 * per_device * fan_out // n_owners)

    slot = lax.broadcasted_iota(jnp.int32, (per_device, n_owners * capacity), 1)
    named = [cold_experts[:, k : k + 1] == slot // capacity for k in range(fan_out)]
    count = sum(m.astype(jnp.bfloat16) for m in named)
    before = (
        lax.broadcasted_iota(jnp.int32, (per_device, per_device), 0)
        > lax.broadcasted_iota(jnp.int32, (per_device, per_device), 1)
    ).astype(jnp.bfloat16)
    rank = jnp.dot(before, count, preferred_element_type=jnp.float32)
    here = rank == (slot % capacity).astype(jnp.float32)
    chosen = [m & here for m in named]
    placed = sum(m.astype(jnp.bfloat16) for m in chosen)
    outgoing = lax.dot_general(
        placed, cold_rows, (((0,), (0,)), ((), ())), preferred_element_type=jnp.float32
    ).astype(jnp.bfloat16)
    cold = lax.all_to_all(outgoing, ("ep", "shadow"), 0, 0, tiled=True)

    root = hot_root[lax.axis_index("ep")]
    half, middle = width // 2, gate_up.shape[0] // 2
    lanes = ([gate_up[:middle], down[:, :half]], [gate_up[middle:], down[:, half:]])
    rows = (middle + hidden_units) // CHUNKS
    own = [[cut(lane, c * rows, rows) for c in range(CHUNKS)] for lane in lanes]
    place = jnp.array([order.index(s) for s in range(n)], jnp.int32)
    me = lax.axis_index("shadow")
    ahead = (place[me] - place[root]) % n
    hops = jnp.stack([ahead, (n - ahead) % n])
    ways = (
        [(order[i], order[(i + 1) % n]) for i in range(n)],
        [(order[(i + 1) % n], order[i]) for i in range(n)],
    )
    weight = res_weight[:, None]
    steps = CHUNKS + (n - 2) * lag
    came, last = [], None
    for t in range(steps):
        mine = tuple(own[i][t] for i in range(2)) if t < CHUNKS else None
        if t >= lag:
            got = came[t - lag]
            if t == lag + 1:
                got, hops, weight = join(got, hops, weight)
            elif t == steps * 3 // 8:
                got, cold = join(got, cold)
                pre = jnp.dot(cold, gate_up, preferred_element_type=jnp.float32)
                cold = jnp.dot(swiglu(pre, hidden_units), down, preferred_element_type=jnp.float32).astype(jnp.bfloat16)
            elif t == steps * 3 // 8 + 1:
                got, cold = join(got, cold)
                cold = lax.all_to_all(cold, ("ep", "shadow"), 0, 0, tiled=True)
            elif t == steps * 7 // 8:
                got, cold = join(got, cold)
                scale = sum(jnp.where(chosen[k], cold_weights[:, k : k + 1], 0.0) for k in range(fan_out))
                high = lax.reduce_precision(scale, 8, 7)
                low = (scale - high).astype(jnp.bfloat16)
                cold = (
                    jnp.dot(high.astype(jnp.bfloat16), cold, preferred_element_type=jnp.float32)
                    + jnp.dot(low, cold, preferred_element_type=jnp.float32)
                ).astype(jnp.bfloat16)
            got, _ = join(got, last)
            mine = tuple(jnp.where(me == root, m, g) for m, g in zip(mine, got)) if t < CHUNKS else got
        mine = last = join(*mine)
        came.append(tuple(lax.ppermute(mine[i], "shadow", ways[i]) for i in range(2)))
    came, cold = join(came, cold)
    hot_out = hot_expert(n, lag, hops, res_rows, weight, gate_up, down, [c for pair in came for c in pair])
    return hot_out, cold


def solution(mesh):
    order = ring_order(mesh)
    rows = P(("parts", "ep", "shadow"), None)
    owners = P(("ep", "shadow"), None, None)
    in_specs = (P("parts"), rows, P(("parts", "ep", "shadow")), rows, rows, rows, owners, owners)
    return jax.shard_map(
        lambda *args: body(order, *args), mesh=mesh, in_specs=in_specs, out_specs=(rows, rows), check_vma=False
    )
```

time: 204 us -> 198 us (0.971)
  local copies, waits for them, and re-layouts: 60.4 us -> 10.3 us
  waiting for transfers between devices: 28.7 us -> 58.7 us
  matrix products: 19.7 us -> 8.27 us
  Pallas kernels: 0 us -> 10.8 us
  starting transfers between devices: 80 us -> 88.5 us
  other arithmetic: 9.74 us -> 15.3 us
    dynamic_update_slice x60 -> x0, local copies, waits for them, and re-layouts: 48.9 us -> none  [ring_broadcast(): held[i] = lax.dynamic_update_slice(held[i], mine[i][None], (at, 0, 0))]
    ppermute x56, waiting for transfers between devices: 28.7 us -> 58.6 us  [body(): lax.ppermute(mine[i], 'shadow', ways[i])]
    dot_general x7 -> x3, matrix products: 16.2 us -> 4.82 us  [the longest x1 3.43 us: body(): pre = jnp.dot(cold, gate_up, preferred_element_type=jnp.float32)]
    pallas_call x0 -> x1, Pallas kernels: none -> 10.8 us  [hot_expert(): pl.pallas_call(functools.partial(hot_kernel, n, CHUNKS, lag), grid=(BLOCK...]
    ppermute x56, starting transfers between devices: 69.2 us -> 77.1 us  [body(): lax.ppermute(mine[i], 'shadow', ways[i])]
    select_n x28 -> x14, other arithmetic: 7.27 us -> 14.7 us  [body(): jnp.where(me == root, m, g)]
    another operation x2 -> x0, local copies, waits for them, and re-layouts: 4.13 us -> none
  transfers between devices with their start and end apart: 58 -> 58, of which waited for: 28 -> 27; matrix products, arithmetic and copies ran while one was open for 42% -> 15% of each run, Pallas kernels for 0% -> 0%
where the time goes in v2:
time: 198 us; the launch traced here: 197 us
  starting transfers between devices  88.5 us (45%)
  waiting for transfers between devices  58.7 us (30%)
  other arithmetic  15.3 us (8%)
  Pallas kernels  10.8 us (5%)
  local copies, waits for them, and re-layouts  10.3 us (5%)
  matrix products  8.27 us (4%)
  between operations  5.23 us (3%)
    ppermute x56, starting transfers between devices, body(): lax.ppermute(mine[i], 'shadow', ways[i])  77.1 us
    ppermute x56, waiting for transfers between devices, body(): lax.ppermute(mine[i], 'shadow', ways[i])  58.6 us
    select_n x14, other arithmetic, body(): jnp.where(me == root, m, g)  14.7 us
    pallas_call x1, Pallas kernels, hot_expert(): pl.pallas_call(functools.partial(hot_kernel, n, CHUNKS, lag), grid=(BLOCK...  10.8 us
    all_to_all x1, starting transfers between devices, body(): cold = lax.all_to_all(outgoing, ('ep', 'shadow'), 0, 0, tiled=True)  6.38 us
    all_to_all x1, starting transfers between devices, body(): cold = lax.all_to_all(cold, ('ep', 'shadow'), 0, 0, tiled=True)  4.97 us
    slice x3, local copies, waits for them, and re-layouts, cut(): out.append(part[low:high])  4.54 us
  transfers between devices with their start and end apart: 58, of which 27 were waited for; matrix products, arithmetic and copies ran while one was open for 15% of the time, Pallas kernels for 0%

profile of v2, /device:TPU:0, one launch (start us, length us, event | category | flops | bytes accessed | tf_op | source)
XLA Modules:
  0.0 197.1 jit_solution(14575497041957977399)
XLA Ops:
  0.7 2.2 %slice_bitcast_fusion = (bf16[96,1024]{1,0:T(8,128)(2,1)}, bf16[96,1024]{1,0:T(8,128)(2,1)}, bf16[96,1024]{1,0:T(8,128)(2,1)}, bf16[96,1024]{1,0:T(8,128)(2,1)}) fusion(bf16[1,2048,1024]{2,1,0:T(8,128)(2,1)} %param.15), kind=kLoop, calls=%fused_computation.36 | loop fusion | bytes 1572864 | tf_op jit(solution)/shard_map/slice | solution.py:116
  2.9 3.0 %collective-permute-start = (bf16[96,1024]{1,0:T(8,128)(2,1)}, bf16[96,1024]{1,0:T(8,128)(2,1)}, u32[]{:S(2)}, u32[]{:S(2)}) collective-permute-start(bf16[96,1024]{1,0:T(8,128)(2,1)} %get-tuple-element.180), channel_id=1, source_target_pairs={{0,2},{2,4},{4,6},{6,7},{7,5},{5,3},{3,1},{1,0},{8,10},{10,12},{12... | collective-permute-start | bytes 589832 | tf_op jit(solution)/shard_map/ppermute | solution.py:191
  6.0 2.0 %collective-permute-start.2 = (bf16[96,1024]{1,0:T(8,128)(2,1)}, bf16[96,1024]{1,0:T(8,128)(2,1)}, u32[]{:S(2)}, u32[]{:S(2)}) collective-permute-start(bf16[96,1024]{1,0:T(8,128)(2,1)} %get-tuple-element.184), channel_id=1, source_target_pairs={{0,2},{2,4},{4,6},{6,7},{7,5},{5,3},{3,1},{1,0},{8,10},{10,12},{12... | collective-permute-start | bytes 589832 | tf_op jit(solution)/shard_map/ppermute | solution.py:191
  9.1 1.5 convolution_convert_fusion.1
  10.6 6.4 %all-to-all-start = ((bf16[16,16,2048]{2,1,0:T(8,128)(2,1)}), bf16[16,16,2048]{2,1,0:T(8,128)(2,1)S(1)}, u32[]{:S(2)}, u32[]{:S(2)}) async-start(bf16[16,16,2048]{2,1,0:T(8,128)(2,1)} %bitcast.29), calls=%async_computation | async-start | bytes 2097152 | tf_op jit(solution)/shard_map/all_to_all | solution.py:148
  22.0 1.6 slice_bitcast_fusion.4
  23.6 1.3 broadcast_in_dim.25
  26.2 1.3 bitcast_select_fusion.14
  27.5 2.0 collective-permute-start.4
  29.5 1.3 bitcast_select_fusion.12
  30.8 2.0 collective-permute-start.6
  32.9 6.7 %collective-permute-done.4.rest_4_ = bf16[96,1024]{1,0:T(8,128)(2,1)S(1)} collective-permute-done((bf16[96,1024]{1,0:T(8,128)(2,1)S(1)}, bf16[96,1024]{1,0:T(8,128)(2,1)S(1)}, u32[]{:S(2)}, u32[]{:S(2)}) %collective-permute-start.4) | collective-permute-done | bytes 196640 | tf_op jit(solution)/shard_map/ppermute | solution.py:191
  39.6 3.1 %collective-permute-done.5.rest_5_ = bf16[96,1024]{1,0:T(8,128)(2,1)S(1)} collective-permute-done((bf16[96,1024]{1,0:T(8,128)(2,1)S(1)}, bf16[96,1024]{1,0:T(8,128)(2,1)S(1)}, u32[]{:S(2)}, u32[]{:S(2)}) %collective-permute-start.5) | collective-permute-done | bytes 196640 | tf_op jit(solution)/shard_map/ppermute | solution.py:191
  42.7 1.2 bitcast_select_fusion.10
  43.9 6.1 %collective-permute-start.8 = (bf16[96,1024]{1,0:T(8,128)(2,1)S(1)}, bf16[96,1024]{1,0:T(8,128)(2,1)S(1)}, u32[]{:S(2)}, u32[]{:S(2)}) collective-permute-start(bf16[96,1024]{1,0:T(8,128)(2,1)S(1)} %get-tuple-element.198), channel_id=1, source_target_pairs={{0,2},{2,4},{4,6},{6,7},{7,5},{5,3},{3,1},{1,0},{8,10},{10,12},{12... | collective-permute-start | bytes 589832 | tf_op jit(solution)/shard_map/ppermute | solution.py:191
  50.0 1.2 bitcast_select_fusion.8
  51.2 2.5 %collective-permute-start.10 = (bf16[96,1024]{1,0:T(8,128)(2,1)S(1)}, bf16[96,1024]{1,0:T(8,128)(2,1)S(1)}, u32[]{:S(2)}, u32[]{:S(2)}) collective-permute-start(bf16[96,1024]{1,0:T(8,128)(2,1)S(1)} %get-tuple-element.202), channel_id=1, source_target_pairs={{0,2},{2,4},{4,6},{6,7},{7,5},{5,3},{3,1},{1,0},{8,10},{10,12},{12... | collective-permute-start | bytes 589832 | tf_op jit(solution)/shard_map/ppermute | solution.py:191
  53.7 1.9 collective-permute-done.9.rest_9_
  55.7 1.2 bitcast_select_fusion.6
  56.8 1.1 collective-permute-start.12
  58.9 1.7 collective-permute-done.11.rest_11_
  60.6 1.2 bitcast_select_fusion.4
  64.8 1.2 bitcast_select_fusion.2
  66.9 1.1 collective-permute-start.17
  69.6 1.9 bitcast_select_fusion
  72.0 1.4 collective-permute-start.19
  74.3 2.0 %maximum_select_fusion = (bf16[96,1024]{1,0:T(8,128)(2,1)}, bf16[96,1024]{1,0:T(8,128)(2,1)}) fusion(bf16[96,1024]{1,0:T(8,128)(2,1)} %copy-done.14, bf16[32,1024]{1,0:T(8,128)(2,1)} %get-tuple-element.391, bf16[64,1024]{1,0:T(8,128)(2,1)} %get-tuple-element.359, pred[]{:T(512)S(6)} %eq.21, bf16[96,1024]{1,0:T(8,128)(2,1)} %collective-permute-done.17.rest_17_, ...), kind=kLoop, calls=%fused_computation.18 | loop fusion | flops 983040 | bytes 1179649 | tf_op jit(solution)/shard_map/jit(_where)/select_n | solution.py:189
  76.9 1.4 collective-permute-start.21
  78.3 3.4 %fusion.31 = f32[256,1024]{1,0:T(8,128)S(1)} fusion(bf16[256,2048]{1,0:T(8,128)(2,1)S(1)} %bitcast.80, bf16[1,2048,1024]{2,1,0:T(8,128)(2,1)} %param.15), kind=kOutput, calls=%fused_computation.83 | convolution fusion | flops 1073741824 | bytes 6291456 | tf_op jit(solution)/shard_map/dot_general | solution.py:174
  81.8 1.7 convolution_convert_fusion
  83.6 5.0 %all-to-all-start.1 = ((bf16[16,16,2048]{2,1,0:T(8,128)(2,1)}), bf16[16,16,2048]{2,1,0:T(8,128)(2,1)S(1)}, u32[]{:S(2)}, u32[]{:S(2)}) async-start(bf16[16,16,2048]{2,1,0:T(8,128)(2,1)} %bitcast.81), calls=%async_computation.1 | async-start | bytes 2097152 | tf_op jit(solution)/shard_map/all_to_all | solution.py:178
  89.6 2.0 collective-permute-start.22
  92.8 2.0 collective-permute-start.24
  94.9 16.3 %collective-permute-done.22.rest_22_ = bf16[96,1024]{1,0:T(8,128)(2,1)S(1)} collective-permute-done((bf16[96,1024]{1,0:T(8,128)(2,1)S(1)}, bf16[96,1024]{1,0:T(8,128)(2,1)S(1)}, u32[]{:S(2)}, u32[]{:S(2)}) %collective-permute-start.22) | collective-permute-done | bytes 196640 | tf_op jit(solution)/shard_map/ppermute | solution.py:191
  111.9 8.5 %collective-permute-start.26 = (bf16[96,1024]{1,0:T(8,128)(2,1)S(1)}, bf16[96,1024]{1,0:T(8,128)(2,1)S(1)}, u32[]{:S(2)}, u32[]{:S(2)}) collective-permute-start(bf16[96,1024]{1,0:T(8,128)(2,1)S(1)} %get-tuple-element.239), channel_id=1, source_target_pairs={{0,2},{2,4},{4,6},{6,7},{7,5},{5,3},{3,1},{1,0},{8,10},{10,12},{12... | collective-permute-start | bytes 589832 | tf_op jit(solution)/shard_map/ppermute | solution.py:191
  120.5 4.1 %collective-permute-start.28 = (bf16[96,1024]{1,0:T(8,128)(2,1)S(1)}, bf16[96,1024]{1,0:T(8,128)(2,1)S(1)}, u32[]{:S(2)}, u32[]{:S(2)}) collective-permute-start(bf16[96,1024]{1,0:T(8,128)(2,1)S(1)} %get-tuple-element.243), channel_id=1, source_target_pairs={{0,2},{2,4},{4,6},{6,7},{7,5},{5,3},{3,1},{1,0},{8,10},{10,12},{12... | collective-permute-start | bytes 589832 | tf_op jit(solution)/shard_map/ppermute | solution.py:191
  124.7 1.5 collective-permute-done.27.rest_27_
  126.2 2.7 %collective-permute-start.30 = (bf16[96,1024]{1,0:T(8,128)(2,1)S(1)}, bf16[96,1024]{1,0:T(8,128)(2,1)S(1)}, u32[]{:S(2)}, u32[]{:S(2)}) collective-permute-start(bf16[96,1024]{1,0:T(8,128)(2,1)S(1)} %get-tuple-element.247), channel_id=1, source_target_pairs={{0,2},{2,4},{4,6},{6,7},{7,5},{5,3},{3,1},{1,0},{8,10},{10,12},{12... | collective-permute-start | bytes 589832 | tf_op jit(solution)/shard_map/ppermute | solution.py:191
  128.9 1.4 collective-permute-done.29.rest_29_
  130.3 2.6 %collective-permute-start.32 = (bf16[96,1024]{1,0:T(8,128)(2,1)S(1)}, bf16[96,1024]{1,0:T(8,128)(2,1)S(1)}, u32[]{:S(2)}, u32[]{:S(2)}) collective-permute-start(bf16[96,1024]{1,0:T(8,128)(2,1)S(1)} %collective-permute-done.28.rest_28_), channel_id=1, source_target_pairs={{0,2},{2,4},{4,6},{6,7},{7,5},{5,3},{3,1},{1,0},{8,10},{10,12},{12... | collective-permute-start | bytes 589832 | tf_op jit(solution)/shard_map/ppermute | solution.py:191
  133.3 1.4 collective-permute-done.31.rest_31_
  134.7 2.5 %collective-permute-start.34 = (bf16[96,1024]{1,0:T(8,128)(2,1)S(1)}, bf16[96,1024]{1,0:T(8,128)(2,1)S(1)}, u32[]{:S(2)}, u32[]{:S(2)}) collective-permute-start(bf16[96,1024]{1,0:T(8,128)(2,1)S(1)} %collective-permute-done.30.rest_30_), channel_id=1, source_target_pairs={{0,2},{2,4},{4,6},{6,7},{7,5},{5,3},{3,1},{1,0},{8,10},{10,12},{12... | collective-permute-start | bytes 589832 | tf_op jit(solution)/shard_map/ppermute | solution.py:191
  137.2 1.7 collective-permute-done.33.rest_33_
  138.9 2.5 %collective-permute-start.36 = (bf16[96,1024]{1,0:T(8,128)(2,1)S(1)}, bf16[96,1024]{1,0:T(8,128)(2,1)S(1)}, u32[]{:S(2)}, u32[]{:S(2)}) collective-permute-start(bf16[96,1024]{1,0:T(8,128)(2,1)S(1)} %collective-permute-done.32.rest_32_), channel_id=1, source_target_pairs={{0,2},{2,4},{4,6},{6,7},{7,5},{5,3},{3,1},{1,0},{8,10},{10,12},{12... | collective-permute-start | bytes 589832 | tf_op jit(solution)/shard_map/ppermute | solution.py:191
  141.4 1.7 collective-permute-done.35.rest_35_
  143.1 2.5 %collective-permute-start.38 = (bf16[96,1024]{1,0:T(8,128)(2,1)S(1)}, bf16[96,1024]{1,0:T(8,128)(2,1)S(1)}, u32[]{:S(2)}, u32[]{:S(2)}) collective-permute-start(bf16[96,1024]{1,0:T(8,128)(2,1)S(1)} %collective-permute-done.34.rest_34_), channel_id=1, source_target_pairs={{0,2},{2,4},{4,6},{6,7},{7,5},{5,3},{3,1},{1,0},{8,10},{10,12},{12... | collective-permute-start | bytes 589832 | tf_op jit(solution)/shard_map/ppermute | solution.py:191
  145.6 1.7 collective-permute-done.37.rest_37_
  147.3 2.5 %collective-permute-start.40 = (bf16[96,1024]{1,0:T(8,128)(2,1)S(1)}, bf16[96,1024]{1,0:T(8,128)(2,1)}, u32[]{:S(2)}, u32[]{:S(2)}) collective-permute-start(bf16[96,1024]{1,0:T(8,128)(2,1)S(1)} %collective-permute-done.36.rest_36_), channel_id=1, source_target_pairs={{0,2},{2,4},{4,6},{6,7},{7,5},{5,3},{3,1},{1,0},{8,10},{10,12},{12... | collective-permute-start | bytes 589832 | tf_op jit(solution)/shard_map/ppermute | solution.py:191
  149.8 1.7 collective-permute-done.39.rest_39_
  151.5 2.5 %collective-permute-start.42 = (bf16[96,1024]{1,0:T(8,128)(2,1)S(1)}, bf16[96,1024]{1,0:T(8,128)(2,1)}, u32[]{:S(2)}, u32[]{:S(2)}) collective-permute-start(bf16[96,1024]{1,0:T(8,128)(2,1)S(1)} %collective-permute-done.38.rest_38_), channel_id=1, source_target_pairs={{0,2},{2,4},{4,6},{6,7},{7,5},{5,3},{3,1},{1,0},{8,10},{10,12},{12... | collective-permute-start | bytes 589832 | tf_op jit(solution)/shard_map/ppermute | solution.py:191
  154.0 1.8 collective-permute-done.41.rest_41_
  155.8 2.5 %collective-permute-start.44 = (bf16[96,1024]{1,0:T(8,128)(2,1)}, bf16[96,1024]{1,0:T(8,128)(2,1)}, u32[]{:S(2)}, u32[]{:S(2)}) collective-permute-start(bf16[96,1024]{1,0:T(8,128)(2,1)} %collective-permute-done.40.rest_40_), channel_id=1, source_target_pairs={{0,2},{2,4},{4,6},{6,7},{7,5},{5,3},{3,1},{1,0},{8,10},{10,12},{12... | collective-permute-start | bytes 589832 | tf_op jit(solution)/shard_map/ppermute | solution.py:191
  158.3 1.6 collective-permute-done.43.rest_43_
  160.0 2.6 %collective-permute-start.46 = (bf16[96,1024]{1,0:T(8,128)(2,1)}, bf16[96,1024]{1,0:T(8,128)(2,1)}, u32[]{:S(2)}, u32[]{:S(2)}) collective-permute-start(bf16[96,1024]{1,0:T(8,128)(2,1)} %collective-permute-done.42.rest_42_), channel_id=1, source_target_pairs={{0,2},{2,4},{4,6},{6,7},{7,5},{5,3},{3,1},{1,0},{8,10},{10,12},{12... | collective-permute-start | bytes 589832 | tf_op jit(solution)/shard_map/ppermute | solution.py:191
  164.4 2.4 %collective-permute-start.48 = (bf16[96,1024]{1,0:T(8,128)(2,1)}, bf16[96,1024]{1,0:T(8,128)(2,1)S(1)}, u32[]{:S(2)}, u32[]{:S(2)}) collective-permute-start(bf16[96,1024]{1,0:T(8,128)(2,1)} %collective-permute-done.44.rest_44_), channel_id=1, source_target_pairs={{0,2},{2,4},{4,6},{6,7},{7,5},{5,3},{3,1},{1,0},{8,10},{10,12},{12... | collective-permute-start | bytes 589832 | tf_op jit(solution)/shard_map/ppermute | solution.py:191
  166.8 1.8 collective-permute-done.47.rest_47_
  168.6 2.4 %collective-permute-start.50 = (bf16[96,1024]{1,0:T(8,128)(2,1)}, bf16[96,1024]{1,0:T(8,128)(2,1)S(1)}, u32[]{:S(2)}, u32[]{:S(2)}) collective-permute-start(bf16[96,1024]{1,0:T(8,128)(2,1)} %collective-permute-done.46.rest_46_), channel_id=1, source_target_pairs={{0,2},{2,4},{4,6},{6,7},{7,5},{5,3},{3,1},{1,0},{8,10},{10,12},{12... | collective-permute-start | bytes 589832 | tf_op jit(solution)/shard_map/ppermute | solution.py:191
  171.4 1.3 collective-permute-done.49.rest_49_
  172.7 2.4 %collective-permute-start.52 = (bf16[96,1024]{1,0:T(8,128)(2,1)S(1)}, bf16[96,1024]{1,0:T(8,128)(2,1)S(1)}, u32[]{:S(2)}, u32[]{:S(2)}) collective-permute-start(bf16[96,1024]{1,0:T(8,128)(2,1)S(1)} %collective-permute-done.48.rest_48_), channel_id=1, source_target_pairs={{0,2},{2,4},{4,6},{6,7},{7,5},{5,3},{3,1},{1,0},{8,10},{10,12},{12... | collective-permute-start | bytes 589832 | tf_op jit(solution)/shard_map/ppermute | solution.py:191
  175.6 1.5 collective-permute-done.51.rest_51_
  177.1 2.2 %collective-permute-start.54 = (bf16[96,1024]{1,0:T(8,128)(2,1)S(1)}, bf16[96,1024]{1,0:T(8,128)(2,1)S(1)}, u32[]{:S(2)}, u32[]{:S(2)}) collective-permute-start(bf16[96,1024]{1,0:T(8,128)(2,1)S(1)} %collective-permute-done.50.rest_50_), channel_id=1, source_target_pairs={{0,2},{2,4},{4,6},{6,7},{7,5},{5,3},{3,1},{1,0},{8,10},{10,12},{12... | collective-permute-start | bytes 589832 | tf_op jit(solution)/shard_map/ppermute | solution.py:191
  181.4 1.8 collective-permute-done.54.rest_54_
  183.1 2.2 %collective-permute-done.55.rest_55_ = bf16[96,1024]{1,0:T(8,128)(2,1)S(1)} collective-permute-done((bf16[96,1024]{1,0:T(8,128)(2,1)S(1)}, bf16[96,1024]{1,0:T(8,128)(2,1)S(1)}, u32[]{:S(2)}, u32[]{:S(2)}) %collective-permute-start.55) | collective-permute-done | bytes 196640 | tf_op jit(solution)/shard_map/ppermute | solution.py:191
  186.1 10.8 %shard_map.104 = bf16[768,2048]{1,0:T(8,128)(2,1)} custom-call(s32[2]{0:T(128)} %pad_add_fusion.hops, bf16[768,2048]{1,0:T(8,128)(2,1)} %x.1, f32[768,1]{1,0:T(8,128)} %copy.11.weight, bf16[2048,1024]{1,0:T(8,128)(2,1)} %bitcast.70, bf16[512,2048]{1,0:T(8,128)(2,1)} %bitcast.73, bf16[96,1024]{1,0:T(8,128)(2,1)} %collective-permute-done.2.rest_0_, ...), custom_call_target="tpu_custom_call" | custom-call | flops 4831838208 | bytes 20971520 | tf_op jit(solution)/shard_map/pallas_call | solution.py:85
  (199 shorter events, 21.2 us)
Async XLA Ops:
  2.9 23.2 %collective-permute-start = (bf16[96,1024]{1,0:T(8,128)(2,1)}, bf16[96,1024]{1,0:T(8,128)(2,1)}, u32[]{:S(2)}, u32[]{:S(2)}) collective-permute-start(bf16[96,1024]{1,0:T(8,128)(2,1)} %get-tuple-element.180), channel_id=1, source_target_pairs={{0,2},{2,4},{4,6},{6,7},{7,5},{5,3},{3,1},{1,0},{8,10},{10,12},{12... | collective-permute-start | bytes 589832 | tf_op jit(solution)/shard_map/ppermute | solution.py:191
  6.0 20.2 %collective-permute-start.1 = (bf16[96,1024]{1,0:T(8,128)(2,1)}, bf16[96,1024]{1,0:T(8,128)(2,1)}, u32[]{:S(2)}, u32[]{:S(2)}) collective-permute-start(bf16[96,1024]{1,0:T(8,128)(2,1)} %get-tuple-element.181), channel_id=1, source_target_pairs={{2,0},{4,2},{6,4},{7,6},{5,7},{3,5},{1,3},{0,1},{10,8},{12,10},{14... | collective-permute-start | bytes 589832 | tf_op jit(solution)/shard_map/ppermute | solution.py:191
  6.0 20.2 %collective-permute-start.2 = (bf16[96,1024]{1,0:T(8,128)(2,1)}, bf16[96,1024]{1,0:T(8,128)(2,1)}, u32[]{:S(2)}, u32[]{:S(2)}) collective-permute-start(bf16[96,1024]{1,0:T(8,128)(2,1)} %get-tuple-element.184), channel_id=1, source_target_pairs={{0,2},{2,4},{4,6},{6,7},{7,5},{5,3},{3,1},{1,0},{8,10},{10,12},{12... | collective-permute-start | bytes 589832 | tf_op jit(solution)/shard_map/ppermute | solution.py:191
  8.0 18.2 %collective-permute-start.3 = (bf16[96,1024]{1,0:T(8,128)(2,1)}, bf16[96,1024]{1,0:T(8,128)(2,1)}, u32[]{:S(2)}, u32[]{:S(2)}) collective-permute-start(bf16[96,1024]{1,0:T(8,128)(2,1)} %get-tuple-element.185), channel_id=1, source_target_pairs={{2,0},{4,2},{6,4},{7,6},{5,7},{3,5},{1,3},{0,1},{10,8},{12,10},{14... | collective-permute-start | bytes 589832 | tf_op jit(solution)/shard_map/ppermute | solution.py:191
  10.6 63.7 %all-to-all-start = ((bf16[16,16,2048]{2,1,0:T(8,128)(2,1)}), bf16[16,16,2048]{2,1,0:T(8,128)(2,1)S(1)}, u32[]{:S(2)}, u32[]{:S(2)}) async-start(bf16[16,16,2048]{2,1,0:T(8,128)(2,1)} %bitcast.29), calls=%async_computation | async-start | bytes 2097152 | tf_op jit(solution)/shard_map/all_to_all | solution.py:148
  27.5 12.2 %collective-permute-start.4 = (bf16[96,1024]{1,0:T(8,128)(2,1)S(1)}, bf16[96,1024]{1,0:T(8,128)(2,1)S(1)}, u32[]{:S(2)}, u32[]{:S(2)}) collective-permute-start(bf16[96,1024]{1,0:T(8,128)(2,1)S(1)} %get-tuple-element.188), channel_id=1, source_target_pairs={{0,2},{2,4},{4,6},{6,7},{7,5},{5,3},{3,1},{1,0},{8,10},{10,12},{12... | collective-permute-start | bytes 589832 | tf_op jit(solution)/shard_map/ppermute | solution.py:191
  29.4 13.3 %collective-permute-start.5 = (bf16[96,1024]{1,0:T(8,128)(2,1)S(1)}, bf16[96,1024]{1,0:T(8,128)(2,1)S(1)}, u32[]{:S(2)}, u32[]{:S(2)}) collective-permute-start(bf16[96,1024]{1,0:T(8,128)(2,1)S(1)} %get-tuple-element.189), channel_id=1, source_target_pairs={{2,0},{4,2},{6,4},{7,6},{5,7},{3,5},{1,3},{0,1},{10,8},{12,10},{14... | collective-permute-start | bytes 589832 | tf_op jit(solution)/shard_map/ppermute | solution.py:191
  30.8 19.2 %collective-permute-start.6 = (bf16[96,1024]{1,0:T(8,128)(2,1)S(1)}, bf16[96,1024]{1,0:T(8,128)(2,1)S(1)}, u32[]{:S(2)}, u32[]{:S(2)}) collective-permute-start(bf16[96,1024]{1,0:T(8,128)(2,1)S(1)} %get-tuple-element.194), channel_id=1, source_target_pairs={{0,2},{2,4},{4,6},{6,7},{7,5},{5,3},{3,1},{1,0},{8,10},{10,12},{12... | collective-permute-start | bytes 589832 | tf_op jit(solution)/shard_map/ppermute | solution.py:191
  32.8 17.2 %collective-permute-start.7 = (bf16[96,1024]{1,0:T(8,128)(2,1)S(1)}, bf16[96,1024]{1,0:T(8,128)(2,1)S(1)}, u32[]{:S(2)}, u32[]{:S(2)}) collective-permute-start(bf16[96,1024]{1,0:T(8,128)(2,1)S(1)} %get-tuple-element.195), channel_id=1, source_target_pairs={{2,0},{4,2},{6,4},{7,6},{5,7},{3,5},{1,3},{0,1},{10,8},{12,10},{14... | collective-permute-start | bytes 589832 | tf_op jit(solution)/shard_map/ppermute | solution.py:191
  43.9 9.8 %collective-permute-start.8 = (bf16[96,1024]{1,0:T(8,128)(2,1)S(1)}, bf16[96,1024]{1,0:T(8,128)(2,1)S(1)}, u32[]{:S(2)}, u32[]{:S(2)}) collective-permute-start(bf16[96,1024]{1,0:T(8,128)(2,1)S(1)} %get-tuple-element.198), channel_id=1, source_target_pairs={{0,2},{2,4},{4,6},{6,7},{7,5},{5,3},{3,1},{1,0},{8,10},{10,12},{12... | collective-permute-start | bytes 589832 | tf_op jit(solution)/shard_map/ppermute | solution.py:191
  50.0 5.7 %collective-permute-start.9 = (bf16[96,1024]{1,0:T(8,128)(2,1)S(1)}, bf16[96,1024]{1,0:T(8,128)(2,1)S(1)}, u32[]{:S(2)}, u32[]{:S(2)}) collective-permute-start(bf16[96,1024]{1,0:T(8,128)(2,1)S(1)} %get-tuple-element.199), channel_id=1, source_target_pairs={{2,0},{4,2},{6,4},{7,6},{5,7},{3,5},{1,3},{0,1},{10,8},{12,10},{14... | collective-permute-start | bytes 589832 | tf_op jit(solution)/shard_map/ppermute | solution.py:191
  51.2 7.7 %collective-permute-start.10 = (bf16[96,1024]{1,0:T(8,128)(2,1)S(1)}, bf16[96,1024]{1,0:T(8,128)(2,1)S(1)}, u32[]{:S(2)}, u32[]{:S(2)}) collective-permute-start(bf16[96,1024]{1,0:T(8,128)(2,1)S(1)} %get-tuple-element.202), channel_id=1, source_target_pairs={{0,2},{2,4},{4,6},{6,7},{7,5},{5,3},{3,1},{1,0},{8,10},{10,12},{12... | collective-permute-start | bytes 589832 | tf_op jit(solution)/shard_map/ppermute | solution.py:191
  53.7 6.9 %collective-permute-start.11 = (bf16[96,1024]{1,0:T(8,128)(2,1)S(1)}, bf16[96,1024]{1,0:T(8,128)(2,1)S(1)}, u32[]{:S(2)}, u32[]{:S(2)}) collective-permute-start(bf16[96,1024]{1,0:T(8,128)(2,1)S(1)} %get-tuple-element.203), channel_id=1, source_target_pairs={{2,0},{4,2},{6,4},{7,6},{5,7},{3,5},{1,3},{0,1},{10,8},{12,10},{14... | collective-permute-start | bytes 589832 | tf_op jit(solution)/shard_map/ppermute | solution.py:191
  56.8 7.0 %collective-permute-start.12 = (bf16[96,1024]{1,0:T(8,128)(2,1)S(1)}, bf16[96,1024]{1,0:T(8,128)(2,1)S(1)}, u32[]{:S(2)}, u32[]{:S(2)}) collective-permute-start(bf16[96,1024]{1,0:T(8,128)(2,1)S(1)} %get-tuple-element.206), channel_id=1, source_target_pairs={{0,2},{2,4},{4,6},{6,7},{7,5},{5,3},{3,1},{1,0},{8,10},{10,12},{12... | collective-permute-start | bytes 589832 | tf_op jit(solution)/shard_map/ppermute | solution.py:191
  57.9 6.9 %collective-permute-start.13 = (bf16[96,1024]{1,0:T(8,128)(2,1)S(1)}, bf16[96,1024]{1,0:T(8,128)(2,1)S(1)}, u32[]{:S(2)}, u32[]{:S(2)}) collective-permute-start(bf16[96,1024]{1,0:T(8,128)(2,1)S(1)} %get-tuple-element.207), channel_id=1, source_target_pairs={{2,0},{4,2},{6,4},{7,6},{5,7},{3,5},{1,3},{0,1},{10,8},{12,10},{14... | collective-permute-start | bytes 589832 | tf_op jit(solution)/shard_map/ppermute | solution.py:191
  61.7 6.9 %collective-permute-start.14 = (bf16[96,1024]{1,0:T(8,128)(2,1)S(1)}, bf16[96,1024]{1,0:T(8,128)(2,1)S(1)}, u32[]{:S(2)}, u32[]{:S(2)}) collective-permute-start(bf16[96,1024]{1,0:T(8,128)(2,1)S(1)} %get-tuple-element.210), channel_id=1, source_target_pairs={{0,2},{2,4},{4,6},{6,7},{7,5},{5,3},{3,1},{1,0},{8,10},{10,12},{12... | collective-permute-start | bytes 589832 | tf_op jit(solution)/shard_map/ppermute | solution.py:191
  62.8 6.8 %collective-permute-start.15 = (bf16[96,1024]{1,0:T(8,128)(2,1)S(1)}, bf16[96,1024]{1,0:T(8,128)(2,1)S(1)}, u32[]{:S(2)}, u32[]{:S(2)}) collective-permute-start(bf16[96,1024]{1,0:T(8,128)(2,1)S(1)} %get-tuple-element.211), channel_id=1, source_target_pairs={{2,0},{4,2},{6,4},{7,6},{5,7},{3,5},{1,3},{0,1},{10,8},{12,10},{14... | collective-permute-start | bytes 589832 | tf_op jit(solution)/shard_map/ppermute | solution.py:191
  66.0 7.5 %collective-permute-start.16 = (bf16[96,1024]{1,0:T(8,128)(2,1)S(1)}, bf16[96,1024]{1,0:T(8,128)(2,1)S(1)}, u32[]{:S(2)}, u32[]{:S(2)}) collective-permute-start(bf16[96,1024]{1,0:T(8,128)(2,1)S(1)} %get-tuple-element.214), channel_id=1, source_target_pairs={{0,2},{2,4},{4,6},{6,7},{7,5},{5,3},{3,1},{1,0},{8,10},{10,12},{12... | collective-permute-start | bytes 589832 | tf_op jit(solution)/shard_map/ppermute | solution.py:191
  66.9 7.4 %collective-permute-start.17 = (bf16[96,1024]{1,0:T(8,128)(2,1)S(1)}, bf16[96,1024]{1,0:T(8,128)(2,1)}, u32[]{:S(2)}, u32[]{:S(2)}) collective-permute-start(bf16[96,1024]{1,0:T(8,128)(2,1)S(1)} %get-tuple-element.215), channel_id=1, source_target_pairs={{2,0},{4,2},{6,4},{7,6},{5,7},{3,5},{1,3},{0,1},{10,8},{12,10},{14... | collective-permute-start | bytes 589832 | tf_op jit(solution)/shard_map/ppermute | solution.py:191
  71.5 12.1 %collective-permute-start.18 = (bf16[96,1024]{1,0:T(8,128)(2,1)}, bf16[96,1024]{1,0:T(8,128)(2,1)}, u32[]{:S(2)}, u32[]{:S(2)}) collective-permute-start(bf16[96,1024]{1,0:T(8,128)(2,1)} %get-tuple-element.218), channel_id=1, source_target_pairs={{0,2},{2,4},{4,6},{6,7},{7,5},{5,3},{3,1},{1,0},{8,10},{10,12},{12... | collective-permute-start | bytes 589832 | tf_op jit(solution)/shard_map/ppermute | solution.py:191
  72.0 11.5 %collective-permute-start.19 = (bf16[96,1024]{1,0:T(8,128)(2,1)}, bf16[96,1024]{1,0:T(8,128)(2,1)}, u32[]{:S(2)}, u32[]{:S(2)}) collective-permute-start(bf16[96,1024]{1,0:T(8,128)(2,1)} %get-tuple-element.219), channel_id=1, source_target_pairs={{2,0},{4,2},{6,4},{7,6},{5,7},{3,5},{1,3},{0,1},{10,8},{12,10},{14... | collective-permute-start | bytes 589832 | tf_op jit(solution)/shard_map/ppermute | solution.py:191
  76.3 15.4 %collective-permute-start.20 = (bf16[96,1024]{1,0:T(8,128)(2,1)}, bf16[96,1024]{1,0:T(8,128)(2,1)}, u32[]{:S(2)}, u32[]{:S(2)}) collective-permute-start(bf16[96,1024]{1,0:T(8,128)(2,1)} %get-tuple-element.224), channel_id=1, source_target_pairs={{0,2},{2,4},{4,6},{6,7},{7,5},{5,3},{3,1},{1,0},{8,10},{10,12},{12... | collective-permute-start | bytes 589832 | tf_op jit(solution)/shard_map/ppermute | solution.py:191
  76.9 14.8 %collective-permute-start.21 = (bf16[96,1024]{1,0:T(8,128)(2,1)}, bf16[96,1024]{1,0:T(8,128)(2,1)}, u32[]{:S(2)}, u32[]{:S(2)}) collective-permute-start(bf16[96,1024]{1,0:T(8,128)(2,1)} %get-tuple-element.225), channel_id=1, source_target_pairs={{2,0},{4,2},{6,4},{7,6},{5,7},{3,5},{1,3},{0,1},{10,8},{12,10},{14... | collective-permute-start | bytes 589832 | tf_op jit(solution)/shard_map/ppermute | solution.py:191
  83.5 79.1 %copy-start.41 = (f32[768,1]{0,1:T(1,128)S(1)}, f32[768,1]{0,1:T(1,128)}, u32[]{:S(2)}) copy-start(f32[768,1]{0,1:T(1,128)} %broadcast_in_dim.25) | copy-start | bytes 9220
  83.5 87.5 %copy-start.43 = (s32[256]{0:T(256)S(1)}, s32[256]{0:T(256)}, u32[]{:S(2)}) copy-start(s32[256]{0:T(256)} %copy-done.42) | copy-start | bytes 3076
  83.5 87.5 %copy-start.45 = (s32[256]{0:T(256)S(1)}, s32[256]{0:T(256)}, u32[]{:S(2)}) copy-start(s32[256]{0:T(256)} %copy-done.44) | copy-start | bytes 3076
  83.5 87.5 %copy-start.47 = (s32[64]{0:T(128)S(1)}, s32[64]{0:T(128)}, u32[]{:S(2)}) copy-start(s32[64]{0:T(128)} %copy-done.46) | copy-start | bytes 772
  83.6 87.5 %copy-start.49 = (s32[64]{0:T(128)S(1)}, s32[64]{0:T(128)}, u32[]{:S(2)}) copy-start(s32[64]{0:T(128)} %copy-done.48) | copy-start | bytes 772
  83.6 87.5 %copy-start.51 = (pred[256]{0:T(512)(128)(4,1)S(1)}, pred[256]{0:T(512)(128)(4,1)}, u32[]{:S(2)}) copy-start(pred[256]{0:T(512)(128)(4,1)} %copy-done.50) | copy-start | bytes 772
  83.6 80.8 %all-to-all-start.1 = ((bf16[16,16,2048]{2,1,0:T(8,128)(2,1)}), bf16[16,16,2048]{2,1,0:T(8,128)(2,1)S(1)}, u32[]{:S(2)}, u32[]{:S(2)}) async-start(bf16[16,16,2048]{2,1,0:T(8,128)(2,1)} %bitcast.81), calls=%async_computation.1 | async-start | bytes 2097152 | tf_op jit(solution)/shard_map/all_to_all | solution.py:178
  89.6 21.6 %collective-permute-start.22 = (bf16[96,1024]{1,0:T(8,128)(2,1)S(1)}, bf16[96,1024]{1,0:T(8,128)(2,1)S(1)}, u32[]{:S(2)}, u32[]{:S(2)}) collective-permute-start(bf16[96,1024]{1,0:T(8,128)(2,1)S(1)} %get-tuple-element.231), channel_id=1, source_target_pairs={{0,2},{2,4},{4,6},{6,7},{7,5},{5,3},{3,1},{1,0},{8,10},{10,12},{12... | collective-permute-start | bytes 589832 | tf_op jit(solution)/shard_map/ppermute | solution.py:191
  91.6 20.2 %collective-permute-start.23 = (bf16[96,1024]{1,0:T(8,128)(2,1)S(1)}, bf16[96,1024]{1,0:T(8,128)(2,1)S(1)}, u32[]{:S(2)}, u32[]{:S(2)}) collective-permute-start(bf16[96,1024]{1,0:T(8,128)(2,1)S(1)} %get-tuple-element.232), channel_id=1, source_target_pairs={{2,0},{4,2},{6,4},{7,6},{5,7},{3,5},{1,3},{0,1},{10,8},{12,10},{14... | collective-permute-start | bytes 589832 | tf_op jit(solution)/shard_map/ppermute | solution.py:191
  92.8 27.7 %collective-permute-start.24 = (bf16[96,1024]{1,0:T(8,128)(2,1)S(1)}, bf16[96,1024]{1,0:T(8,128)(2,1)S(1)}, u32[]{:S(2)}, u32[]{:S(2)}) collective-permute-start(bf16[96,1024]{1,0:T(8,128)(2,1)S(1)} %get-tuple-element.235), channel_id=1, source_target_pairs={{0,2},{2,4},{4,6},{6,7},{7,5},{5,3},{3,1},{1,0},{8,10},{10,12},{12... | collective-permute-start | bytes 589832 | tf_op jit(solution)/shard_map/ppermute | solution.py:191
  94.8 25.7 %collective-permute-start.25 = (bf16[96,1024]{1,0:T(8,128)(2,1)S(1)}, bf16[96,1024]{1,0:T(8,128)(2,1)S(1)}, u32[]{:S(2)}, u32[]{:S(2)}) collective-permute-start(bf16[96,1024]{1,0:T(8,128)(2,1)S(1)} %get-tuple-element.236), channel_id=1, source_target_pairs={{2,0},{4,2},{6,4},{7,6},{5,7},{3,5},{1,3},{0,1},{10,8},{12,10},{14... | collective-permute-start | bytes 589832 | tf_op jit(solution)/shard_map/ppermute | solution.py:191
  111.9 12.7 %collective-permute-start.26 = (bf16[96,1024]{1,0:T(8,128)(2,1)S(1)}, bf16[96,1024]{1,0:T(8,128)(2,1)S(1)}, u32[]{:S(2)}, u32[]{:S(2)}) collective-permute-start(bf16[96,1024]{1,0:T(8,128)(2,1)S(1)} %get-tuple-element.239), channel_id=1, source_target_pairs={{0,2},{2,4},{4,6},{6,7},{7,5},{5,3},{3,1},{1,0},{8,10},{10,12},{12... | collective-permute-start | bytes 589832 | tf_op jit(solution)/shard_map/ppermute | solution.py:191
  120.4 5.7 %collective-permute-start.27 = (bf16[96,1024]{1,0:T(8,128)(2,1)S(1)}, bf16[96,1024]{1,0:T(8,128)(2,1)S(1)}, u32[]{:S(2)}, u32[]{:S(2)}) collective-permute-start(bf16[96,1024]{1,0:T(8,128)(2,1)S(1)} %get-tuple-element.240), channel_id=1, source_target_pairs={{2,0},{4,2},{6,4},{7,6},{5,7},{3,5},{1,3},{0,1},{10,8},{12,10},{14... | collective-permute-start | bytes 589832 | tf_op jit(solution)/shard_map/ppermute | solution.py:191
  120.5 8.4 %collective-permute-start.28 = (bf16[96,1024]{1,0:T(8,128)(2,1)S(1)}, bf16[96,1024]{1,0:T(8,128)(2,1)S(1)}, u32[]{:S(2)}, u32[]{:S(2)}) collective-permute-start(bf16[96,1024]{1,0:T(8,128)(2,1)S(1)} %get-tuple-element.243), channel_id=1, source_target_pairs={{0,2},{2,4},{4,6},{6,7},{7,5},{5,3},{3,1},{1,0},{8,10},{10,12},{12... | collective-permute-start | bytes 589832 | tf_op jit(solution)/shard_map/ppermute | solution.py:191
  124.6 5.7 %collective-permute-start.29 = (bf16[96,1024]{1,0:T(8,128)(2,1)S(1)}, bf16[96,1024]{1,0:T(8,128)(2,1)S(1)}, u32[]{:S(2)}, u32[]{:S(2)}) collective-permute-start(bf16[96,1024]{1,0:T(8,128)(2,1)S(1)} %get-tuple-element.244), channel_id=1, source_target_pairs={{2,0},{4,2},{6,4},{7,6},{5,7},{3,5},{1,3},{0,1},{10,8},{12,10},{14... | collective-permute-start | bytes 589832 | tf_op jit(solution)/shard_map/ppermute | solution.py:191
  126.2 7.0 %collective-permute-start.30 = (bf16[96,1024]{1,0:T(8,128)(2,1)S(1)}, bf16[96,1024]{1,0:T(8,128)(2,1)S(1)}, u32[]{:S(2)}, u32[]{:S(2)}) collective-permute-start(bf16[96,1024]{1,0:T(8,128)(2,1)S(1)} %get-tuple-element.247), channel_id=1, source_target_pairs={{0,2},{2,4},{4,6},{6,7},{7,5},{5,3},{3,1},{1,0},{8,10},{10,12},{12... | collective-permute-start | bytes 589832 | tf_op jit(solution)/shard_map/ppermute | solution.py:191
  128.9 5.8 %collective-permute-start.31 = (bf16[96,1024]{1,0:T(8,128)(2,1)S(1)}, bf16[96,1024]{1,0:T(8,128)(2,1)S(1)}, u32[]{:S(2)}, u32[]{:S(2)}) collective-permute-start(bf16[96,1024]{1,0:T(8,128)(2,1)S(1)} %get-tuple-element.248), channel_id=1, source_target_pairs={{2,0},{4,2},{6,4},{7,6},{5,7},{3,5},{1,3},{0,1},{10,8},{12,10},{14... | collective-permute-start | bytes 589832 | tf_op jit(solution)/shard_map/ppermute | solution.py:191
  130.3 6.8 %collective-permute-start.32 = (bf16[96,1024]{1,0:T(8,128)(2,1)S(1)}, bf16[96,1024]{1,0:T(8,128)(2,1)S(1)}, u32[]{:S(2)}, u32[]{:S(2)}) collective-permute-start(bf16[96,1024]{1,0:T(8,128)(2,1)S(1)} %collective-permute-done.28.rest_28_), channel_id=1, source_target_pairs={{0,2},{2,4},{4,6},{6,7},{7,5},{5,3},{3,1},{1,0},{8,10},{10,12},{12... | collective-permute-start | bytes 589832 | tf_op jit(solution)/shard_map/ppermute | solution.py:191
  133.0 5.9 %collective-permute-start.33 = (bf16[96,1024]{1,0:T(8,128)(2,1)S(1)}, bf16[96,1024]{1,0:T(8,128)(2,1)S(1)}, u32[]{:S(2)}, u32[]{:S(2)}) collective-permute-start(bf16[96,1024]{1,0:T(8,128)(2,1)S(1)} %collective-permute-done.29.rest_29_), channel_id=1, source_target_pairs={{2,0},{4,2},{6,4},{7,6},{5,7},{3,5},{1,3},{0,1},{10,8},{12,10},{14... | collective-permute-start | bytes 589832 | tf_op jit(solution)/shard_map/ppermute | solution.py:191
  134.7 6.7 %collective-permute-start.34 = (bf16[96,1024]{1,0:T(8,128)(2,1)S(1)}, bf16[96,1024]{1,0:T(8,128)(2,1)S(1)}, u32[]{:S(2)}, u32[]{:S(2)}) collective-permute-start(bf16[96,1024]{1,0:T(8,128)(2,1)S(1)} %collective-permute-done.30.rest_30_), channel_id=1, source_target_pairs={{0,2},{2,4},{4,6},{6,7},{7,5},{5,3},{3,1},{1,0},{8,10},{10,12},{12... | collective-permute-start | bytes 589832 | tf_op jit(solution)/shard_map/ppermute | solution.py:191
  137.2 5.9 %collective-permute-start.35 = (bf16[96,1024]{1,0:T(8,128)(2,1)S(1)}, bf16[96,1024]{1,0:T(8,128)(2,1)S(1)}, u32[]{:S(2)}, u32[]{:S(2)}) collective-permute-start(bf16[96,1024]{1,0:T(8,128)(2,1)S(1)} %collective-permute-done.31.rest_31_), channel_id=1, source_target_pairs={{2,0},{4,2},{6,4},{7,6},{5,7},{3,5},{1,3},{0,1},{10,8},{12,10},{14... | collective-permute-start | bytes 589832 | tf_op jit(solution)/shard_map/ppermute | solution.py:191
  138.9 6.7 %collective-permute-start.36 = (bf16[96,1024]{1,0:T(8,128)(2,1)S(1)}, bf16[96,1024]{1,0:T(8,128)(2,1)S(1)}, u32[]{:S(2)}, u32[]{:S(2)}) collective-permute-start(bf16[96,1024]{1,0:T(8,128)(2,1)S(1)} %collective-permute-done.32.rest_32_), channel_id=1, source_target_pairs={{0,2},{2,4},{4,6},{6,7},{7,5},{5,3},{3,1},{1,0},{8,10},{10,12},{12... | collective-permute-start | bytes 589832 | tf_op jit(solution)/shard_map/ppermute | solution.py:191
  141.4 5.9 %collective-permute-start.37 = (bf16[96,1024]{1,0:T(8,128)(2,1)S(1)}, bf16[96,1024]{1,0:T(8,128)(2,1)S(1)}, u32[]{:S(2)}, u32[]{:S(2)}) collective-permute-start(bf16[96,1024]{1,0:T(8,128)(2,1)S(1)} %collective-permute-done.33.rest_33_), channel_id=1, source_target_pairs={{2,0},{4,2},{6,4},{7,6},{5,7},{3,5},{1,3},{0,1},{10,8},{12,10},{14... | collective-permute-start | bytes 589832 | tf_op jit(solution)/shard_map/ppermute | solution.py:191
  143.1 6.7 %collective-permute-start.38 = (bf16[96,1024]{1,0:T(8,128)(2,1)S(1)}, bf16[96,1024]{1,0:T(8,128)(2,1)S(1)}, u32[]{:S(2)}, u32[]{:S(2)}) collective-permute-start(bf16[96,1024]{1,0:T(8,128)(2,1)S(1)} %collective-permute-done.34.rest_34_), channel_id=1, source_target_pairs={{0,2},{2,4},{4,6},{6,7},{7,5},{5,3},{3,1},{1,0},{8,10},{10,12},{12... | collective-permute-start | bytes 589832 | tf_op jit(solution)/shard_map/ppermute | solution.py:191
  145.6 5.9 %collective-permute-start.39 = (bf16[96,1024]{1,0:T(8,128)(2,1)S(1)}, bf16[96,1024]{1,0:T(8,128)(2,1)S(1)}, u32[]{:S(2)}, u32[]{:S(2)}) collective-permute-start(bf16[96,1024]{1,0:T(8,128)(2,1)S(1)} %collective-permute-done.35.rest_35_), channel_id=1, source_target_pairs={{2,0},{4,2},{6,4},{7,6},{5,7},{3,5},{1,3},{0,1},{10,8},{12,10},{14... | collective-permute-start | bytes 589832 | tf_op jit(solution)/shard_map/ppermute | solution.py:191
  147.3 6.7 %collective-permute-start.40 = (bf16[96,1024]{1,0:T(8,128)(2,1)S(1)}, bf16[96,1024]{1,0:T(8,128)(2,1)}, u32[]{:S(2)}, u32[]{:S(2)}) collective-permute-start(bf16[96,1024]{1,0:T(8,128)(2,1)S(1)} %collective-permute-done.36.rest_36_), channel_id=1, source_target_pairs={{0,2},{2,4},{4,6},{6,7},{7,5},{5,3},{3,1},{1,0},{8,10},{10,12},{12... | collective-permute-start | bytes 589832 | tf_op jit(solution)/shard_map/ppermute | solution.py:191
  149.8 6.0 %collective-permute-start.41 = (bf16[96,1024]{1,0:T(8,128)(2,1)S(1)}, bf16[96,1024]{1,0:T(8,128)(2,1)}, u32[]{:S(2)}, u32[]{:S(2)}) collective-permute-start(bf16[96,1024]{1,0:T(8,128)(2,1)S(1)} %collective-permute-done.37.rest_37_), channel_id=1, source_target_pairs={{2,0},{4,2},{6,4},{7,6},{5,7},{3,5},{1,3},{0,1},{10,8},{12,10},{14... | collective-permute-start | bytes 589832 | tf_op jit(solution)/shard_map/ppermute | solution.py:191
  151.5 6.8 %collective-permute-start.42 = (bf16[96,1024]{1,0:T(8,128)(2,1)S(1)}, bf16[96,1024]{1,0:T(8,128)(2,1)}, u32[]{:S(2)}, u32[]{:S(2)}) collective-permute-start(bf16[96,1024]{1,0:T(8,128)(2,1)S(1)} %collective-permute-done.38.rest_38_), channel_id=1, source_target_pairs={{0,2},{2,4},{4,6},{6,7},{7,5},{5,3},{3,1},{1,0},{8,10},{10,12},{12... | collective-permute-start | bytes 589832 | tf_op jit(solution)/shard_map/ppermute | solution.py:191
  154.0 5.9 %collective-permute-start.43 = (bf16[96,1024]{1,0:T(8,128)(2,1)S(1)}, bf16[96,1024]{1,0:T(8,128)(2,1)}, u32[]{:S(2)}, u32[]{:S(2)}) collective-permute-start(bf16[96,1024]{1,0:T(8,128)(2,1)S(1)} %collective-permute-done.39.rest_39_), channel_id=1, source_target_pairs={{2,0},{4,2},{6,4},{7,6},{5,7},{3,5},{1,3},{0,1},{10,8},{12,10},{14... | collective-permute-start | bytes 589832 | tf_op jit(solution)/shard_map/ppermute | solution.py:191
  155.8 7.7 %collective-permute-start.44 = (bf16[96,1024]{1,0:T(8,128)(2,1)}, bf16[96,1024]{1,0:T(8,128)(2,1)}, u32[]{:S(2)}, u32[]{:S(2)}) collective-permute-start(bf16[96,1024]{1,0:T(8,128)(2,1)} %collective-permute-done.40.rest_40_), channel_id=1, source_target_pairs={{0,2},{2,4},{4,6},{6,7},{7,5},{5,3},{3,1},{1,0},{8,10},{10,12},{12... | collective-permute-start | bytes 589832 | tf_op jit(solution)/shard_map/ppermute | solution.py:191
  158.3 6.0 %collective-permute-start.45 = (bf16[96,1024]{1,0:T(8,128)(2,1)}, bf16[96,1024]{1,0:T(8,128)(2,1)}, u32[]{:S(2)}, u32[]{:S(2)}) collective-permute-start(bf16[96,1024]{1,0:T(8,128)(2,1)} %collective-permute-done.41.rest_41_), channel_id=1, source_target_pairs={{2,0},{4,2},{6,4},{7,6},{5,7},{3,5},{1,3},{0,1},{10,8},{12,10},{14... | collective-permute-start | bytes 589832 | tf_op jit(solution)/shard_map/ppermute | solution.py:191
  160.0 6.8 %collective-permute-start.46 = (bf16[96,1024]{1,0:T(8,128)(2,1)}, bf16[96,1024]{1,0:T(8,128)(2,1)}, u32[]{:S(2)}, u32[]{:S(2)}) collective-permute-start(bf16[96,1024]{1,0:T(8,128)(2,1)} %collective-permute-done.42.rest_42_), channel_id=1, source_target_pairs={{0,2},{2,4},{4,6},{6,7},{7,5},{5,3},{3,1},{1,0},{8,10},{10,12},{12... | collective-permute-start | bytes 589832 | tf_op jit(solution)/shard_map/ppermute | solution.py:191
  162.6 6.0 %collective-permute-start.47 = (bf16[96,1024]{1,0:T(8,128)(2,1)}, bf16[96,1024]{1,0:T(8,128)(2,1)}, u32[]{:S(2)}, u32[]{:S(2)}) collective-permute-start(bf16[96,1024]{1,0:T(8,128)(2,1)} %collective-permute-done.43.rest_43_), channel_id=1, source_target_pairs={{2,0},{4,2},{6,4},{7,6},{5,7},{3,5},{1,3},{0,1},{10,8},{12,10},{14... | collective-permute-start | bytes 589832 | tf_op jit(solution)/shard_map/ppermute | solution.py:191
  164.4 7.0 %collective-permute-start.48 = (bf16[96,1024]{1,0:T(8,128)(2,1)}, bf16[96,1024]{1,0:T(8,128)(2,1)S(1)}, u32[]{:S(2)}, u32[]{:S(2)}) collective-permute-start(bf16[96,1024]{1,0:T(8,128)(2,1)} %collective-permute-done.44.rest_44_), channel_id=1, source_target_pairs={{0,2},{2,4},{4,6},{6,7},{7,5},{5,3},{3,1},{1,0},{8,10},{10,12},{12... | collective-permute-start | bytes 589832 | tf_op jit(solution)/shard_map/ppermute | solution.py:191
  166.8 5.9 %collective-permute-start.49 = (bf16[96,1024]{1,0:T(8,128)(2,1)}, bf16[96,1024]{1,0:T(8,128)(2,1)S(1)}, u32[]{:S(2)}, u32[]{:S(2)}) collective-permute-start(bf16[96,1024]{1,0:T(8,128)(2,1)} %collective-permute-done.45.rest_45_), channel_id=1, source_target_pairs={{2,0},{4,2},{6,4},{7,6},{5,7},{3,5},{1,3},{0,1},{10,8},{12,10},{14... | collective-permute-start | bytes 589832 | tf_op jit(solution)/shard_map/ppermute | solution.py:191
  168.6 7.1 %collective-permute-start.50 = (bf16[96,1024]{1,0:T(8,128)(2,1)}, bf16[96,1024]{1,0:T(8,128)(2,1)S(1)}, u32[]{:S(2)}, u32[]{:S(2)}) collective-permute-start(bf16[96,1024]{1,0:T(8,128)(2,1)} %collective-permute-done.46.rest_46_), channel_id=1, source_target_pairs={{0,2},{2,4},{4,6},{6,7},{7,5},{5,3},{3,1},{1,0},{8,10},{10,12},{12... | collective-permute-start | bytes 589832 | tf_op jit(solution)/shard_map/ppermute | solution.py:191
  171.0 6.2 %collective-permute-start.51 = (bf16[96,1024]{1,0:T(8,128)(2,1)}, bf16[96,1024]{1,0:T(8,128)(2,1)S(1)}, u32[]{:S(2)}, u32[]{:S(2)}) collective-permute-start(bf16[96,1024]{1,0:T(8,128)(2,1)} %collective-permute-done.47.rest_47_), channel_id=1, source_target_pairs={{2,0},{4,2},{6,4},{7,6},{5,7},{3,5},{1,3},{0,1},{10,8},{12,10},{14... | collective-permute-start | bytes 589832 | tf_op jit(solution)/shard_map/ppermute | solution.py:191
  172.7 7.7 %collective-permute-start.52 = (bf16[96,1024]{1,0:T(8,128)(2,1)S(1)}, bf16[96,1024]{1,0:T(8,128)(2,1)S(1)}, u32[]{:S(2)}, u32[]{:S(2)}) collective-permute-start(bf16[96,1024]{1,0:T(8,128)(2,1)S(1)} %collective-permute-done.48.rest_48_), channel_id=1, source_target_pairs={{0,2},{2,4},{4,6},{6,7},{7,5},{5,3},{3,1},{1,0},{8,10},{10,12},{12... | collective-permute-start | bytes 589832 | tf_op jit(solution)/shard_map/ppermute | solution.py:191
  175.1 6.3 %collective-permute-start.53 = (bf16[96,1024]{1,0:T(8,128)(2,1)S(1)}, bf16[96,1024]{1,0:T(8,128)(2,1)S(1)}, u32[]{:S(2)}, u32[]{:S(2)}) collective-permute-start(bf16[96,1024]{1,0:T(8,128)(2,1)S(1)} %collective-permute-done.49.rest_49_), channel_id=1, source_target_pairs={{2,0},{4,2},{6,4},{7,6},{5,7},{3,5},{1,3},{0,1},{10,8},{12,10},{14... | collective-permute-start | bytes 589832 | tf_op jit(solution)/shard_map/ppermute | solution.py:191
  177.1 6.0 %collective-permute-start.54 = (bf16[96,1024]{1,0:T(8,128)(2,1)S(1)}, bf16[96,1024]{1,0:T(8,128)(2,1)S(1)}, u32[]{:S(2)}, u32[]{:S(2)}) collective-permute-start(bf16[96,1024]{1,0:T(8,128)(2,1)S(1)} %collective-permute-done.50.rest_50_), channel_id=1, source_target_pairs={{0,2},{2,4},{4,6},{6,7},{7,5},{5,3},{3,1},{1,0},{8,10},{10,12},{12... | collective-permute-start | bytes 589832 | tf_op jit(solution)/shard_map/ppermute | solution.py:191
  179.3 6.0 %collective-permute-start.55 = (bf16[96,1024]{1,0:T(8,128)(2,1)S(1)}, bf16[96,1024]{1,0:T(8,128)(2,1)S(1)}, u32[]{:S(2)}, u32[]{:S(2)}) collective-permute-start(bf16[96,1024]{1,0:T(8,128)(2,1)S(1)} %collective-permute-done.51.rest_51_), channel_id=1, source_target_pairs={{2,0},{4,2},{6,4},{7,6},{5,7},{3,5},{1,3},{0,1},{10,8},{12,10},{14... | collective-permute-start | bytes 589832 | tf_op jit(solution)/shard_map/ppermute | solution.py:191
  (49 other events, 885.2 us)

commit v3 on v2

--- a/solution.py
+++ b/solution.py
@@ -7,7 +7,7 @@
 from jax.experimental.pallas import tpu as pltpu
 from jax.sharding import PartitionSpec as P
 
-CHUNKS = 16
+ROWS = 96
 BLOCKS = 2
 
 
@@ -36,17 +36,21 @@
     return (jax.nn.silu(pre[:, :hidden_units]) * pre[:, hidden_units:]).astype(jnp.bfloat16)
 
 
-def hot_kernel(n, chunks, lag, hops, x, weight, gate_up, down, *rest):
+def hot_kernel(n, lag, hops, x, weight, gate_up, down, *rest):
     came = rest[:-5]
-    out, gate_all, down_all, gate_sem, down_sem = rest[-5:]
+    out, gate_all, down_all, gate_sems, down_sem = rest[-5:]
     middle, half = gate_all.shape[0] // 2, down_all.shape[1] // 2
-    rows = (middle + down_all.shape[0]) // chunks
-
-    @pl.when(pl.program_id(0) == 0)
+    rows = came[0].shape[0]
+    starts = starts_of(middle + down_all.shape[0], rows)
+    first = pl.program_id(0) == 0
+
+    @pl.when(first)
     def _():
         @pl.when(hops[0] == 0)
         def _():
-            pltpu.make_async_copy(gate_up, gate_all, gate_sem).start()
+            for way in range(2):
+                part = pl.ds(way * middle, middle)
+                pltpu.make_async_copy(gate_up.at[part, :], gate_all.at[part, :], gate_sems.at[way]).start()
             pltpu.make_async_copy(down, down_all, down_sem).start()
 
         for way in range(2):
@@ -54,23 +58,30 @@
 
                 @pl.when(hops[way] == h)
                 def _(way=way, h=h):
-                    for c in range(chunks):
+                    for c, at in enumerate(starts):
                         source = came[2 * (c + lag * (h - 1)) + way]
-                        at = c * rows
-                        gate = min(max(middle - at, 0), rows)
-                        if gate:
-                            target = gate_all.at[pl.ds(way * middle + at, gate), :]
-                            pltpu.make_async_copy(source.at[pl.ds(0, gate), :], target, gate_sem).start()
+                        low = c * rows - at
+                        gate = min(max(middle - at, low), rows)
+                        if low < gate:
+                            target = gate_all.at[pl.ds(way * middle + at + low, gate - low), :]
+                            part = source.at[pl.ds(low, gate - low), :]
+                            pltpu.make_async_copy(part, target, gate_sems.at[way]).start()
                         if gate < rows:
                             target = down_all.at[pl.ds(at + gate - middle, rows - gate), pl.ds(way * half, half)]
                             pltpu.make_async_copy(source.at[pl.ds(gate, rows - gate), :], target, down_sem).start()
 
-        pltpu.make_async_copy(gate_all, gate_all, gate_sem).wait()
-
-    pre = jnp.dot(x[...], gate_all[...], preferred_element_type=jnp.float32)
+    pre = 0.0
+    for way in range(2):
+        part = pl.ds(way * middle, middle)
+
+        @pl.when(first)
+        def _(way=way, part=part):
+            pltpu.make_async_copy(gate_all.at[part, :], gate_all.at[part, :], gate_sems.at[way]).wait()
+
+        pre += jnp.dot(x[:, part], gate_all[part, :], preferred_element_type=jnp.float32)
     hidden = swiglu(pre, down_all.shape[0])
 
-    @pl.when(pl.program_id(0) == 0)
+    @pl.when(first)
     def _():
         pltpu.make_async_copy(down_all, down_all, down_sem).wait()
 
@@ -83,7 +94,7 @@
     block = tokens // BLOCKS
     whole = pl.BlockSpec(memory_space=pl.ANY)
     return pl.pallas_call(
-        functools.partial(hot_kernel, n, CHUNKS, lag),
+        functools.partial(hot_kernel, n, lag),
         grid=(BLOCKS,),
         out_shape=jax.ShapeDtypeStruct((tokens, width), jnp.bfloat16),
         in_specs=[
@@ -98,7 +109,7 @@
         scratch_shapes=[
             pltpu.VMEM(gate_up.shape, gate_up.dtype),
             pltpu.VMEM(down.shape, down.dtype),
-            pltpu.SemaphoreType.DMA,
+            pltpu.SemaphoreType.DMA((2,)),
             pltpu.SemaphoreType.DMA,
         ],
         compiler_params=pltpu.CompilerParams(vmem_limit_bytes=60 * 2**20),
@@ -106,6 +117,10 @@
             flops=2 * tokens * (gate_up.size + down.size), bytes_accessed=20 * 2**20, transcendentals=0
         ),
     )(hops, x, weight, gate_up, down, *came)
+
+
+def starts_of(total, rows):
+    return [min(at, total - rows) for at in range(0, total, rows)]
 
 
 def cut(parts, start, size):
@@ -126,7 +141,6 @@
     gate_up, down = w_gate_up[0], w_down[0]
     hidden_units, width = down.shape
     n = len(order)
-    lag = 2 if n < CHUNKS else 1
     n_owners = lax.axis_size("ep") * n
     per_device, fan_out = cold_experts.shape
     capacity = max(2, 2 * per_device * fan_out // n_owners)
@@ -150,8 +164,10 @@
     root = hot_root[lax.axis_index("ep")]
     half, middle = width // 2, gate_up.shape[0] // 2
     lanes = ([gate_up[:middle], down[:, :half]], [gate_up[middle:], down[:, half:]])
-    rows = (middle + hidden_units) // CHUNKS
-    own = [[cut(lane, c * rows, rows) for c in range(CHUNKS)] for lane in lanes]
+    starts = starts_of(middle + hidden_units, ROWS)
+    chunks = len(starts)
+    lag = 2 if n < chunks else 1
+    own = [[cut(lane, at, ROWS) for at in starts] for lane in lanes]
     place = jnp.array([order.index(s) for s in range(n)], jnp.int32)
     me = lax.axis_index("shadow")
     ahead = (place[me] - place[root]) % n
@@ -161,22 +177,22 @@
         [(order[(i + 1) % n], order[i]) for i in range(n)],
     )
     weight = res_weight[:, None]
-    steps = CHUNKS + (n - 2) * lag
+    steps = chunks + (n - 2) * lag
     came, last = [], None
     for t in range(steps):
-        mine = tuple(own[i][t] for i in range(2)) if t < CHUNKS else None
+        mine = tuple(own[i][t] for i in range(2)) if t < chunks else None
         if t >= lag:
             got = came[t - lag]
             if t == lag + 1:
                 got, hops, weight = join(got, hops, weight)
-            elif t == steps * 3 // 8:
+            elif t == steps * 2 // 7:
                 got, cold = join(got, cold)
                 pre = jnp.dot(cold, gate_up, preferred_element_type=jnp.float32)
                 cold = jnp.dot(swiglu(pre, hidden_units), down, preferred_element_type=jnp.float32).astype(jnp.bfloat16)
-            elif t == steps * 3 // 8 + 1:
+            elif t == steps * 2 // 7 + 1:
                 got, cold = join(got, cold)
                 cold = lax.all_to_all(cold, ("ep", "shadow"), 0, 0, tiled=True)
-            elif t == steps * 7 // 8:
+            elif t == steps - 2:
                 got, cold = join(got, cold)
                 scale = sum(jnp.where(chosen[k], cold_weights[:, k : k + 1], 0.0) for k in range(fan_out))
                 high = lax.reduce_precision(scale, 8, 7)
@@ -186,7 +202,7 @@
                     + jnp.dot(low, cold, preferred_element_type=jnp.float32)
                 ).astype(jnp.bfloat16)
             got, _ = join(got, last)
-            mine = tuple(jnp.where(me == root, m, g) for m, g in zip(mine, got)) if t < CHUNKS else got
+            mine = tuple(jnp.where(me == root, m, g) for m, g in zip(mine, got)) if t < chunks else got
         mine = last = join(*mine)
         came.append(tuple(lax.ppermute(mine[i], "shadow", ways[i]) for i in range(2)))
     came, cold = join(came, cold)

time: 198 us -> 196 us (0.990)
  starting transfers between devices: 88.5 us -> 90.6 us
    ppermute x56, starting transfers between devices: 77.1 us -> 79.5 us  [body(): lax.ppermute(mine[i], 'shadow', ways[i])]
  transfers between devices with their start and end apart: 58 -> 58, of which waited for: 27 -> 24; matrix products, arithmetic and copies ran while one was open for 15% -> 14% of each run, Pallas kernels for 0% -> 0%
where the time goes in v3:
time: 196 us
  starting transfers between devices  90.6 us (46%)
  waiting for transfers between devices  58.3 us (30%)
  other arithmetic  13.5 us (7%)
  Pallas kernels  11.1 us (6%)
  local copies, waits for them, and re-layouts  8.94 us (5%)
  matrix products  8.28 us (4%)
  between operations  5.15 us (3%)
    ppermute x56, starting transfers between devices, body(): lax.ppermute(mine[i], 'shadow', ways[i])  79.5 us
    ppermute x56, waiting for transfers between devices, body(): lax.ppermute(mine[i], 'shadow', ways[i])  58.3 us
    select_n x14, other arithmetic, body(): jnp.where(me == root, m, g)  12.9 us
    pallas_call x1, Pallas kernels, hot_expert(): pl.pallas_call(functools.partial(hot_kernel, n, lag), grid=(BLOCKS,), out...  11.1 us
    all_to_all x1, starting transfers between devices, body(): cold = lax.all_to_all(outgoing, ('ep', 'shadow'), 0, 0, tiled=True)  6.38 us
    all_to_all x1, starting transfers between devices, body(): cold = lax.all_to_all(cold, ('ep', 'shadow'), 0, 0, tiled=True)  4.67 us
    slice x3, local copies, waits for them, and re-layouts, cut(): out.append(part[low:high])  4.55 us
  transfers between devices with their start and end apart: 58, of which 24 were waited for; matrix products, arithmetic and copies ran while one was open for 14% of the time, Pallas kernels for 0%

profile of v3, /device:TPU:0, one launch (start us, length us, event | category | flops | bytes accessed | tf_op | source)
XLA Modules:
  0.0 195.8 jit_solution(4780460553999159859)
XLA Ops:
  0.7 2.3 %slice_bitcast_fusion = (bf16[96,1024]{1,0:T(8,128)(2,1)}, bf16[96,1024]{1,0:T(8,128)(2,1)}, bf16[96,1024]{1,0:T(8,128)(2,1)}, bf16[96,1024]{1,0:T(8,128)(2,1)}) fusion(bf16[1,2048,1024]{2,1,0:T(8,128)(2,1)} %param.15), kind=kLoop, calls=%fused_computation.36 | loop fusion | bytes 1572864 | tf_op jit(solution)/shard_map/slice | solution.py:131
  2.9 3.0 %collective-permute-start = (bf16[96,1024]{1,0:T(8,128)(2,1)}, bf16[96,1024]{1,0:T(8,128)(2,1)}, u32[]{:S(2)}, u32[]{:S(2)}) collective-permute-start(bf16[96,1024]{1,0:T(8,128)(2,1)} %get-tuple-element.180), channel_id=1, source_target_pairs={{0,2},{2,4},{4,6},{6,7},{7,5},{5,3},{3,1},{1,0},{8,10},{10,12},{12... | collective-permute-start | bytes 589832 | tf_op jit(solution)/shard_map/ppermute | solution.py:207
  6.0 2.0 %collective-permute-start.2 = (bf16[96,1024]{1,0:T(8,128)(2,1)}, bf16[96,1024]{1,0:T(8,128)(2,1)}, u32[]{:S(2)}, u32[]{:S(2)}) collective-permute-start(bf16[96,1024]{1,0:T(8,128)(2,1)} %get-tuple-element.184), channel_id=1, source_target_pairs={{0,2},{2,4},{4,6},{6,7},{7,5},{5,3},{3,1},{1,0},{8,10},{10,12},{12... | collective-permute-start | bytes 589832 | tf_op jit(solution)/shard_map/ppermute | solution.py:207
  9.1 1.5 convolution_convert_fusion.1
  10.6 6.4 %all-to-all-start = ((bf16[16,16,2048]{2,1,0:T(8,128)(2,1)}), bf16[16,16,2048]{2,1,0:T(8,128)(2,1)S(1)}, u32[]{:S(2)}, u32[]{:S(2)}) async-start(bf16[16,16,2048]{2,1,0:T(8,128)(2,1)} %bitcast.25), calls=%async_computation | async-start | bytes 2097152 | tf_op jit(solution)/shard_map/all_to_all | solution.py:162
  23.1 1.6 slice_bitcast_fusion.4
  25.4 1.3 bitcast_select_fusion.14
  26.7 2.0 %collective-permute-start.4 = (bf16[96,1024]{1,0:T(8,128)(2,1)S(1)}, bf16[96,1024]{1,0:T(8,128)(2,1)S(1)}, u32[]{:S(2)}, u32[]{:S(2)}) collective-permute-start(bf16[96,1024]{1,0:T(8,128)(2,1)S(1)} %get-tuple-element.188), channel_id=1, source_target_pairs={{0,2},{2,4},{4,6},{6,7},{7,5},{5,3},{3,1},{1,0},{8,10},{10,12},{12... | collective-permute-start | bytes 589832 | tf_op jit(solution)/shard_map/ppermute | solution.py:207
  28.8 1.3 bitcast_select_fusion.12
  30.1 2.0 %collective-permute-start.6 = (bf16[96,1024]{1,0:T(8,128)(2,1)S(1)}, bf16[96,1024]{1,0:T(8,128)(2,1)S(1)}, u32[]{:S(2)}, u32[]{:S(2)}) collective-permute-start(bf16[96,1024]{1,0:T(8,128)(2,1)S(1)} %get-tuple-element.194), channel_id=1, source_target_pairs={{0,2},{2,4},{4,6},{6,7},{7,5},{5,3},{3,1},{1,0},{8,10},{10,12},{12... | collective-permute-start | bytes 589832 | tf_op jit(solution)/shard_map/ppermute | solution.py:207
  32.1 7.5 %collective-permute-done.4.rest_4_ = bf16[96,1024]{1,0:T(8,128)(2,1)S(1)} collective-permute-done((bf16[96,1024]{1,0:T(8,128)(2,1)S(1)}, bf16[96,1024]{1,0:T(8,128)(2,1)S(1)}, u32[]{:S(2)}, u32[]{:S(2)}) %collective-permute-start.4) | collective-permute-done | bytes 196640 | tf_op jit(solution)/shard_map/ppermute | solution.py:207
  39.6 2.4 %collective-permute-done.5.rest_5_ = bf16[96,1024]{1,0:T(8,128)(2,1)S(1)} collective-permute-done((bf16[96,1024]{1,0:T(8,128)(2,1)S(1)}, bf16[96,1024]{1,0:T(8,128)(2,1)S(1)}, u32[]{:S(2)}, u32[]{:S(2)}) %collective-permute-start.5) | collective-permute-done | bytes 196640 | tf_op jit(solution)/shard_map/ppermute | solution.py:207
  42.0 1.2 bitcast_select_fusion.10
  43.2 6.8 %collective-permute-start.8 = (bf16[96,1024]{1,0:T(8,128)(2,1)S(1)}, bf16[96,1024]{1,0:T(8,128)(2,1)S(1)}, u32[]{:S(2)}, u32[]{:S(2)}) collective-permute-start(bf16[96,1024]{1,0:T(8,128)(2,1)S(1)} %get-tuple-element.198), channel_id=1, source_target_pairs={{0,2},{2,4},{4,6},{6,7},{7,5},{5,3},{3,1},{1,0},{8,10},{10,12},{12... | collective-permute-start | bytes 589832 | tf_op jit(solution)/shard_map/ppermute | solution.py:207
  50.0 1.2 bitcast_select_fusion.8
  51.2 2.5 %collective-permute-start.10 = (bf16[96,1024]{1,0:T(8,128)(2,1)S(1)}, bf16[96,1024]{1,0:T(8,128)(2,1)S(1)}, u32[]{:S(2)}, u32[]{:S(2)}) collective-permute-start(bf16[96,1024]{1,0:T(8,128)(2,1)S(1)} %get-tuple-element.202), channel_id=1, source_target_pairs={{0,2},{2,4},{4,6},{6,7},{7,5},{5,3},{3,1},{1,0},{8,10},{10,12},{12... | collective-permute-start | bytes 589832 | tf_op jit(solution)/shard_map/ppermute | solution.py:207
  53.7 1.9 collective-permute-done.9.rest_9_
  55.7 1.2 bitcast_select_fusion.6
  56.8 1.1 collective-permute-start.12
  58.9 1.7 collective-permute-done.11.rest_11_
  60.6 1.9 bitcast_select_fusion.4
  65.3 2.0 %bitcast_select_fusion.2 = (bf16[96,1024]{1,0:T(8,128)(2,1)}, bf16[96,1024]{1,0:T(8,128)(2,1)}) fusion(bf16[96,1024]{1,0:T(8,128)(2,1)} %collective-permute-done.13.rest_13_, bf16[1,2048,1024]{2,1,0:T(8,128)(2,1)} %param.15, pred[]{:T(512)S(6)} %eq.21, bf16[96,1024]{1,0:T(8,128)(2,1)} %copy-done.10), kind=kLoop, calls=%fused_computation.22 | loop fusion | flops 196608 | bytes 1179649 | tf_op jit(solution)/shard_map/jit(_where)/select_n | solution.py:205
  69.4 3.4 %fusion.31 = f32[256,1024]{1,0:T(8,128)S(1)} fusion(bf16[256,2048]{1,0:T(8,128)(2,1)S(1)} %bitcast.81, bf16[1,2048,1024]{2,1,0:T(8,128)(2,1)} %param.15), kind=kOutput, calls=%fused_computation.83 | convolution fusion | flops 1073741824 | bytes 6291456 | tf_op jit(solution)/shard_map/dot_general | solution.py:190
  72.8 1.7 convolution_convert_fusion
  74.5 4.7 %all-to-all-start.1 = ((bf16[16,16,2048]{2,1,0:T(8,128)(2,1)}), bf16[16,16,2048]{2,1,0:T(8,128)(2,1)S(1)}, u32[]{:S(2)}, u32[]{:S(2)}) async-start(bf16[16,16,2048]{2,1,0:T(8,128)(2,1)} %bitcast.80), calls=%async_computation.1 | async-start | bytes 2097152 | tf_op jit(solution)/shard_map/all_to_all | solution.py:194
  79.2 1.3 bitcast_select_fusion
  80.5 2.0 %collective-permute-start.18 = (bf16[96,1024]{1,0:T(8,128)(2,1)S(1)}, bf16[96,1024]{1,0:T(8,128)(2,1)S(1)}, u32[]{:S(2)}, u32[]{:S(2)}) collective-permute-start(bf16[96,1024]{1,0:T(8,128)(2,1)S(1)} %get-tuple-element.223), channel_id=1, source_target_pairs={{0,2},{2,4},{4,6},{6,7},{7,5},{5,3},{3,1},{1,0},{8,10},{10,12},{12... | collective-permute-start | bytes 589832 | tf_op jit(solution)/shard_map/ppermute | solution.py:207
  82.6 1.3 maximum_select_fusion
  83.9 2.0 %collective-permute-start.20 = (bf16[96,1024]{1,0:T(8,128)(2,1)S(1)}, bf16[96,1024]{1,0:T(8,128)(2,1)S(1)}, u32[]{:S(2)}, u32[]{:S(2)}) collective-permute-start(bf16[96,1024]{1,0:T(8,128)(2,1)S(1)} %get-tuple-element.227), channel_id=1, source_target_pairs={{0,2},{2,4},{4,6},{6,7},{7,5},{5,3},{3,1},{1,0},{8,10},{10,12},{12... | collective-permute-start | bytes 589832 | tf_op jit(solution)/shard_map/ppermute | solution.py:207
  86.0 15.9 %collective-permute-done.18.rest_18_ = bf16[96,1024]{1,0:T(8,128)(2,1)S(1)} collective-permute-done((bf16[96,1024]{1,0:T(8,128)(2,1)S(1)}, bf16[96,1024]{1,0:T(8,128)(2,1)S(1)}, u32[]{:S(2)}, u32[]{:S(2)}) %collective-permute-start.18) | collective-permute-done | bytes 196640 | tf_op jit(solution)/shard_map/ppermute | solution.py:207
  102.5 8.5 %collective-permute-start.22 = (bf16[96,1024]{1,0:T(8,128)(2,1)S(1)}, bf16[96,1024]{1,0:T(8,128)(2,1)S(1)}, u32[]{:S(2)}, u32[]{:S(2)}) collective-permute-start(bf16[96,1024]{1,0:T(8,128)(2,1)S(1)} %get-tuple-element.231), channel_id=1, source_target_pairs={{0,2},{2,4},{4,6},{6,7},{7,5},{5,3},{3,1},{1,0},{8,10},{10,12},{12... | collective-permute-start | bytes 589832 | tf_op jit(solution)/shard_map/ppermute | solution.py:207
  111.2 4.1 %collective-permute-start.24 = (bf16[96,1024]{1,0:T(8,128)(2,1)S(1)}, bf16[96,1024]{1,0:T(8,128)(2,1)S(1)}, u32[]{:S(2)}, u32[]{:S(2)}) collective-permute-start(bf16[96,1024]{1,0:T(8,128)(2,1)S(1)} %get-tuple-element.235), channel_id=1, source_target_pairs={{0,2},{2,4},{4,6},{6,7},{7,5},{5,3},{3,1},{1,0},{8,10},{10,12},{12... | collective-permute-start | bytes 589832 | tf_op jit(solution)/shard_map/ppermute | solution.py:207
  115.3 1.4 collective-permute-done.23.rest_23_
  116.8 2.7 %collective-permute-start.26 = (bf16[96,1024]{1,0:T(8,128)(2,1)S(1)}, bf16[96,1024]{1,0:T(8,128)(2,1)S(1)}, u32[]{:S(2)}, u32[]{:S(2)}) collective-permute-start(bf16[96,1024]{1,0:T(8,128)(2,1)S(1)} %get-tuple-element.239), channel_id=1, source_target_pairs={{0,2},{2,4},{4,6},{6,7},{7,5},{5,3},{3,1},{1,0},{8,10},{10,12},{12... | collective-permute-start | bytes 589832 | tf_op jit(solution)/shard_map/ppermute | solution.py:207
  119.5 1.5 collective-permute-done.25.rest_25_
  121.1 2.7 %collective-permute-start.28 = (bf16[96,1024]{1,0:T(8,128)(2,1)S(1)}, bf16[96,1024]{1,0:T(8,128)(2,1)S(1)}, u32[]{:S(2)}, u32[]{:S(2)}) collective-permute-start(bf16[96,1024]{1,0:T(8,128)(2,1)S(1)} %get-tuple-element.243), channel_id=1, source_target_pairs={{0,2},{2,4},{4,6},{6,7},{7,5},{5,3},{3,1},{1,0},{8,10},{10,12},{12... | collective-permute-start | bytes 589832 | tf_op jit(solution)/shard_map/ppermute | solution.py:207
  123.7 1.5 collective-permute-done.27.rest_27_
  125.3 2.7 %collective-permute-start.30 = (bf16[96,1024]{1,0:T(8,128)(2,1)S(1)}, bf16[96,1024]{1,0:T(8,128)(2,1)S(1)}, u32[]{:S(2)}, u32[]{:S(2)}) collective-permute-start(bf16[96,1024]{1,0:T(8,128)(2,1)S(1)} %get-tuple-element.247), channel_id=1, source_target_pairs={{0,2},{2,4},{4,6},{6,7},{7,5},{5,3},{3,1},{1,0},{8,10},{10,12},{12... | collective-permute-start | bytes 589832 | tf_op jit(solution)/shard_map/ppermute | solution.py:207
  128.0 1.4 collective-permute-done.29.rest_29_
  129.4 2.6 %collective-permute-start.32 = (bf16[96,1024]{1,0:T(8,128)(2,1)S(1)}, bf16[96,1024]{1,0:T(8,128)(2,1)S(1)}, u32[]{:S(2)}, u32[]{:S(2)}) collective-permute-start(bf16[96,1024]{1,0:T(8,128)(2,1)S(1)} %collective-permute-done.28.rest_28_), channel_id=1, source_target_pairs={{0,2},{2,4},{4,6},{6,7},{7,5},{5,3},{3,1},{1,0},{8,10},{10,12},{12... | collective-permute-start | bytes 589832 | tf_op jit(solution)/shard_map/ppermute | solution.py:207
  132.1 1.7 collective-permute-done.31.rest_31_
  133.8 2.5 %collective-permute-start.34 = (bf16[96,1024]{1,0:T(8,128)(2,1)S(1)}, bf16[96,1024]{1,0:T(8,128)(2,1)S(1)}, u32[]{:S(2)}, u32[]{:S(2)}) collective-permute-start(bf16[96,1024]{1,0:T(8,128)(2,1)S(1)} %collective-permute-done.30.rest_30_), channel_id=1, source_target_pairs={{0,2},{2,4},{4,6},{6,7},{7,5},{5,3},{3,1},{1,0},{8,10},{10,12},{12... | collective-permute-start | bytes 589832 | tf_op jit(solution)/shard_map/ppermute | solution.py:207
  136.3 1.7 collective-permute-done.33.rest_33_
  138.0 2.5 %collective-permute-start.36 = (bf16[96,1024]{1,0:T(8,128)(2,1)S(1)}, bf16[96,1024]{1,0:T(8,128)(2,1)S(1)}, u32[]{:S(2)}, u32[]{:S(2)}) collective-permute-start(bf16[96,1024]{1,0:T(8,128)(2,1)S(1)} %collective-permute-done.32.rest_32_), channel_id=1, source_target_pairs={{0,2},{2,4},{4,6},{6,7},{7,5},{5,3},{3,1},{1,0},{8,10},{10,12},{12... | collective-permute-start | bytes 589832 | tf_op jit(solution)/shard_map/ppermute | solution.py:207
  140.5 1.7 collective-permute-done.35.rest_35_
  142.2 2.5 %collective-permute-start.38 = (bf16[96,1024]{1,0:T(8,128)(2,1)S(1)}, bf16[96,1024]{1,0:T(8,128)(2,1)S(1)}, u32[]{:S(2)}, u32[]{:S(2)}) collective-permute-start(bf16[96,1024]{1,0:T(8,128)(2,1)S(1)} %collective-permute-done.34.rest_34_), channel_id=1, source_target_pairs={{0,2},{2,4},{4,6},{6,7},{7,5},{5,3},{3,1},{1,0},{8,10},{10,12},{12... | collective-permute-start | bytes 589832 | tf_op jit(solution)/shard_map/ppermute | solution.py:207
  144.7 1.7 collective-permute-done.37.rest_37_
  146.4 2.5 %collective-permute-start.40 = (bf16[96,1024]{1,0:T(8,128)(2,1)S(1)}, bf16[96,1024]{1,0:T(8,128)(2,1)S(1)}, u32[]{:S(2)}, u32[]{:S(2)}) collective-permute-start(bf16[96,1024]{1,0:T(8,128)(2,1)S(1)} %collective-permute-done.36.rest_36_), channel_id=1, source_target_pairs={{0,2},{2,4},{4,6},{6,7},{7,5},{5,3},{3,1},{1,0},{8,10},{10,12},{12... | collective-permute-start | bytes 589832 | tf_op jit(solution)/shard_map/ppermute | solution.py:207
  148.9 1.7 collective-permute-done.39.rest_39_
  150.6 2.5 %collective-permute-start.42 = (bf16[96,1024]{1,0:T(8,128)(2,1)S(1)}, bf16[96,1024]{1,0:T(8,128)(2,1)S(1)}, u32[]{:S(2)}, u32[]{:S(2)}) collective-permute-start(bf16[96,1024]{1,0:T(8,128)(2,1)S(1)} %collective-permute-done.38.rest_38_), channel_id=1, source_target_pairs={{0,2},{2,4},{4,6},{6,7},{7,5},{5,3},{3,1},{1,0},{8,10},{10,12},{12... | collective-permute-start | bytes 589832 | tf_op jit(solution)/shard_map/ppermute | solution.py:207
  153.1 1.7 collective-permute-done.41.rest_41_
  154.8 2.5 %collective-permute-start.44 = (bf16[96,1024]{1,0:T(8,128)(2,1)S(1)}, bf16[96,1024]{1,0:T(8,128)(2,1)}, u32[]{:S(2)}, u32[]{:S(2)}) collective-permute-start(bf16[96,1024]{1,0:T(8,128)(2,1)S(1)} %collective-permute-done.40.rest_40_), channel_id=1, source_target_pairs={{0,2},{2,4},{4,6},{6,7},{7,5},{5,3},{3,1},{1,0},{8,10},{10,12},{12... | collective-permute-start | bytes 589832 | tf_op jit(solution)/shard_map/ppermute | solution.py:207
  157.3 1.7 collective-permute-done.43.rest_43_
  159.0 2.5 %collective-permute-start.46 = (bf16[96,1024]{1,0:T(8,128)(2,1)S(1)}, bf16[96,1024]{1,0:T(8,128)(2,1)}, u32[]{:S(2)}, u32[]{:S(2)}) collective-permute-start(bf16[96,1024]{1,0:T(8,128)(2,1)S(1)} %collective-permute-done.42.rest_42_), channel_id=1, source_target_pairs={{0,2},{2,4},{4,6},{6,7},{7,5},{5,3},{3,1},{1,0},{8,10},{10,12},{12... | collective-permute-start | bytes 589832 | tf_op jit(solution)/shard_map/ppermute | solution.py:207
  161.5 1.8 collective-permute-done.45.rest_45_
  163.3 2.5 %collective-permute-start.48 = (bf16[96,1024]{1,0:T(8,128)(2,1)}, bf16[96,1024]{1,0:T(8,128)(2,1)}, u32[]{:S(2)}, u32[]{:S(2)}) collective-permute-start(bf16[96,1024]{1,0:T(8,128)(2,1)} %collective-permute-done.44.rest_44_), channel_id=1, source_target_pairs={{0,2},{2,4},{4,6},{6,7},{7,5},{5,3},{3,1},{1,0},{8,10},{10,12},{12... | collective-permute-start | bytes 589832 | tf_op jit(solution)/shard_map/ppermute | solution.py:207
  165.9 1.6 collective-permute-done.47.rest_47_
  167.5 2.6 %collective-permute-start.50 = (bf16[96,1024]{1,0:T(8,128)(2,1)}, bf16[96,1024]{1,0:T(8,128)(2,1)}, u32[]{:S(2)}, u32[]{:S(2)}) collective-permute-start(bf16[96,1024]{1,0:T(8,128)(2,1)} %collective-permute-done.46.rest_46_), channel_id=1, source_target_pairs={{0,2},{2,4},{4,6},{6,7},{7,5},{5,3},{3,1},{1,0},{8,10},{10,12},{12... | collective-permute-start | bytes 589832 | tf_op jit(solution)/shard_map/ppermute | solution.py:207
  171.9 2.4 %collective-permute-start.52 = (bf16[96,1024]{1,0:T(8,128)(2,1)}, bf16[96,1024]{1,0:T(8,128)(2,1)S(1)}, u32[]{:S(2)}, u32[]{:S(2)}) collective-permute-start(bf16[96,1024]{1,0:T(8,128)(2,1)} %collective-permute-done.48.rest_48_), channel_id=1, source_target_pairs={{0,2},{2,4},{4,6},{6,7},{7,5},{5,3},{3,1},{1,0},{8,10},{10,12},{12... | collective-permute-start | bytes 589832 | tf_op jit(solution)/shard_map/ppermute | solution.py:207
  174.3 1.8 collective-permute-done.51.rest_51_
  176.1 2.4 %collective-permute-start.54 = (bf16[96,1024]{1,0:T(8,128)(2,1)}, bf16[96,1024]{1,0:T(8,128)(2,1)}, u32[]{:S(2)}, u32[]{:S(2)}) collective-permute-start(bf16[96,1024]{1,0:T(8,128)(2,1)} %collective-permute-done.50.rest_50_), channel_id=1, source_target_pairs={{0,2},{2,4},{4,6},{6,7},{7,5},{5,3},{3,1},{1,0},{8,10},{10,12},{12... | collective-permute-start | bytes 589832 | tf_op jit(solution)/shard_map/ppermute | solution.py:207
  180.2 2.1 %collective-permute-done.54.rest_54_ = bf16[96,1024]{1,0:T(8,128)(2,1)} collective-permute-done((bf16[96,1024]{1,0:T(8,128)(2,1)}, bf16[96,1024]{1,0:T(8,128)(2,1)}, u32[]{:S(2)}, u32[]{:S(2)}) %collective-permute-start.54) | collective-permute-done | bytes 196640 | tf_op jit(solution)/shard_map/ppermute | solution.py:207
  182.3 2.2 %collective-permute-done.55.rest_55_ = bf16[96,1024]{1,0:T(8,128)(2,1)} collective-permute-done((bf16[96,1024]{1,0:T(8,128)(2,1)}, bf16[96,1024]{1,0:T(8,128)(2,1)}, u32[]{:S(2)}, u32[]{:S(2)}) %collective-permute-start.55) | collective-permute-done | bytes 196640 | tf_op jit(solution)/shard_map/ppermute | solution.py:207
  184.6 11.1 %shard_map.104 = bf16[768,2048]{1,0:T(8,128)(2,1)} custom-call(s32[2]{0:T(128)} %pad_add_fusion.hops, bf16[768,2048]{1,0:T(8,128)(2,1)} %x.1, f32[768,1]{1,0:T(8,128)} %copy.11.weight, bf16[2048,1024]{1,0:T(8,128)(2,1)} %bitcast.70, bf16[512,2048]{1,0:T(8,128)(2,1)} %bitcast.73, bf16[96,1024]{1,0:T(8,128)(2,1)} %collective-permute-done.2.rest_0_, ...), custom_call_target="tpu_custom_call" | custom-call | flops 4831838208 | bytes 20971520 | tf_op jit(solution)/shard_map/pallas_call | solution.py:96
  (197 shorter events, 14.9 us)
Async XLA Ops:
  2.9 22.5 %collective-permute-start = (bf16[96,1024]{1,0:T(8,128)(2,1)}, bf16[96,1024]{1,0:T(8,128)(2,1)}, u32[]{:S(2)}, u32[]{:S(2)}) collective-permute-start(bf16[96,1024]{1,0:T(8,128)(2,1)} %get-tuple-element.180), channel_id=1, source_target_pairs={{0,2},{2,4},{4,6},{6,7},{7,5},{5,3},{3,1},{1,0},{8,10},{10,12},{12... | collective-permute-start | bytes 589832 | tf_op jit(solution)/shard_map/ppermute | solution.py:207
  6.0 19.5 %collective-permute-start.1 = (bf16[96,1024]{1,0:T(8,128)(2,1)}, bf16[96,1024]{1,0:T(8,128)(2,1)}, u32[]{:S(2)}, u32[]{:S(2)}) collective-permute-start(bf16[96,1024]{1,0:T(8,128)(2,1)} %get-tuple-element.181), channel_id=1, source_target_pairs={{2,0},{4,2},{6,4},{7,6},{5,7},{3,5},{1,3},{0,1},{10,8},{12,10},{14... | collective-permute-start | bytes 589832 | tf_op jit(solution)/shard_map/ppermute | solution.py:207
  6.0 19.5 %collective-permute-start.2 = (bf16[96,1024]{1,0:T(8,128)(2,1)}, bf16[96,1024]{1,0:T(8,128)(2,1)}, u32[]{:S(2)}, u32[]{:S(2)}) collective-permute-start(bf16[96,1024]{1,0:T(8,128)(2,1)} %get-tuple-element.184), channel_id=1, source_target_pairs={{0,2},{2,4},{4,6},{6,7},{7,5},{5,3},{3,1},{1,0},{8,10},{10,12},{12... | collective-permute-start | bytes 589832 | tf_op jit(solution)/shard_map/ppermute | solution.py:207
  8.0 17.4 %collective-permute-start.3 = (bf16[96,1024]{1,0:T(8,128)(2,1)}, bf16[96,1024]{1,0:T(8,128)(2,1)}, u32[]{:S(2)}, u32[]{:S(2)}) collective-permute-start(bf16[96,1024]{1,0:T(8,128)(2,1)} %get-tuple-element.185), channel_id=1, source_target_pairs={{2,0},{4,2},{6,4},{7,6},{5,7},{3,5},{1,3},{0,1},{10,8},{12,10},{14... | collective-permute-start | bytes 589832 | tf_op jit(solution)/shard_map/ppermute | solution.py:207
  10.6 54.7 %all-to-all-start = ((bf16[16,16,2048]{2,1,0:T(8,128)(2,1)}), bf16[16,16,2048]{2,1,0:T(8,128)(2,1)S(1)}, u32[]{:S(2)}, u32[]{:S(2)}) async-start(bf16[16,16,2048]{2,1,0:T(8,128)(2,1)} %bitcast.25), calls=%async_computation | async-start | bytes 2097152 | tf_op jit(solution)/shard_map/all_to_all | solution.py:162
  26.7 12.9 %collective-permute-start.4 = (bf16[96,1024]{1,0:T(8,128)(2,1)S(1)}, bf16[96,1024]{1,0:T(8,128)(2,1)S(1)}, u32[]{:S(2)}, u32[]{:S(2)}) collective-permute-start(bf16[96,1024]{1,0:T(8,128)(2,1)S(1)} %get-tuple-element.188), channel_id=1, source_target_pairs={{0,2},{2,4},{4,6},{6,7},{7,5},{5,3},{3,1},{1,0},{8,10},{10,12},{12... | collective-permute-start | bytes 589832 | tf_op jit(solution)/shard_map/ppermute | solution.py:207
  28.7 13.4 %collective-permute-start.5 = (bf16[96,1024]{1,0:T(8,128)(2,1)S(1)}, bf16[96,1024]{1,0:T(8,128)(2,1)S(1)}, u32[]{:S(2)}, u32[]{:S(2)}) collective-permute-start(bf16[96,1024]{1,0:T(8,128)(2,1)S(1)} %get-tuple-element.189), channel_id=1, source_target_pairs={{2,0},{4,2},{6,4},{7,6},{5,7},{3,5},{1,3},{0,1},{10,8},{12,10},{14... | collective-permute-start | bytes 589832 | tf_op jit(solution)/shard_map/ppermute | solution.py:207
  30.1 19.9 %collective-permute-start.6 = (bf16[96,1024]{1,0:T(8,128)(2,1)S(1)}, bf16[96,1024]{1,0:T(8,128)(2,1)S(1)}, u32[]{:S(2)}, u32[]{:S(2)}) collective-permute-start(bf16[96,1024]{1,0:T(8,128)(2,1)S(1)} %get-tuple-element.194), channel_id=1, source_target_pairs={{0,2},{2,4},{4,6},{6,7},{7,5},{5,3},{3,1},{1,0},{8,10},{10,12},{12... | collective-permute-start | bytes 589832 | tf_op jit(solution)/shard_map/ppermute | solution.py:207
  32.0 18.0 %collective-permute-start.7 = (bf16[96,1024]{1,0:T(8,128)(2,1)S(1)}, bf16[96,1024]{1,0:T(8,128)(2,1)S(1)}, u32[]{:S(2)}, u32[]{:S(2)}) collective-permute-start(bf16[96,1024]{1,0:T(8,128)(2,1)S(1)} %get-tuple-element.195), channel_id=1, source_target_pairs={{2,0},{4,2},{6,4},{7,6},{5,7},{3,5},{1,3},{0,1},{10,8},{12,10},{14... | collective-permute-start | bytes 589832 | tf_op jit(solution)/shard_map/ppermute | solution.py:207
  43.2 10.5 %collective-permute-start.8 = (bf16[96,1024]{1,0:T(8,128)(2,1)S(1)}, bf16[96,1024]{1,0:T(8,128)(2,1)S(1)}, u32[]{:S(2)}, u32[]{:S(2)}) collective-permute-start(bf16[96,1024]{1,0:T(8,128)(2,1)S(1)} %get-tuple-element.198), channel_id=1, source_target_pairs={{0,2},{2,4},{4,6},{6,7},{7,5},{5,3},{3,1},{1,0},{8,10},{10,12},{12... | collective-permute-start | bytes 589832 | tf_op jit(solution)/shard_map/ppermute | solution.py:207
  50.0 5.7 %collective-permute-start.9 = (bf16[96,1024]{1,0:T(8,128)(2,1)S(1)}, bf16[96,1024]{1,0:T(8,128)(2,1)S(1)}, u32[]{:S(2)}, u32[]{:S(2)}) collective-permute-start(bf16[96,1024]{1,0:T(8,128)(2,1)S(1)} %get-tuple-element.199), channel_id=1, source_target_pairs={{2,0},{4,2},{6,4},{7,6},{5,7},{3,5},{1,3},{0,1},{10,8},{12,10},{14... | collective-permute-start | bytes 589832 | tf_op jit(solution)/shard_map/ppermute | solution.py:207
  51.2 7.7 %collective-permute-start.10 = (bf16[96,1024]{1,0:T(8,128)(2,1)S(1)}, bf16[96,1024]{1,0:T(8,128)(2,1)S(1)}, u32[]{:S(2)}, u32[]{:S(2)}) collective-permute-start(bf16[96,1024]{1,0:T(8,128)(2,1)S(1)} %get-tuple-element.202), channel_id=1, source_target_pairs={{0,2},{2,4},{4,6},{6,7},{7,5},{5,3},{3,1},{1,0},{8,10},{10,12},{12... | collective-permute-start | bytes 589832 | tf_op jit(solution)/shard_map/ppermute | solution.py:207
  53.7 6.9 %collective-permute-start.11 = (bf16[96,1024]{1,0:T(8,128)(2,1)S(1)}, bf16[96,1024]{1,0:T(8,128)(2,1)S(1)}, u32[]{:S(2)}, u32[]{:S(2)}) collective-permute-start(bf16[96,1024]{1,0:T(8,128)(2,1)S(1)} %get-tuple-element.203), channel_id=1, source_target_pairs={{2,0},{4,2},{6,4},{7,6},{5,7},{3,5},{1,3},{0,1},{10,8},{12,10},{14... | collective-permute-start | bytes 589832 | tf_op jit(solution)/shard_map/ppermute | solution.py:207
  56.8 7.7 %collective-permute-start.12 = (bf16[96,1024]{1,0:T(8,128)(2,1)S(1)}, bf16[96,1024]{1,0:T(8,128)(2,1)S(1)}, u32[]{:S(2)}, u32[]{:S(2)}) collective-permute-start(bf16[96,1024]{1,0:T(8,128)(2,1)S(1)} %get-tuple-element.206), channel_id=1, source_target_pairs={{0,2},{2,4},{4,6},{6,7},{7,5},{5,3},{3,1},{1,0},{8,10},{10,12},{12... | collective-permute-start | bytes 589832 | tf_op jit(solution)/shard_map/ppermute | solution.py:207
  57.9 7.4 %collective-permute-start.13 = (bf16[96,1024]{1,0:T(8,128)(2,1)S(1)}, bf16[96,1024]{1,0:T(8,128)(2,1)}, u32[]{:S(2)}, u32[]{:S(2)}) collective-permute-start(bf16[96,1024]{1,0:T(8,128)(2,1)S(1)} %get-tuple-element.207), channel_id=1, source_target_pairs={{2,0},{4,2},{6,4},{7,6},{5,7},{3,5},{1,3},{0,1},{10,8},{12,10},{14... | collective-permute-start | bytes 589832 | tf_op jit(solution)/shard_map/ppermute | solution.py:207
  62.5 12.0 %collective-permute-start.14 = (bf16[96,1024]{1,0:T(8,128)(2,1)}, bf16[96,1024]{1,0:T(8,128)(2,1)}, u32[]{:S(2)}, u32[]{:S(2)}) collective-permute-start(bf16[96,1024]{1,0:T(8,128)(2,1)} %get-tuple-element.210), channel_id=1, source_target_pairs={{0,2},{2,4},{4,6},{6,7},{7,5},{5,3},{3,1},{1,0},{8,10},{10,12},{12... | collective-permute-start | bytes 589832 | tf_op jit(solution)/shard_map/ppermute | solution.py:207
  63.5 11.0 %collective-permute-start.15 = (bf16[96,1024]{1,0:T(8,128)(2,1)}, bf16[96,1024]{1,0:T(8,128)(2,1)}, u32[]{:S(2)}, u32[]{:S(2)}) collective-permute-start(bf16[96,1024]{1,0:T(8,128)(2,1)} %get-tuple-element.211), channel_id=1, source_target_pairs={{2,0},{4,2},{6,4},{7,6},{5,7},{3,5},{1,3},{0,1},{10,8},{12,10},{14... | collective-permute-start | bytes 589832 | tf_op jit(solution)/shard_map/ppermute | solution.py:207
  67.3 15.2 %collective-permute-start.16 = (bf16[96,1024]{1,0:T(8,128)(2,1)}, bf16[96,1024]{1,0:T(8,128)(2,1)}, u32[]{:S(2)}, u32[]{:S(2)}) collective-permute-start(bf16[96,1024]{1,0:T(8,128)(2,1)} %get-tuple-element.216), channel_id=1, source_target_pairs={{0,2},{2,4},{4,6},{6,7},{7,5},{5,3},{3,1},{1,0},{8,10},{10,12},{12... | collective-permute-start | bytes 589832 | tf_op jit(solution)/shard_map/ppermute | solution.py:207
  68.3 14.3 %collective-permute-start.17 = (bf16[96,1024]{1,0:T(8,128)(2,1)}, bf16[96,1024]{1,0:T(8,128)(2,1)}, u32[]{:S(2)}, u32[]{:S(2)}) collective-permute-start(bf16[96,1024]{1,0:T(8,128)(2,1)} %get-tuple-element.217), channel_id=1, source_target_pairs={{2,0},{4,2},{6,4},{7,6},{5,7},{3,5},{1,3},{0,1},{10,8},{12,10},{14... | collective-permute-start | bytes 589832 | tf_op jit(solution)/shard_map/ppermute | solution.py:207
  74.5 97.3 %all-to-all-start.1 = ((bf16[16,16,2048]{2,1,0:T(8,128)(2,1)}), bf16[16,16,2048]{2,1,0:T(8,128)(2,1)S(1)}, u32[]{:S(2)}, u32[]{:S(2)}) async-start(bf16[16,16,2048]{2,1,0:T(8,128)(2,1)} %bitcast.80), calls=%async_computation.1 | async-start | bytes 2097152 | tf_op jit(solution)/shard_map/all_to_all | solution.py:194
  79.2 90.9 %copy-start.52 = (f32[64,2]{0,1:T(2,128)S(1)}, f32[64,2]{0,1:T(2,128)}, u32[]{:S(2)}) copy-start(f32[64,2]{0,1:T(2,128)} %param.14) | copy-start | bytes 1540
  80.5 21.4 %collective-permute-start.18 = (bf16[96,1024]{1,0:T(8,128)(2,1)S(1)}, bf16[96,1024]{1,0:T(8,128)(2,1)S(1)}, u32[]{:S(2)}, u32[]{:S(2)}) collective-permute-start(bf16[96,1024]{1,0:T(8,128)(2,1)S(1)} %get-tuple-element.223), channel_id=1, source_target_pairs={{0,2},{2,4},{4,6},{6,7},{7,5},{5,3},{3,1},{1,0},{8,10},{10,12},{12... | collective-permute-start | bytes 589832 | tf_op jit(solution)/shard_map/ppermute | solution.py:207
  82.5 20.0 %collective-permute-start.19 = (bf16[96,1024]{1,0:T(8,128)(2,1)S(1)}, bf16[96,1024]{1,0:T(8,128)(2,1)S(1)}, u32[]{:S(2)}, u32[]{:S(2)}) collective-permute-start(bf16[96,1024]{1,0:T(8,128)(2,1)S(1)} %get-tuple-element.224), channel_id=1, source_target_pairs={{2,0},{4,2},{6,4},{7,6},{5,7},{3,5},{1,3},{0,1},{10,8},{12,10},{14... | collective-permute-start | bytes 589832 | tf_op jit(solution)/shard_map/ppermute | solution.py:207
  83.9 94.6 %copy-start.41 = (s32[256]{0:T(256)S(1)}, s32[256]{0:T(256)}, u32[]{:S(2)}) copy-start(s32[256]{0:T(256)} %copy-done.40) | copy-start | bytes 3076
  83.9 94.6 %copy-start.43 = (s32[256]{0:T(256)S(1)}, s32[256]{0:T(256)}, u32[]{:S(2)}) copy-start(s32[256]{0:T(256)} %copy-done.42) | copy-start | bytes 3076
  83.9 94.6 %copy-start.45 = (s32[64]{0:T(128)S(1)}, s32[64]{0:T(128)}, u32[]{:S(2)}) copy-start(s32[64]{0:T(128)} %copy-done.44) | copy-start | bytes 772
  83.9 94.6 %copy-start.47 = (s32[64]{0:T(128)S(1)}, s32[64]{0:T(128)}, u32[]{:S(2)}) copy-start(s32[64]{0:T(128)} %copy-done.46) | copy-start | bytes 772
  83.9 94.6 %copy-start.49 = (pred[256]{0:T(512)(128)(4,1)S(1)}, pred[256]{0:T(512)(128)(4,1)}, u32[]{:S(2)}) copy-start(pred[256]{0:T(512)(128)(4,1)} %copy-done.48) | copy-start | bytes 772
  83.9 27.2 %collective-permute-start.20 = (bf16[96,1024]{1,0:T(8,128)(2,1)S(1)}, bf16[96,1024]{1,0:T(8,128)(2,1)S(1)}, u32[]{:S(2)}, u32[]{:S(2)}) collective-permute-start(bf16[96,1024]{1,0:T(8,128)(2,1)S(1)} %get-tuple-element.227), channel_id=1, source_target_pairs={{0,2},{2,4},{4,6},{6,7},{7,5},{5,3},{3,1},{1,0},{8,10},{10,12},{12... | collective-permute-start | bytes 589832 | tf_op jit(solution)/shard_map/ppermute | solution.py:207
  85.9 25.2 %collective-permute-start.21 = (bf16[96,1024]{1,0:T(8,128)(2,1)S(1)}, bf16[96,1024]{1,0:T(8,128)(2,1)S(1)}, u32[]{:S(2)}, u32[]{:S(2)}) collective-permute-start(bf16[96,1024]{1,0:T(8,128)(2,1)S(1)} %get-tuple-element.228), channel_id=1, source_target_pairs={{2,0},{4,2},{6,4},{7,6},{5,7},{3,5},{1,3},{0,1},{10,8},{12,10},{14... | collective-permute-start | bytes 589832 | tf_op jit(solution)/shard_map/ppermute | solution.py:207
  102.5 12.8 %collective-permute-start.22 = (bf16[96,1024]{1,0:T(8,128)(2,1)S(1)}, bf16[96,1024]{1,0:T(8,128)(2,1)S(1)}, u32[]{:S(2)}, u32[]{:S(2)}) collective-permute-start(bf16[96,1024]{1,0:T(8,128)(2,1)S(1)} %get-tuple-element.231), channel_id=1, source_target_pairs={{0,2},{2,4},{4,6},{6,7},{7,5},{5,3},{3,1},{1,0},{8,10},{10,12},{12... | collective-permute-start | bytes 589832 | tf_op jit(solution)/shard_map/ppermute | solution.py:207
  111.1 5.7 %collective-permute-start.23 = (bf16[96,1024]{1,0:T(8,128)(2,1)S(1)}, bf16[96,1024]{1,0:T(8,128)(2,1)S(1)}, u32[]{:S(2)}, u32[]{:S(2)}) collective-permute-start(bf16[96,1024]{1,0:T(8,128)(2,1)S(1)} %get-tuple-element.232), channel_id=1, source_target_pairs={{2,0},{4,2},{6,4},{7,6},{5,7},{3,5},{1,3},{0,1},{10,8},{12,10},{14... | collective-permute-start | bytes 589832 | tf_op jit(solution)/shard_map/ppermute | solution.py:207
  111.2 8.3 %collective-permute-start.24 = (bf16[96,1024]{1,0:T(8,128)(2,1)S(1)}, bf16[96,1024]{1,0:T(8,128)(2,1)S(1)}, u32[]{:S(2)}, u32[]{:S(2)}) collective-permute-start(bf16[96,1024]{1,0:T(8,128)(2,1)S(1)} %get-tuple-element.235), channel_id=1, source_target_pairs={{0,2},{2,4},{4,6},{6,7},{7,5},{5,3},{3,1},{1,0},{8,10},{10,12},{12... | collective-permute-start | bytes 589832 | tf_op jit(solution)/shard_map/ppermute | solution.py:207
  115.3 5.7 %collective-permute-start.25 = (bf16[96,1024]{1,0:T(8,128)(2,1)S(1)}, bf16[96,1024]{1,0:T(8,128)(2,1)S(1)}, u32[]{:S(2)}, u32[]{:S(2)}) collective-permute-start(bf16[96,1024]{1,0:T(8,128)(2,1)S(1)} %get-tuple-element.236), channel_id=1, source_target_pairs={{2,0},{4,2},{6,4},{7,6},{5,7},{3,5},{1,3},{0,1},{10,8},{12,10},{14... | collective-permute-start | bytes 589832 | tf_op jit(solution)/shard_map/ppermute | solution.py:207
  116.8 6.9 %collective-permute-start.26 = (bf16[96,1024]{1,0:T(8,128)(2,1)S(1)}, bf16[96,1024]{1,0:T(8,128)(2,1)S(1)}, u32[]{:S(2)}, u32[]{:S(2)}) collective-permute-start(bf16[96,1024]{1,0:T(8,128)(2,1)S(1)} %get-tuple-element.239), channel_id=1, source_target_pairs={{0,2},{2,4},{4,6},{6,7},{7,5},{5,3},{3,1},{1,0},{8,10},{10,12},{12... | collective-permute-start | bytes 589832 | tf_op jit(solution)/shard_map/ppermute | solution.py:207
  119.5 5.7 %collective-permute-start.27 = (bf16[96,1024]{1,0:T(8,128)(2,1)S(1)}, bf16[96,1024]{1,0:T(8,128)(2,1)S(1)}, u32[]{:S(2)}, u32[]{:S(2)}) collective-permute-start(bf16[96,1024]{1,0:T(8,128)(2,1)S(1)} %get-tuple-element.240), channel_id=1, source_target_pairs={{2,0},{4,2},{6,4},{7,6},{5,7},{3,5},{1,3},{0,1},{10,8},{12,10},{14... | collective-permute-start | bytes 589832 | tf_op jit(solution)/shard_map/ppermute | solution.py:207
  121.1 6.9 %collective-permute-start.28 = (bf16[96,1024]{1,0:T(8,128)(2,1)S(1)}, bf16[96,1024]{1,0:T(8,128)(2,1)S(1)}, u32[]{:S(2)}, u32[]{:S(2)}) collective-permute-start(bf16[96,1024]{1,0:T(8,128)(2,1)S(1)} %get-tuple-element.243), channel_id=1, source_target_pairs={{0,2},{2,4},{4,6},{6,7},{7,5},{5,3},{3,1},{1,0},{8,10},{10,12},{12... | collective-permute-start | bytes 589832 | tf_op jit(solution)/shard_map/ppermute | solution.py:207
  123.7 5.7 %collective-permute-start.29 = (bf16[96,1024]{1,0:T(8,128)(2,1)S(1)}, bf16[96,1024]{1,0:T(8,128)(2,1)S(1)}, u32[]{:S(2)}, u32[]{:S(2)}) collective-permute-start(bf16[96,1024]{1,0:T(8,128)(2,1)S(1)} %get-tuple-element.244), channel_id=1, source_target_pairs={{2,0},{4,2},{6,4},{7,6},{5,7},{3,5},{1,3},{0,1},{10,8},{12,10},{14... | collective-permute-start | bytes 589832 | tf_op jit(solution)/shard_map/ppermute | solution.py:207
  125.3 6.8 %collective-permute-start.30 = (bf16[96,1024]{1,0:T(8,128)(2,1)S(1)}, bf16[96,1024]{1,0:T(8,128)(2,1)S(1)}, u32[]{:S(2)}, u32[]{:S(2)}) collective-permute-start(bf16[96,1024]{1,0:T(8,128)(2,1)S(1)} %get-tuple-element.247), channel_id=1, source_target_pairs={{0,2},{2,4},{4,6},{6,7},{7,5},{5,3},{3,1},{1,0},{8,10},{10,12},{12... | collective-permute-start | bytes 589832 | tf_op jit(solution)/shard_map/ppermute | solution.py:207
  128.0 5.8 %collective-permute-start.31 = (bf16[96,1024]{1,0:T(8,128)(2,1)S(1)}, bf16[96,1024]{1,0:T(8,128)(2,1)S(1)}, u32[]{:S(2)}, u32[]{:S(2)}) collective-permute-start(bf16[96,1024]{1,0:T(8,128)(2,1)S(1)} %get-tuple-element.248), channel_id=1, source_target_pairs={{2,0},{4,2},{6,4},{7,6},{5,7},{3,5},{1,3},{0,1},{10,8},{12,10},{14... | collective-permute-start | bytes 589832 | tf_op jit(solution)/shard_map/ppermute | solution.py:207
  129.4 6.8 %collective-permute-start.32 = (bf16[96,1024]{1,0:T(8,128)(2,1)S(1)}, bf16[96,1024]{1,0:T(8,128)(2,1)S(1)}, u32[]{:S(2)}, u32[]{:S(2)}) collective-permute-start(bf16[96,1024]{1,0:T(8,128)(2,1)S(1)} %collective-permute-done.28.rest_28_), channel_id=1, source_target_pairs={{0,2},{2,4},{4,6},{6,7},{7,5},{5,3},{3,1},{1,0},{8,10},{10,12},{12... | collective-permute-start | bytes 589832 | tf_op jit(solution)/shard_map/ppermute | solution.py:207
  132.0 5.9 %collective-permute-start.33 = (bf16[96,1024]{1,0:T(8,128)(2,1)S(1)}, bf16[96,1024]{1,0:T(8,128)(2,1)S(1)}, u32[]{:S(2)}, u32[]{:S(2)}) collective-permute-start(bf16[96,1024]{1,0:T(8,128)(2,1)S(1)} %collective-permute-done.29.rest_29_), channel_id=1, source_target_pairs={{2,0},{4,2},{6,4},{7,6},{5,7},{3,5},{1,3},{0,1},{10,8},{12,10},{14... | collective-permute-start | bytes 589832 | tf_op jit(solution)/shard_map/ppermute | solution.py:207
  133.8 6.7 %collective-permute-start.34 = (bf16[96,1024]{1,0:T(8,128)(2,1)S(1)}, bf16[96,1024]{1,0:T(8,128)(2,1)S(1)}, u32[]{:S(2)}, u32[]{:S(2)}) collective-permute-start(bf16[96,1024]{1,0:T(8,128)(2,1)S(1)} %collective-permute-done.30.rest_30_), channel_id=1, source_target_pairs={{0,2},{2,4},{4,6},{6,7},{7,5},{5,3},{3,1},{1,0},{8,10},{10,12},{12... | collective-permute-start | bytes 589832 | tf_op jit(solution)/shard_map/ppermute | solution.py:207
  136.3 5.9 %collective-permute-start.35 = (bf16[96,1024]{1,0:T(8,128)(2,1)S(1)}, bf16[96,1024]{1,0:T(8,128)(2,1)S(1)}, u32[]{:S(2)}, u32[]{:S(2)}) collective-permute-start(bf16[96,1024]{1,0:T(8,128)(2,1)S(1)} %collective-permute-done.31.rest_31_), channel_id=1, source_target_pairs={{2,0},{4,2},{6,4},{7,6},{5,7},{3,5},{1,3},{0,1},{10,8},{12,10},{14... | collective-permute-start | bytes 589832 | tf_op jit(solution)/shard_map/ppermute | solution.py:207
  138.0 6.7 %collective-permute-start.36 = (bf16[96,1024]{1,0:T(8,128)(2,1)S(1)}, bf16[96,1024]{1,0:T(8,128)(2,1)S(1)}, u32[]{:S(2)}, u32[]{:S(2)}) collective-permute-start(bf16[96,1024]{1,0:T(8,128)(2,1)S(1)} %collective-permute-done.32.rest_32_), channel_id=1, source_target_pairs={{0,2},{2,4},{4,6},{6,7},{7,5},{5,3},{3,1},{1,0},{8,10},{10,12},{12... | collective-permute-start | bytes 589832 | tf_op jit(solution)/shard_map/ppermute | solution.py:207
  140.5 5.9 %collective-permute-start.37 = (bf16[96,1024]{1,0:T(8,128)(2,1)S(1)}, bf16[96,1024]{1,0:T(8,128)(2,1)S(1)}, u32[]{:S(2)}, u32[]{:S(2)}) collective-permute-start(bf16[96,1024]{1,0:T(8,128)(2,1)S(1)} %collective-permute-done.33.rest_33_), channel_id=1, source_target_pairs={{2,0},{4,2},{6,4},{7,6},{5,7},{3,5},{1,3},{0,1},{10,8},{12,10},{14... | collective-permute-start | bytes 589832 | tf_op jit(solution)/shard_map/ppermute | solution.py:207
  142.2 6.7 %collective-permute-start.38 = (bf16[96,1024]{1,0:T(8,128)(2,1)S(1)}, bf16[96,1024]{1,0:T(8,128)(2,1)S(1)}, u32[]{:S(2)}, u32[]{:S(2)}) collective-permute-start(bf16[96,1024]{1,0:T(8,128)(2,1)S(1)} %collective-permute-done.34.rest_34_), channel_id=1, source_target_pairs={{0,2},{2,4},{4,6},{6,7},{7,5},{5,3},{3,1},{1,0},{8,10},{10,12},{12... | collective-permute-start | bytes 589832 | tf_op jit(solution)/shard_map/ppermute | solution.py:207
  144.7 5.9 %collective-permute-start.39 = (bf16[96,1024]{1,0:T(8,128)(2,1)S(1)}, bf16[96,1024]{1,0:T(8,128)(2,1)S(1)}, u32[]{:S(2)}, u32[]{:S(2)}) collective-permute-start(bf16[96,1024]{1,0:T(8,128)(2,1)S(1)} %collective-permute-done.35.rest_35_), channel_id=1, source_target_pairs={{2,0},{4,2},{6,4},{7,6},{5,7},{3,5},{1,3},{0,1},{10,8},{12,10},{14... | collective-permute-start | bytes 589832 | tf_op jit(solution)/shard_map/ppermute | solution.py:207
  146.4 6.7 %collective-permute-start.40 = (bf16[96,1024]{1,0:T(8,128)(2,1)S(1)}, bf16[96,1024]{1,0:T(8,128)(2,1)S(1)}, u32[]{:S(2)}, u32[]{:S(2)}) collective-permute-start(bf16[96,1024]{1,0:T(8,128)(2,1)S(1)} %collective-permute-done.36.rest_36_), channel_id=1, source_target_pairs={{0,2},{2,4},{4,6},{6,7},{7,5},{5,3},{3,1},{1,0},{8,10},{10,12},{12... | collective-permute-start | bytes 589832 | tf_op jit(solution)/shard_map/ppermute | solution.py:207
  148.9 5.9 %collective-permute-start.41 = (bf16[96,1024]{1,0:T(8,128)(2,1)S(1)}, bf16[96,1024]{1,0:T(8,128)(2,1)S(1)}, u32[]{:S(2)}, u32[]{:S(2)}) collective-permute-start(bf16[96,1024]{1,0:T(8,128)(2,1)S(1)} %collective-permute-done.37.rest_37_), channel_id=1, source_target_pairs={{2,0},{4,2},{6,4},{7,6},{5,7},{3,5},{1,3},{0,1},{10,8},{12,10},{14... | collective-permute-start | bytes 589832 | tf_op jit(solution)/shard_map/ppermute | solution.py:207
  150.6 6.7 %collective-permute-start.42 = (bf16[96,1024]{1,0:T(8,128)(2,1)S(1)}, bf16[96,1024]{1,0:T(8,128)(2,1)S(1)}, u32[]{:S(2)}, u32[]{:S(2)}) collective-permute-start(bf16[96,1024]{1,0:T(8,128)(2,1)S(1)} %collective-permute-done.38.rest_38_), channel_id=1, source_target_pairs={{0,2},{2,4},{4,6},{6,7},{7,5},{5,3},{3,1},{1,0},{8,10},{10,12},{12... | collective-permute-start | bytes 589832 | tf_op jit(solution)/shard_map/ppermute | solution.py:207
  153.1 5.9 %collective-permute-start.43 = (bf16[96,1024]{1,0:T(8,128)(2,1)S(1)}, bf16[96,1024]{1,0:T(8,128)(2,1)S(1)}, u32[]{:S(2)}, u32[]{:S(2)}) collective-permute-start(bf16[96,1024]{1,0:T(8,128)(2,1)S(1)} %collective-permute-done.39.rest_39_), channel_id=1, source_target_pairs={{2,0},{4,2},{6,4},{7,6},{5,7},{3,5},{1,3},{0,1},{10,8},{12,10},{14... | collective-permute-start | bytes 589832 | tf_op jit(solution)/shard_map/ppermute | solution.py:207
  154.8 6.7 %collective-permute-start.44 = (bf16[96,1024]{1,0:T(8,128)(2,1)S(1)}, bf16[96,1024]{1,0:T(8,128)(2,1)}, u32[]{:S(2)}, u32[]{:S(2)}) collective-permute-start(bf16[96,1024]{1,0:T(8,128)(2,1)S(1)} %collective-permute-done.40.rest_40_), channel_id=1, source_target_pairs={{0,2},{2,4},{4,6},{6,7},{7,5},{5,3},{3,1},{1,0},{8,10},{10,12},{12... | collective-permute-start | bytes 589832 | tf_op jit(solution)/shard_map/ppermute | solution.py:207
  157.3 6.0 %collective-permute-start.45 = (bf16[96,1024]{1,0:T(8,128)(2,1)S(1)}, bf16[96,1024]{1,0:T(8,128)(2,1)}, u32[]{:S(2)}, u32[]{:S(2)}) collective-permute-start(bf16[96,1024]{1,0:T(8,128)(2,1)S(1)} %collective-permute-done.41.rest_41_), channel_id=1, source_target_pairs={{2,0},{4,2},{6,4},{7,6},{5,7},{3,5},{1,3},{0,1},{10,8},{12,10},{14... | collective-permute-start | bytes 589832 | tf_op jit(solution)/shard_map/ppermute | solution.py:207
  159.0 6.8 %collective-permute-start.46 = (bf16[96,1024]{1,0:T(8,128)(2,1)S(1)}, bf16[96,1024]{1,0:T(8,128)(2,1)}, u32[]{:S(2)}, u32[]{:S(2)}) collective-permute-start(bf16[96,1024]{1,0:T(8,128)(2,1)S(1)} %collective-permute-done.42.rest_42_), channel_id=1, source_target_pairs={{0,2},{2,4},{4,6},{6,7},{7,5},{5,3},{3,1},{1,0},{8,10},{10,12},{12... | collective-permute-start | bytes 589832 | tf_op jit(solution)/shard_map/ppermute | solution.py:207
  161.5 5.9 %collective-permute-start.47 = (bf16[96,1024]{1,0:T(8,128)(2,1)S(1)}, bf16[96,1024]{1,0:T(8,128)(2,1)}, u32[]{:S(2)}, u32[]{:S(2)}) collective-permute-start(bf16[96,1024]{1,0:T(8,128)(2,1)S(1)} %collective-permute-done.43.rest_43_), channel_id=1, source_target_pairs={{2,0},{4,2},{6,4},{7,6},{5,7},{3,5},{1,3},{0,1},{10,8},{12,10},{14... | collective-permute-start | bytes 589832 | tf_op jit(solution)/shard_map/ppermute | solution.py:207
  163.3 7.7 %collective-permute-start.48 = (bf16[96,1024]{1,0:T(8,128)(2,1)}, bf16[96,1024]{1,0:T(8,128)(2,1)}, u32[]{:S(2)}, u32[]{:S(2)}) collective-permute-start(bf16[96,1024]{1,0:T(8,128)(2,1)} %collective-permute-done.44.rest_44_), channel_id=1, source_target_pairs={{0,2},{2,4},{4,6},{6,7},{7,5},{5,3},{3,1},{1,0},{8,10},{10,12},{12... | collective-permute-start | bytes 589832 | tf_op jit(solution)/shard_map/ppermute | solution.py:207
  165.9 6.0 %collective-permute-start.49 = (bf16[96,1024]{1,0:T(8,128)(2,1)}, bf16[96,1024]{1,0:T(8,128)(2,1)}, u32[]{:S(2)}, u32[]{:S(2)}) collective-permute-start(bf16[96,1024]{1,0:T(8,128)(2,1)} %collective-permute-done.45.rest_45_), channel_id=1, source_target_pairs={{2,0},{4,2},{6,4},{7,6},{5,7},{3,5},{1,3},{0,1},{10,8},{12,10},{14... | collective-permute-start | bytes 589832 | tf_op jit(solution)/shard_map/ppermute | solution.py:207
  167.5 6.8 %collective-permute-start.50 = (bf16[96,1024]{1,0:T(8,128)(2,1)}, bf16[96,1024]{1,0:T(8,128)(2,1)}, u32[]{:S(2)}, u32[]{:S(2)}) collective-permute-start(bf16[96,1024]{1,0:T(8,128)(2,1)} %collective-permute-done.46.rest_46_), channel_id=1, source_target_pairs={{0,2},{2,4},{4,6},{6,7},{7,5},{5,3},{3,1},{1,0},{8,10},{10,12},{12... | collective-permute-start | bytes 589832 | tf_op jit(solution)/shard_map/ppermute | solution.py:207
  170.1 6.0 %collective-permute-start.51 = (bf16[96,1024]{1,0:T(8,128)(2,1)}, bf16[96,1024]{1,0:T(8,128)(2,1)}, u32[]{:S(2)}, u32[]{:S(2)}) collective-permute-start(bf16[96,1024]{1,0:T(8,128)(2,1)} %collective-permute-done.47.rest_47_), channel_id=1, source_target_pairs={{2,0},{4,2},{6,4},{7,6},{5,7},{3,5},{1,3},{0,1},{10,8},{12,10},{14... | collective-permute-start | bytes 589832 | tf_op jit(solution)/shard_map/ppermute | solution.py:207
  171.9 8.1 %collective-permute-start.52 = (bf16[96,1024]{1,0:T(8,128)(2,1)}, bf16[96,1024]{1,0:T(8,128)(2,1)S(1)}, u32[]{:S(2)}, u32[]{:S(2)}) collective-permute-start(bf16[96,1024]{1,0:T(8,128)(2,1)} %collective-permute-done.48.rest_48_), channel_id=1, source_target_pairs={{0,2},{2,4},{4,6},{6,7},{7,5},{5,3},{3,1},{1,0},{8,10},{10,12},{12... | collective-permute-start | bytes 589832 | tf_op jit(solution)/shard_map/ppermute | solution.py:207
  174.3 5.9 %collective-permute-start.53 = (bf16[96,1024]{1,0:T(8,128)(2,1)}, bf16[96,1024]{1,0:T(8,128)(2,1)S(1)}, u32[]{:S(2)}, u32[]{:S(2)}) collective-permute-start(bf16[96,1024]{1,0:T(8,128)(2,1)} %collective-permute-done.49.rest_49_), channel_id=1, source_target_pairs={{2,0},{4,2},{6,4},{7,6},{5,7},{3,5},{1,3},{0,1},{10,8},{12,10},{14... | collective-permute-start | bytes 589832 | tf_op jit(solution)/shard_map/ppermute | solution.py:207
  176.1 6.2 %collective-permute-start.54 = (bf16[96,1024]{1,0:T(8,128)(2,1)}, bf16[96,1024]{1,0:T(8,128)(2,1)}, u32[]{:S(2)}, u32[]{:S(2)}) collective-permute-start(bf16[96,1024]{1,0:T(8,128)(2,1)} %collective-permute-done.50.rest_50_), channel_id=1, source_target_pairs={{0,2},{2,4},{4,6},{6,7},{7,5},{5,3},{3,1},{1,0},{8,10},{10,12},{12... | collective-permute-start | bytes 589832 | tf_op jit(solution)/shard_map/ppermute | solution.py:207
  178.5 6.0 %collective-permute-start.55 = (bf16[96,1024]{1,0:T(8,128)(2,1)}, bf16[96,1024]{1,0:T(8,128)(2,1)}, u32[]{:S(2)}, u32[]{:S(2)}) collective-permute-start(bf16[96,1024]{1,0:T(8,128)(2,1)} %collective-permute-done.51.rest_51_), channel_id=1, source_target_pairs={{2,0},{4,2},{6,4},{7,6},{5,7},{3,5},{1,3},{0,1},{10,8},{12,10},{14... | collective-permute-start | bytes 589832 | tf_op jit(solution)/shard_map/ppermute | solution.py:207
  (48 other events, 896.5 us)

commit v4 on v3

--- a/solution.py
+++ b/solution.py
@@ -36,6 +36,25 @@
     return (jax.nn.silu(pre[:, :hidden_units]) * pre[:, hidden_units:]).astype(jnp.bfloat16)
 
 
+def both_ways(n, chunks, lag):
+    return min(chunks, (n - 1 - n // 2) * lag // 2)
+
+
+def order_of(n, chunks, lag):
+    single = chunks - both_ways(n, chunks, lag)
+    shared = [(lane, c) for c in range(single, chunks) for lane in range(2)]
+    return [[(way, c) for c in range(single)] + shared for way in range(2)]
+
+
+def arrivals(n, chunks, lag, h):
+    single = chunks - both_ways(n, chunks, lag)
+    nearer = 0 if h <= n // 2 else 1
+    for way, turns in enumerate(order_of(n, chunks, lag)):
+        for turn, (lane, c) in enumerate(turns):
+            if c < single or way == nearer:
+                yield lane, c, way, turn + lag * ((h, n - h)[way] - 1)
+
+
 def hot_kernel(n, lag, hops, x, weight, gate_up, down, *rest):
     came = rest[:-5]
     out, gate_all, down_all, gate_sems, down_sem = rest[-5:]
@@ -53,22 +72,23 @@
                 pltpu.make_async_copy(gate_up.at[part, :], gate_all.at[part, :], gate_sems.at[way]).start()
             pltpu.make_async_copy(down, down_all, down_sem).start()
 
-        for way in range(2):
-            for h in range(1, n):
-
-                @pl.when(hops[way] == h)
-                def _(way=way, h=h):
-                    for c, at in enumerate(starts):
-                        source = came[2 * (c + lag * (h - 1)) + way]
-                        low = c * rows - at
-                        gate = min(max(middle - at, low), rows)
-                        if low < gate:
-                            target = gate_all.at[pl.ds(way * middle + at + low, gate - low), :]
-                            part = source.at[pl.ds(low, gate - low), :]
-                            pltpu.make_async_copy(part, target, gate_sems.at[way]).start()
-                        if gate < rows:
-                            target = down_all.at[pl.ds(at + gate - middle, rows - gate), pl.ds(way * half, half)]
-                            pltpu.make_async_copy(source.at[pl.ds(gate, rows - gate), :], target, down_sem).start()
+        for h in range(1, n):
+
+            @pl.when(hops[0] == h)
+            def _(h=h):
+                for lane, c, way, t in arrivals(n, len(starts), lag, h):
+                    source = came[2 * t + way]
+                    at = starts[c]
+                    low = c * rows - at
+                    gate = min(max(middle - at, low), rows)
+                    if low < gate:
+                        target = gate_all.at[pl.ds(lane * middle + at + low, gate - low), :]
+                        part = source.at[pl.ds(low, gate - low), :]
+                        pltpu.make_async_copy(part, target, gate_sems.at[lane]).start()
+                    low = max(low, gate)
+                    if low < rows:
+                        target = down_all.at[pl.ds(at + low - middle, rows - low), pl.ds(lane * half, half)]
+                        pltpu.make_async_copy(source.at[pl.ds(low, rows - low), :], target, down_sem).start()
 
     pre = 0.0
     for way in range(2):
@@ -177,19 +197,21 @@
         [(order[(i + 1) % n], order[i]) for i in range(n)],
     )
     weight = res_weight[:, None]
-    steps = chunks + (n - 2) * lag
+    turns = order_of(n, chunks, lag)
+    sends = len(turns[0])
+    steps = 1 + max(t for h in range(1, n) for _, _, _, t in arrivals(n, chunks, lag, h))
     came, last = [], None
     for t in range(steps):
-        mine = tuple(own[i][t] for i in range(2)) if t < chunks else None
+        mine = tuple(own[lane][c] for lane, c in (turns[0][t], turns[1][t])) if t < sends else None
         if t >= lag:
             got = came[t - lag]
             if t == lag + 1:
                 got, hops, weight = join(got, hops, weight)
-            elif t == steps * 2 // 7:
+            elif t == steps // 3:
                 got, cold = join(got, cold)
                 pre = jnp.dot(cold, gate_up, preferred_element_type=jnp.float32)
                 cold = jnp.dot(swiglu(pre, hidden_units), down, preferred_element_type=jnp.float32).astype(jnp.bfloat16)
-            elif t == steps * 2 // 7 + 1:
+            elif t == steps // 3 + 1:
                 got, cold = join(got, cold)
                 cold = lax.all_to_all(cold, ("ep", "shadow"), 0, 0, tiled=True)
             elif t == steps - 2:
@@ -202,7 +224,7 @@
                     + jnp.dot(low, cold, preferred_element_type=jnp.float32)
                 ).astype(jnp.bfloat16)
             got, _ = join(got, last)
-            mine = tuple(jnp.where(me == root, m, g) for m, g in zip(mine, got)) if t < chunks else got
+            mine = tuple(jnp.where(me == root, m, g) for m, g in zip(mine, got)) if t < sends else got
         mine = last = join(*mine)
         came.append(tuple(lax.ppermute(mine[i], "shadow", ways[i]) for i in range(2)))
     came, cold = join(came, cold)

time: 196 us -> 186 us (0.949)
  starting transfers between devices: 90.6 us -> 77.6 us
  other arithmetic: 13.5 us -> 19.5 us
  waiting for transfers between devices: 58.3 us -> 55.2 us
    ppermute x56 -> x50, starting transfers between devices: 79.5 us -> 66.5 us  [body(): lax.ppermute(mine[i], 'shadow', ways[i])]
    select_n x14 -> x17, other arithmetic: 12.9 us -> 18.9 us  [body(): jnp.where(me == root, m, g)]
    ppermute x56 -> x50, waiting for transfers between devices: 58.3 us -> 55.2 us  [body(): lax.ppermute(mine[i], 'shadow', ways[i])]
  transfers between devices with their start and end apart: 58 -> 52, of which waited for: 24 -> 25; matrix products, arithmetic and copies ran while one was open for 14% -> 18% of each run, Pallas kernels for 0% -> 0%
where the time goes in v4:
time: 186 us
  starting transfers between devices  77.6 us (42%)
  waiting for transfers between devices  55.2 us (30%)
  other arithmetic  19.5 us (10%)
  Pallas kernels  10.8 us (6%)
  local copies, waits for them, and re-layouts  9.04 us (5%)
  matrix products  8.28 us (4%)
  between operations  5.24 us (3%)
    ppermute x50, starting transfers between devices, body(): lax.ppermute(mine[i], 'shadow', ways[i])  66.5 us
    ppermute x50, waiting for transfers between devices, body(): lax.ppermute(mine[i], 'shadow', ways[i])  55.2 us
    select_n x17, other arithmetic, body(): jnp.where(me == root, m, g)  18.9 us
    pallas_call x1, Pallas kernels, hot_expert(): pl.pallas_call(functools.partial(hot_kernel, n, lag), grid=(BLOCKS,), out...  10.8 us
    all_to_all x1, starting transfers between devices, body(): cold = lax.all_to_all(outgoing, ('ep', 'shadow'), 0, 0, tiled=True)  6.38 us
    all_to_all x1, starting transfers between devices, body(): cold = lax.all_to_all(cold, ('ep', 'shadow'), 0, 0, tiled=True)  4.67 us
    slice x3, local copies, waits for them, and re-layouts, cut(): out.append(part[low:high])  4.54 us
  transfers between devices with their start and end apart: 52, of which 25 were waited for; matrix products, arithmetic and copies ran while one was open for 18% of the time, Pallas kernels for 0%

profile of v4, /device:TPU:0, one launch (start us, length us, event | category | flops | bytes accessed | tf_op | source)
XLA Modules:
  0.0 185.7 jit_solution(10625513626425196146)
XLA Ops:
  0.7 2.2 %slice_bitcast_fusion = (bf16[96,1024]{1,0:T(8,128)(2,1)}, bf16[96,1024]{1,0:T(8,128)(2,1)}, bf16[96,1024]{1,0:T(8,128)(2,1)}, bf16[96,1024]{1,0:T(8,128)(2,1)}) fusion(bf16[1,2048,1024]{2,1,0:T(8,128)(2,1)} %param.15), kind=kLoop, calls=%fused_computation.30 | loop fusion | bytes 1572864 | tf_op jit(solution)/shard_map/slice | solution.py:151
  2.9 3.0 %collective-permute-start = (bf16[96,1024]{1,0:T(8,128)(2,1)}, bf16[96,1024]{1,0:T(8,128)(2,1)}, u32[]{:S(2)}, u32[]{:S(2)}) collective-permute-start(bf16[96,1024]{1,0:T(8,128)(2,1)} %get-tuple-element.162), channel_id=1, source_target_pairs={{0,2},{2,4},{4,6},{6,7},{7,5},{5,3},{3,1},{1,0},{8,10},{10,12},{12... | collective-permute-start | bytes 589832 | tf_op jit(solution)/shard_map/ppermute | solution.py:229
  6.0 2.0 %collective-permute-start.2 = (bf16[96,1024]{1,0:T(8,128)(2,1)}, bf16[96,1024]{1,0:T(8,128)(2,1)}, u32[]{:S(2)}, u32[]{:S(2)}) collective-permute-start(bf16[96,1024]{1,0:T(8,128)(2,1)} %get-tuple-element.166), channel_id=1, source_target_pairs={{0,2},{2,4},{4,6},{6,7},{7,5},{5,3},{3,1},{1,0},{8,10},{10,12},{12... | collective-permute-start | bytes 589832 | tf_op jit(solution)/shard_map/ppermute | solution.py:229
  9.1 1.5 convolution_convert_fusion.1
  10.6 6.4 %all-to-all-start = ((bf16[16,16,2048]{2,1,0:T(8,128)(2,1)}), bf16[16,16,2048]{2,1,0:T(8,128)(2,1)S(1)}, u32[]{:S(2)}, u32[]{:S(2)}) async-start(bf16[16,16,2048]{2,1,0:T(8,128)(2,1)} %bitcast.25), calls=%async_computation | async-start | bytes 2097152 | tf_op jit(solution)/shard_map/all_to_all | solution.py:182
  23.4 1.6 slice_bitcast_fusion.4
  25.7 1.3 bitcast_select_fusion.14
  27.0 2.0 %collective-permute-start.4 = (bf16[96,1024]{1,0:T(8,128)(2,1)S(1)}, bf16[96,1024]{1,0:T(8,128)(2,1)S(1)}, u32[]{:S(2)}, u32[]{:S(2)}) collective-permute-start(bf16[96,1024]{1,0:T(8,128)(2,1)S(1)} %get-tuple-element.170), channel_id=1, source_target_pairs={{0,2},{2,4},{4,6},{6,7},{7,5},{5,3},{3,1},{1,0},{8,10},{10,12},{12... | collective-permute-start | bytes 589832 | tf_op jit(solution)/shard_map/ppermute | solution.py:229
  29.1 1.3 bitcast_select_fusion.12
  30.3 2.0 %collective-permute-start.6 = (bf16[96,1024]{1,0:T(8,128)(2,1)S(1)}, bf16[96,1024]{1,0:T(8,128)(2,1)S(1)}, u32[]{:S(2)}, u32[]{:S(2)}) collective-permute-start(bf16[96,1024]{1,0:T(8,128)(2,1)S(1)} %get-tuple-element.176), channel_id=1, source_target_pairs={{0,2},{2,4},{4,6},{6,7},{7,5},{5,3},{3,1},{1,0},{8,10},{10,12},{12... | collective-permute-start | bytes 589832 | tf_op jit(solution)/shard_map/ppermute | solution.py:229
  32.4 7.2 %collective-permute-done.4.rest_4_ = bf16[96,1024]{1,0:T(8,128)(2,1)S(1)} collective-permute-done((bf16[96,1024]{1,0:T(8,128)(2,1)S(1)}, bf16[96,1024]{1,0:T(8,128)(2,1)S(1)}, u32[]{:S(2)}, u32[]{:S(2)}) %collective-permute-start.4) | collective-permute-done | bytes 196640 | tf_op jit(solution)/shard_map/ppermute | solution.py:229
  39.6 2.7 %collective-permute-done.5.rest_5_ = bf16[96,1024]{1,0:T(8,128)(2,1)S(1)} collective-permute-done((bf16[96,1024]{1,0:T(8,128)(2,1)S(1)}, bf16[96,1024]{1,0:T(8,128)(2,1)S(1)}, u32[]{:S(2)}, u32[]{:S(2)}) %collective-permute-start.5) | collective-permute-done | bytes 196640 | tf_op jit(solution)/shard_map/ppermute | solution.py:229
  42.4 1.2 bitcast_select_fusion.10
  43.5 6.4 %collective-permute-start.8 = (bf16[96,1024]{1,0:T(8,128)(2,1)S(1)}, bf16[96,1024]{1,0:T(8,128)(2,1)S(1)}, u32[]{:S(2)}, u32[]{:S(2)}) collective-permute-start(bf16[96,1024]{1,0:T(8,128)(2,1)S(1)} %get-tuple-element.180), channel_id=1, source_target_pairs={{0,2},{2,4},{4,6},{6,7},{7,5},{5,3},{3,1},{1,0},{8,10},{10,12},{12... | collective-permute-start | bytes 589832 | tf_op jit(solution)/shard_map/ppermute | solution.py:229
  50.0 1.2 bitcast_select_fusion.8
  51.2 2.5 %collective-permute-start.10 = (bf16[96,1024]{1,0:T(8,128)(2,1)S(1)}, bf16[96,1024]{1,0:T(8,128)(2,1)S(1)}, u32[]{:S(2)}, u32[]{:S(2)}) collective-permute-start(bf16[96,1024]{1,0:T(8,128)(2,1)S(1)} %get-tuple-element.184), channel_id=1, source_target_pairs={{0,2},{2,4},{4,6},{6,7},{7,5},{5,3},{3,1},{1,0},{8,10},{10,12},{12... | collective-permute-start | bytes 589832 | tf_op jit(solution)/shard_map/ppermute | solution.py:229
  53.7 1.9 %collective-permute-done.9.rest_9_ = bf16[96,1024]{1,0:T(8,128)(2,1)S(1)} collective-permute-done((bf16[96,1024]{1,0:T(8,128)(2,1)S(1)}, bf16[96,1024]{1,0:T(8,128)(2,1)S(1)}, u32[]{:S(2)}, u32[]{:S(2)}) %collective-permute-start.9) | collective-permute-done | bytes 196640 | tf_op jit(solution)/shard_map/ppermute | solution.py:229
  55.7 1.2 bitcast_select_fusion.6
  56.8 1.1 collective-permute-start.12
  58.9 1.7 collective-permute-done.11.rest_11_
  60.6 1.9 %bitcast_select_fusion.4 = (bf16[96,1024]{1,0:T(8,128)(2,1)}, bf16[96,1024]{1,0:T(8,128)(2,1)}) fusion(bf16[96,1024]{1,0:T(8,128)(2,1)S(1)} %collective-permute-done.11.rest_11_, bf16[1,2048,1024]{2,1,0:T(8,128)(2,1)} %param.15, pred[]{:T(512)S(6)} %eq.21, bf16[96,1024]{1,0:T(8,128)(2,1)S(1)} %collective-permute-done.10.rest_10_), kind=kLoop, calls=%fused_computation.18 | loop fusion | flops 196608 | bytes 1179649 | tf_op jit(solution)/shard_map/jit(_where)/select_n | solution.py:227
  63.5 1.0 collective-permute-start.15
  65.3 2.0 %bitcast_select_fusion.2 = (bf16[96,1024]{1,0:T(8,128)(2,1)}, bf16[96,1024]{1,0:T(8,128)(2,1)}) fusion(bf16[96,1024]{1,0:T(8,128)(2,1)} %collective-permute-done.13.rest_13_, bf16[1,2048,1024]{2,1,0:T(8,128)(2,1)} %param.15, pred[]{:T(512)S(6)} %eq.21, bf16[96,1024]{1,0:T(8,128)(2,1)} %copy-done.22), kind=kLoop, calls=%fused_computation.16 | loop fusion | flops 196608 | bytes 1179649 | tf_op jit(solution)/shard_map/jit(_where)/select_n | solution.py:227
  68.3 1.0 collective-permute-start.17
  69.3 3.4 %fusion.31 = f32[256,1024]{1,0:T(8,128)S(1)} fusion(bf16[256,2048]{1,0:T(8,128)(2,1)S(1)} %bitcast.84, bf16[1,2048,1024]{2,1,0:T(8,128)(2,1)} %param.15), kind=kOutput, calls=%fused_computation.89 | convolution fusion | flops 1073741824 | bytes 6291456 | tf_op jit(solution)/shard_map/dot_general | solution.py:212
  72.8 1.7 convolution_convert_fusion
  74.5 4.7 %all-to-all-start.1 = ((bf16[16,16,2048]{2,1,0:T(8,128)(2,1)}), bf16[16,16,2048]{2,1,0:T(8,128)(2,1)S(1)}, u32[]{:S(2)}, u32[]{:S(2)}) async-start(bf16[16,16,2048]{2,1,0:T(8,128)(2,1)} %bitcast.83), calls=%async_computation.1 | async-start | bytes 2097152 | tf_op jit(solution)/shard_map/all_to_all | solution.py:216
  79.2 1.3 bitcast_select_fusion
  80.5 2.0 %collective-permute-start.18 = (bf16[96,1024]{1,0:T(8,128)(2,1)S(1)}, bf16[96,1024]{1,0:T(8,128)(2,1)S(1)}, u32[]{:S(2)}, u32[]{:S(2)}) collective-permute-start(bf16[96,1024]{1,0:T(8,128)(2,1)S(1)} %get-tuple-element.205), channel_id=1, source_target_pairs={{0,2},{2,4},{4,6},{6,7},{7,5},{5,3},{3,1},{1,0},{8,10},{10,12},{12... | collective-permute-start | bytes 589832 | tf_op jit(solution)/shard_map/ppermute | solution.py:229
  82.5 1.3 maximum_select_fusion
  83.8 2.0 %collective-permute-start.20 = (bf16[96,1024]{1,0:T(8,128)(2,1)S(1)}, bf16[96,1024]{1,0:T(8,128)(2,1)S(1)}, u32[]{:S(2)}, u32[]{:S(2)}) collective-permute-start(bf16[96,1024]{1,0:T(8,128)(2,1)S(1)} %get-tuple-element.209), channel_id=1, source_target_pairs={{0,2},{2,4},{4,6},{6,7},{7,5},{5,3},{3,1},{1,0},{8,10},{10,12},{12... | collective-permute-start | bytes 589832 | tf_op jit(solution)/shard_map/ppermute | solution.py:229
  85.9 15.9 %collective-permute-done.18.rest_18_ = bf16[96,1024]{1,0:T(8,128)(2,1)S(1)} collective-permute-done((bf16[96,1024]{1,0:T(8,128)(2,1)S(1)}, bf16[96,1024]{1,0:T(8,128)(2,1)S(1)}, u32[]{:S(2)}, u32[]{:S(2)}) %collective-permute-start.18) | collective-permute-done | bytes 196640 | tf_op jit(solution)/shard_map/ppermute | solution.py:229
  102.5 8.5 %collective-permute-start.22 = (bf16[96,1024]{1,0:T(8,128)(2,1)S(1)}, bf16[96,1024]{1,0:T(8,128)(2,1)S(1)}, u32[]{:S(2)}, u32[]{:S(2)}) collective-permute-start(bf16[96,1024]{1,0:T(8,128)(2,1)S(1)} %get-tuple-element.213), channel_id=1, source_target_pairs={{0,2},{2,4},{4,6},{6,7},{7,5},{5,3},{3,1},{1,0},{8,10},{10,12},{12... | collective-permute-start | bytes 589832 | tf_op jit(solution)/shard_map/ppermute | solution.py:229
  111.2 4.1 %collective-permute-start.24 = (bf16[96,1024]{1,0:T(8,128)(2,1)S(1)}, bf16[96,1024]{1,0:T(8,128)(2,1)S(1)}, u32[]{:S(2)}, u32[]{:S(2)}) collective-permute-start(bf16[96,1024]{1,0:T(8,128)(2,1)S(1)} %get-tuple-element.217), channel_id=1, source_target_pairs={{0,2},{2,4},{4,6},{6,7},{7,5},{5,3},{3,1},{1,0},{8,10},{10,12},{12... | collective-permute-start | bytes 589832 | tf_op jit(solution)/shard_map/ppermute | solution.py:229
  115.4 1.4 collective-permute-done.23.rest_23_
  116.7 1.1 broadcast_select_fusion.10
  117.8 2.7 %collective-permute-start.26 = (bf16[96,1024]{1,0:T(8,128)(2,1)S(1)}, bf16[96,1024]{1,0:T(8,128)(2,1)S(1)}, u32[]{:S(2)}, u32[]{:S(2)}) collective-permute-start(bf16[96,1024]{1,0:T(8,128)(2,1)S(1)} %get-tuple-element.221), channel_id=1, source_target_pairs={{0,2},{2,4},{4,6},{6,7},{7,5},{5,3},{3,1},{1,0},{8,10},{10,12},{12... | collective-permute-start | bytes 589832 | tf_op jit(solution)/shard_map/ppermute | solution.py:229
  121.0 1.0 broadcast_select_fusion.8
  122.1 2.1 %collective-permute-start.28 = (bf16[96,1024]{1,0:T(8,128)(2,1)S(1)}, bf16[96,1024]{1,0:T(8,128)(2,1)S(1)}, u32[]{:S(2)}, u32[]{:S(2)}) collective-permute-start(bf16[96,1024]{1,0:T(8,128)(2,1)S(1)} %get-tuple-element.225), channel_id=1, source_target_pairs={{0,2},{2,4},{4,6},{6,7},{7,5},{5,3},{3,1},{1,0},{8,10},{10,12},{12... | collective-permute-start | bytes 589832 | tf_op jit(solution)/shard_map/ppermute | solution.py:229
  124.2 2.0 %collective-permute-done.27.rest_27_ = bf16[96,1024]{1,0:T(8,128)(2,1)S(1)} collective-permute-done((bf16[96,1024]{1,0:T(8,128)(2,1)S(1)}, bf16[96,1024]{1,0:T(8,128)(2,1)S(1)}, u32[]{:S(2)}, u32[]{:S(2)}) %collective-permute-start.27) | collective-permute-done | bytes 196640 | tf_op jit(solution)/shard_map/ppermute | solution.py:229
  126.2 1.0 broadcast_select_fusion.6
  127.2 2.3 %collective-permute-start.30 = (bf16[96,1024]{1,0:T(8,128)(2,1)S(1)}, bf16[96,1024]{1,0:T(8,128)(2,1)S(1)}, u32[]{:S(2)}, u32[]{:S(2)}) collective-permute-start(bf16[96,1024]{1,0:T(8,128)(2,1)S(1)} %get-tuple-element.229), channel_id=1, source_target_pairs={{0,2},{2,4},{4,6},{6,7},{7,5},{5,3},{3,1},{1,0},{8,10},{10,12},{12... | collective-permute-start | bytes 589832 | tf_op jit(solution)/shard_map/ppermute | solution.py:229
  129.5 1.1 collective-permute-done.29.rest_29_
  131.7 2.1 %collective-permute-start.32 = (bf16[96,1024]{1,0:T(8,128)(2,1)S(1)}, bf16[96,1024]{1,0:T(8,128)(2,1)S(1)}, u32[]{:S(2)}, u32[]{:S(2)}) collective-permute-start(bf16[96,1024]{1,0:T(8,128)(2,1)S(1)} %get-tuple-element.233), channel_id=1, source_target_pairs={{0,2},{2,4},{4,6},{6,7},{7,5},{5,3},{3,1},{1,0},{8,10},{10,12},{12... | collective-permute-start | bytes 589832 | tf_op jit(solution)/shard_map/ppermute | solution.py:229
  133.8 1.5 collective-permute-done.31.rest_31_
  136.3 1.9 %collective-permute-start.34 = (bf16[96,1024]{1,0:T(8,128)(2,1)S(1)}, bf16[96,1024]{1,0:T(8,128)(2,1)S(1)}, u32[]{:S(2)}, u32[]{:S(2)}) collective-permute-start(bf16[96,1024]{1,0:T(8,128)(2,1)S(1)} %get-tuple-element.237), channel_id=1, source_target_pairs={{0,2},{2,4},{4,6},{6,7},{7,5},{5,3},{3,1},{1,0},{8,10},{10,12},{12... | collective-permute-start | bytes 589832 | tf_op jit(solution)/shard_map/ppermute | solution.py:229
  138.5 1.9 %collective-permute-done.33.rest_33_ = bf16[96,1024]{1,0:T(8,128)(2,1)S(1)} collective-permute-done((bf16[96,1024]{1,0:T(8,128)(2,1)S(1)}, bf16[96,1024]{1,0:T(8,128)(2,1)S(1)}, u32[]{:S(2)}, u32[]{:S(2)}) %collective-permute-start.33) | collective-permute-done | bytes 196640 | tf_op jit(solution)/shard_map/ppermute | solution.py:229
  141.5 1.5 collective-permute-start.36
  143.6 1.5 collective-permute-done.35.rest_35_
  145.1 1.1 collective-permute-start.38
  147.1 1.3 collective-permute-done.36.rest_36_
  148.4 2.4 %collective-permute-done.37.rest_37_ = bf16[96,1024]{1,0:T(8,128)(2,1)S(1)} collective-permute-done((bf16[96,1024]{1,0:T(8,128)(2,1)S(1)}, bf16[96,1024]{1,0:T(8,128)(2,1)S(1)}, u32[]{:S(2)}, u32[]{:S(2)}) %collective-permute-start.37) | collective-permute-done | bytes 196640 | tf_op jit(solution)/shard_map/ppermute | solution.py:229
  151.4 1.5 collective-permute-start.41
  153.0 2.2 %collective-permute-done.39.rest_39_ = bf16[96,1024]{1,0:T(8,128)(2,1)} collective-permute-done((bf16[96,1024]{1,0:T(8,128)(2,1)S(1)}, bf16[96,1024]{1,0:T(8,128)(2,1)}, u32[]{:S(2)}, u32[]{:S(2)}) %collective-permute-start.39) | collective-permute-done | bytes 196640 | tf_op jit(solution)/shard_map/ppermute | solution.py:229
  155.7 1.5 collective-permute-start.43
  157.5 1.9 %collective-permute-done.41.rest_41_ = bf16[96,1024]{1,0:T(8,128)(2,1)} collective-permute-done((bf16[96,1024]{1,0:T(8,128)(2,1)S(1)}, bf16[96,1024]{1,0:T(8,128)(2,1)}, u32[]{:S(2)}, u32[]{:S(2)}) %collective-permute-start.41) | collective-permute-done | bytes 196640 | tf_op jit(solution)/shard_map/ppermute | solution.py:229
  159.9 1.5 collective-permute-start.45
  162.4 1.4 collective-permute-done.43.rest_43_
  164.5 1.4 collective-permute-start.47
  166.2 1.9 %collective-permute-done.45.rest_45_ = bf16[96,1024]{1,0:T(8,128)(2,1)} collective-permute-done((bf16[96,1024]{1,0:T(8,128)(2,1)}, bf16[96,1024]{1,0:T(8,128)(2,1)}, u32[]{:S(2)}, u32[]{:S(2)}) %collective-permute-start.45) | collective-permute-done | bytes 196640 | tf_op jit(solution)/shard_map/ppermute | solution.py:229
  168.7 1.4 collective-permute-start.49
  170.5 1.0 fusion
  171.6 2.5 %collective-permute-done.48.rest_48_ = bf16[96,1024]{1,0:T(8,128)(2,1)} collective-permute-done((bf16[96,1024]{1,0:T(8,128)(2,1)}, bf16[96,1024]{1,0:T(8,128)(2,1)}, u32[]{:S(2)}, u32[]{:S(2)}) %collective-permute-start.48) | collective-permute-done | bytes 196640 | tf_op jit(solution)/shard_map/ppermute | solution.py:229
  174.7 10.8 %shard_map.104 = bf16[768,2048]{1,0:T(8,128)(2,1)} custom-call(s32[2]{0:T(128)} %pad_add_fusion.hops, bf16[768,2048]{1,0:T(8,128)(2,1)} %x.1, f32[768,1]{1,0:T(8,128)} %copy.11.weight, bf16[2048,1024]{1,0:T(8,128)(2,1)} %bitcast.70, bf16[512,2048]{1,0:T(8,128)(2,1)} %bitcast.79, bf16[96,1024]{1,0:T(8,128)(2,1)} %collective-permute-done.2.rest_0_, ...), custom_call_target="tpu_custom_call" | custom-call | flops 4831838208 | bytes 20971520 | tf_op jit(solution)/shard_map/pallas_call | solution.py:116
  (176 shorter events, 20.3 us)
Async XLA Ops:
  2.9 22.8 %collective-permute-start = (bf16[96,1024]{1,0:T(8,128)(2,1)}, bf16[96,1024]{1,0:T(8,128)(2,1)}, u32[]{:S(2)}, u32[]{:S(2)}) collective-permute-start(bf16[96,1024]{1,0:T(8,128)(2,1)} %get-tuple-element.162), channel_id=1, source_target_pairs={{0,2},{2,4},{4,6},{6,7},{7,5},{5,3},{3,1},{1,0},{8,10},{10,12},{12... | collective-permute-start | bytes 589832 | tf_op jit(solution)/shard_map/ppermute | solution.py:229
  6.0 19.8 %collective-permute-start.1 = (bf16[96,1024]{1,0:T(8,128)(2,1)}, bf16[96,1024]{1,0:T(8,128)(2,1)}, u32[]{:S(2)}, u32[]{:S(2)}) collective-permute-start(bf16[96,1024]{1,0:T(8,128)(2,1)} %get-tuple-element.163), channel_id=1, source_target_pairs={{2,0},{4,2},{6,4},{7,6},{5,7},{3,5},{1,3},{0,1},{10,8},{12,10},{14... | collective-permute-start | bytes 589832 | tf_op jit(solution)/shard_map/ppermute | solution.py:229
  6.0 19.8 %collective-permute-start.2 = (bf16[96,1024]{1,0:T(8,128)(2,1)}, bf16[96,1024]{1,0:T(8,128)(2,1)}, u32[]{:S(2)}, u32[]{:S(2)}) collective-permute-start(bf16[96,1024]{1,0:T(8,128)(2,1)} %get-tuple-element.166), channel_id=1, source_target_pairs={{0,2},{2,4},{4,6},{6,7},{7,5},{5,3},{3,1},{1,0},{8,10},{10,12},{12... | collective-permute-start | bytes 589832 | tf_op jit(solution)/shard_map/ppermute | solution.py:229
  8.0 17.7 %collective-permute-start.3 = (bf16[96,1024]{1,0:T(8,128)(2,1)}, bf16[96,1024]{1,0:T(8,128)(2,1)}, u32[]{:S(2)}, u32[]{:S(2)}) collective-permute-start(bf16[96,1024]{1,0:T(8,128)(2,1)} %get-tuple-element.167), channel_id=1, source_target_pairs={{2,0},{4,2},{6,4},{7,6},{5,7},{3,5},{1,3},{0,1},{10,8},{12,10},{14... | collective-permute-start | bytes 589832 | tf_op jit(solution)/shard_map/ppermute | solution.py:229
  10.6 54.7 %all-to-all-start = ((bf16[16,16,2048]{2,1,0:T(8,128)(2,1)}), bf16[16,16,2048]{2,1,0:T(8,128)(2,1)S(1)}, u32[]{:S(2)}, u32[]{:S(2)}) async-start(bf16[16,16,2048]{2,1,0:T(8,128)(2,1)} %bitcast.25), calls=%async_computation | async-start | bytes 2097152 | tf_op jit(solution)/shard_map/all_to_all | solution.py:182
  27.0 12.6 %collective-permute-start.4 = (bf16[96,1024]{1,0:T(8,128)(2,1)S(1)}, bf16[96,1024]{1,0:T(8,128)(2,1)S(1)}, u32[]{:S(2)}, u32[]{:S(2)}) collective-permute-start(bf16[96,1024]{1,0:T(8,128)(2,1)S(1)} %get-tuple-element.170), channel_id=1, source_target_pairs={{0,2},{2,4},{4,6},{6,7},{7,5},{5,3},{3,1},{1,0},{8,10},{10,12},{12... | collective-permute-start | bytes 589832 | tf_op jit(solution)/shard_map/ppermute | solution.py:229
  29.0 13.4 %collective-permute-start.5 = (bf16[96,1024]{1,0:T(8,128)(2,1)S(1)}, bf16[96,1024]{1,0:T(8,128)(2,1)S(1)}, u32[]{:S(2)}, u32[]{:S(2)}) collective-permute-start(bf16[96,1024]{1,0:T(8,128)(2,1)S(1)} %get-tuple-element.171), channel_id=1, source_target_pairs={{2,0},{4,2},{6,4},{7,6},{5,7},{3,5},{1,3},{0,1},{10,8},{12,10},{14... | collective-permute-start | bytes 589832 | tf_op jit(solution)/shard_map/ppermute | solution.py:229
  30.3 19.6 %collective-permute-start.6 = (bf16[96,1024]{1,0:T(8,128)(2,1)S(1)}, bf16[96,1024]{1,0:T(8,128)(2,1)S(1)}, u32[]{:S(2)}, u32[]{:S(2)}) collective-permute-start(bf16[96,1024]{1,0:T(8,128)(2,1)S(1)} %get-tuple-element.176), channel_id=1, source_target_pairs={{0,2},{2,4},{4,6},{6,7},{7,5},{5,3},{3,1},{1,0},{8,10},{10,12},{12... | collective-permute-start | bytes 589832 | tf_op jit(solution)/shard_map/ppermute | solution.py:229
  32.3 17.7 %collective-permute-start.7 = (bf16[96,1024]{1,0:T(8,128)(2,1)S(1)}, bf16[96,1024]{1,0:T(8,128)(2,1)S(1)}, u32[]{:S(2)}, u32[]{:S(2)}) collective-permute-start(bf16[96,1024]{1,0:T(8,128)(2,1)S(1)} %get-tuple-element.177), channel_id=1, source_target_pairs={{2,0},{4,2},{6,4},{7,6},{5,7},{3,5},{1,3},{0,1},{10,8},{12,10},{14... | collective-permute-start | bytes 589832 | tf_op jit(solution)/shard_map/ppermute | solution.py:229
  43.5 10.2 %collective-permute-start.8 = (bf16[96,1024]{1,0:T(8,128)(2,1)S(1)}, bf16[96,1024]{1,0:T(8,128)(2,1)S(1)}, u32[]{:S(2)}, u32[]{:S(2)}) collective-permute-start(bf16[96,1024]{1,0:T(8,128)(2,1)S(1)} %get-tuple-element.180), channel_id=1, source_target_pairs={{0,2},{2,4},{4,6},{6,7},{7,5},{5,3},{3,1},{1,0},{8,10},{10,12},{12... | collective-permute-start | bytes 589832 | tf_op jit(solution)/shard_map/ppermute | solution.py:229
  50.0 5.7 %collective-permute-start.9 = (bf16[96,1024]{1,0:T(8,128)(2,1)S(1)}, bf16[96,1024]{1,0:T(8,128)(2,1)S(1)}, u32[]{:S(2)}, u32[]{:S(2)}) collective-permute-start(bf16[96,1024]{1,0:T(8,128)(2,1)S(1)} %get-tuple-element.181), channel_id=1, source_target_pairs={{2,0},{4,2},{6,4},{7,6},{5,7},{3,5},{1,3},{0,1},{10,8},{12,10},{14... | collective-permute-start | bytes 589832 | tf_op jit(solution)/shard_map/ppermute | solution.py:229
  51.2 7.7 %collective-permute-start.10 = (bf16[96,1024]{1,0:T(8,128)(2,1)S(1)}, bf16[96,1024]{1,0:T(8,128)(2,1)S(1)}, u32[]{:S(2)}, u32[]{:S(2)}) collective-permute-start(bf16[96,1024]{1,0:T(8,128)(2,1)S(1)} %get-tuple-element.184), channel_id=1, source_target_pairs={{0,2},{2,4},{4,6},{6,7},{7,5},{5,3},{3,1},{1,0},{8,10},{10,12},{12... | collective-permute-start | bytes 589832 | tf_op jit(solution)/shard_map/ppermute | solution.py:229
  53.7 6.9 %collective-permute-start.11 = (bf16[96,1024]{1,0:T(8,128)(2,1)S(1)}, bf16[96,1024]{1,0:T(8,128)(2,1)S(1)}, u32[]{:S(2)}, u32[]{:S(2)}) collective-permute-start(bf16[96,1024]{1,0:T(8,128)(2,1)S(1)} %get-tuple-element.185), channel_id=1, source_target_pairs={{2,0},{4,2},{6,4},{7,6},{5,7},{3,5},{1,3},{0,1},{10,8},{12,10},{14... | collective-permute-start | bytes 589832 | tf_op jit(solution)/shard_map/ppermute | solution.py:229
  56.8 7.7 %collective-permute-start.12 = (bf16[96,1024]{1,0:T(8,128)(2,1)S(1)}, bf16[96,1024]{1,0:T(8,128)(2,1)S(1)}, u32[]{:S(2)}, u32[]{:S(2)}) collective-permute-start(bf16[96,1024]{1,0:T(8,128)(2,1)S(1)} %get-tuple-element.188), channel_id=1, source_target_pairs={{0,2},{2,4},{4,6},{6,7},{7,5},{5,3},{3,1},{1,0},{8,10},{10,12},{12... | collective-permute-start | bytes 589832 | tf_op jit(solution)/shard_map/ppermute | solution.py:229
  57.9 7.4 %collective-permute-start.13 = (bf16[96,1024]{1,0:T(8,128)(2,1)S(1)}, bf16[96,1024]{1,0:T(8,128)(2,1)}, u32[]{:S(2)}, u32[]{:S(2)}) collective-permute-start(bf16[96,1024]{1,0:T(8,128)(2,1)S(1)} %get-tuple-element.189), channel_id=1, source_target_pairs={{2,0},{4,2},{6,4},{7,6},{5,7},{3,5},{1,3},{0,1},{10,8},{12,10},{14... | collective-permute-start | bytes 589832 | tf_op jit(solution)/shard_map/ppermute | solution.py:229
  62.5 12.0 %collective-permute-start.14 = (bf16[96,1024]{1,0:T(8,128)(2,1)}, bf16[96,1024]{1,0:T(8,128)(2,1)}, u32[]{:S(2)}, u32[]{:S(2)}) collective-permute-start(bf16[96,1024]{1,0:T(8,128)(2,1)} %get-tuple-element.192), channel_id=1, source_target_pairs={{0,2},{2,4},{4,6},{6,7},{7,5},{5,3},{3,1},{1,0},{8,10},{10,12},{12... | collective-permute-start | bytes 589832 | tf_op jit(solution)/shard_map/ppermute | solution.py:229
  63.5 11.0 %collective-permute-start.15 = (bf16[96,1024]{1,0:T(8,128)(2,1)}, bf16[96,1024]{1,0:T(8,128)(2,1)}, u32[]{:S(2)}, u32[]{:S(2)}) collective-permute-start(bf16[96,1024]{1,0:T(8,128)(2,1)} %get-tuple-element.193), channel_id=1, source_target_pairs={{2,0},{4,2},{6,4},{7,6},{5,7},{3,5},{1,3},{0,1},{10,8},{12,10},{14... | collective-permute-start | bytes 589832 | tf_op jit(solution)/shard_map/ppermute | solution.py:229
  67.3 15.2 %collective-permute-start.16 = (bf16[96,1024]{1,0:T(8,128)(2,1)}, bf16[96,1024]{1,0:T(8,128)(2,1)}, u32[]{:S(2)}, u32[]{:S(2)}) collective-permute-start(bf16[96,1024]{1,0:T(8,128)(2,1)} %get-tuple-element.198), channel_id=1, source_target_pairs={{0,2},{2,4},{4,6},{6,7},{7,5},{5,3},{3,1},{1,0},{8,10},{10,12},{12... | collective-permute-start | bytes 589832 | tf_op jit(solution)/shard_map/ppermute | solution.py:229
  68.3 14.2 %collective-permute-start.17 = (bf16[96,1024]{1,0:T(8,128)(2,1)}, bf16[96,1024]{1,0:T(8,128)(2,1)}, u32[]{:S(2)}, u32[]{:S(2)}) collective-permute-start(bf16[96,1024]{1,0:T(8,128)(2,1)} %get-tuple-element.199), channel_id=1, source_target_pairs={{2,0},{4,2},{6,4},{7,6},{5,7},{3,5},{1,3},{0,1},{10,8},{12,10},{14... | collective-permute-start | bytes 589832 | tf_op jit(solution)/shard_map/ppermute | solution.py:229
  74.5 89.3 %all-to-all-start.1 = ((bf16[16,16,2048]{2,1,0:T(8,128)(2,1)}), bf16[16,16,2048]{2,1,0:T(8,128)(2,1)S(1)}, u32[]{:S(2)}, u32[]{:S(2)}) async-start(bf16[16,16,2048]{2,1,0:T(8,128)(2,1)} %bitcast.83), calls=%async_computation.1 | async-start | bytes 2097152 | tf_op jit(solution)/shard_map/all_to_all | solution.py:216
  80.5 21.4 %collective-permute-start.18 = (bf16[96,1024]{1,0:T(8,128)(2,1)S(1)}, bf16[96,1024]{1,0:T(8,128)(2,1)S(1)}, u32[]{:S(2)}, u32[]{:S(2)}) collective-permute-start(bf16[96,1024]{1,0:T(8,128)(2,1)S(1)} %get-tuple-element.205), channel_id=1, source_target_pairs={{0,2},{2,4},{4,6},{6,7},{7,5},{5,3},{3,1},{1,0},{8,10},{10,12},{12... | collective-permute-start | bytes 589832 | tf_op jit(solution)/shard_map/ppermute | solution.py:229
  82.4 20.0 %collective-permute-start.19 = (bf16[96,1024]{1,0:T(8,128)(2,1)S(1)}, bf16[96,1024]{1,0:T(8,128)(2,1)S(1)}, u32[]{:S(2)}, u32[]{:S(2)}) collective-permute-start(bf16[96,1024]{1,0:T(8,128)(2,1)S(1)} %get-tuple-element.206), channel_id=1, source_target_pairs={{2,0},{4,2},{6,4},{7,6},{5,7},{3,5},{1,3},{0,1},{10,8},{12,10},{14... | collective-permute-start | bytes 589832 | tf_op jit(solution)/shard_map/ppermute | solution.py:229
  83.8 27.2 %collective-permute-start.20 = (bf16[96,1024]{1,0:T(8,128)(2,1)S(1)}, bf16[96,1024]{1,0:T(8,128)(2,1)S(1)}, u32[]{:S(2)}, u32[]{:S(2)}) collective-permute-start(bf16[96,1024]{1,0:T(8,128)(2,1)S(1)} %get-tuple-element.209), channel_id=1, source_target_pairs={{0,2},{2,4},{4,6},{6,7},{7,5},{5,3},{3,1},{1,0},{8,10},{10,12},{12... | collective-permute-start | bytes 589832 | tf_op jit(solution)/shard_map/ppermute | solution.py:229
  85.8 25.3 %collective-permute-start.21 = (bf16[96,1024]{1,0:T(8,128)(2,1)S(1)}, bf16[96,1024]{1,0:T(8,128)(2,1)S(1)}, u32[]{:S(2)}, u32[]{:S(2)}) collective-permute-start(bf16[96,1024]{1,0:T(8,128)(2,1)S(1)} %get-tuple-element.210), channel_id=1, source_target_pairs={{2,0},{4,2},{6,4},{7,6},{5,7},{3,5},{1,3},{0,1},{10,8},{12,10},{14... | collective-permute-start | bytes 589832 | tf_op jit(solution)/shard_map/ppermute | solution.py:229
  102.5 12.8 %collective-permute-start.22 = (bf16[96,1024]{1,0:T(8,128)(2,1)S(1)}, bf16[96,1024]{1,0:T(8,128)(2,1)S(1)}, u32[]{:S(2)}, u32[]{:S(2)}) collective-permute-start(bf16[96,1024]{1,0:T(8,128)(2,1)S(1)} %get-tuple-element.213), channel_id=1, source_target_pairs={{0,2},{2,4},{4,6},{6,7},{7,5},{5,3},{3,1},{1,0},{8,10},{10,12},{12... | collective-permute-start | bytes 589832 | tf_op jit(solution)/shard_map/ppermute | solution.py:229
  111.0 5.7 %collective-permute-start.23 = (bf16[96,1024]{1,0:T(8,128)(2,1)S(1)}, bf16[96,1024]{1,0:T(8,128)(2,1)S(1)}, u32[]{:S(2)}, u32[]{:S(2)}) collective-permute-start(bf16[96,1024]{1,0:T(8,128)(2,1)S(1)} %get-tuple-element.214), channel_id=1, source_target_pairs={{2,0},{4,2},{6,4},{7,6},{5,7},{3,5},{1,3},{0,1},{10,8},{12,10},{14... | collective-permute-start | bytes 589832 | tf_op jit(solution)/shard_map/ppermute | solution.py:229
  111.1 50.3 %copy-start.46 = (f32[64,2]{0,1:T(2,128)S(1)}, f32[64,2]{0,1:T(2,128)}, u32[]{:S(2)}) copy-start(f32[64,2]{0,1:T(2,128)} %param.14) | copy-start | bytes 1540
  111.2 50.3 %copy-start.33 = (f32[768,1]{0,1:T(1,128)S(1)}, f32[768,1]{0,1:T(1,128)}, u32[]{:S(2)}) copy-start(f32[768,1]{0,1:T(1,128)} %broadcast_in_dim.25) | copy-start | bytes 9220
  111.2 58.9 %copy-start.35 = (s32[256]{0:T(256)S(1)}, s32[256]{0:T(256)}, u32[]{:S(2)}) copy-start(s32[256]{0:T(256)} %copy-done.34) | copy-start | bytes 3076
  111.2 58.9 %copy-start.37 = (s32[256]{0:T(256)S(1)}, s32[256]{0:T(256)}, u32[]{:S(2)}) copy-start(s32[256]{0:T(256)} %copy-done.36) | copy-start | bytes 3076
  111.2 58.9 %copy-start.39 = (s32[64]{0:T(128)S(1)}, s32[64]{0:T(128)}, u32[]{:S(2)}) copy-start(s32[64]{0:T(128)} %copy-done.38) | copy-start | bytes 772
  111.2 58.9 %copy-start.41 = (s32[64]{0:T(128)S(1)}, s32[64]{0:T(128)}, u32[]{:S(2)}) copy-start(s32[64]{0:T(128)} %copy-done.40) | copy-start | bytes 772
  111.2 58.9 %copy-start.43 = (pred[256]{0:T(512)(128)(4,1)S(1)}, pred[256]{0:T(512)(128)(4,1)}, u32[]{:S(2)}) copy-start(pred[256]{0:T(512)(128)(4,1)} %copy-done.42) | copy-start | bytes 772
  111.2 9.3 %collective-permute-start.24 = (bf16[96,1024]{1,0:T(8,128)(2,1)S(1)}, bf16[96,1024]{1,0:T(8,128)(2,1)S(1)}, u32[]{:S(2)}, u32[]{:S(2)}) collective-permute-start(bf16[96,1024]{1,0:T(8,128)(2,1)S(1)} %get-tuple-element.217), channel_id=1, source_target_pairs={{0,2},{2,4},{4,6},{6,7},{7,5},{5,3},{3,1},{1,0},{8,10},{10,12},{12... | collective-permute-start | bytes 589832 | tf_op jit(solution)/shard_map/ppermute | solution.py:229
  115.4 5.7 %collective-permute-start.25 = (bf16[96,1024]{1,0:T(8,128)(2,1)S(1)}, bf16[96,1024]{1,0:T(8,128)(2,1)S(1)}, u32[]{:S(2)}, u32[]{:S(2)}) collective-permute-start(bf16[96,1024]{1,0:T(8,128)(2,1)S(1)} %get-tuple-element.218), channel_id=1, source_target_pairs={{2,0},{4,2},{6,4},{7,6},{5,7},{3,5},{1,3},{0,1},{10,8},{12,10},{14... | collective-permute-start | bytes 589832 | tf_op jit(solution)/shard_map/ppermute | solution.py:229
  117.8 6.4 %collective-permute-start.26 = (bf16[96,1024]{1,0:T(8,128)(2,1)S(1)}, bf16[96,1024]{1,0:T(8,128)(2,1)S(1)}, u32[]{:S(2)}, u32[]{:S(2)}) collective-permute-start(bf16[96,1024]{1,0:T(8,128)(2,1)S(1)} %get-tuple-element.221), channel_id=1, source_target_pairs={{0,2},{2,4},{4,6},{6,7},{7,5},{5,3},{3,1},{1,0},{8,10},{10,12},{12... | collective-permute-start | bytes 589832 | tf_op jit(solution)/shard_map/ppermute | solution.py:229
  120.5 5.7 %collective-permute-start.27 = (bf16[96,1024]{1,0:T(8,128)(2,1)S(1)}, bf16[96,1024]{1,0:T(8,128)(2,1)S(1)}, u32[]{:S(2)}, u32[]{:S(2)}) collective-permute-start(bf16[96,1024]{1,0:T(8,128)(2,1)S(1)} %get-tuple-element.222), channel_id=1, source_target_pairs={{2,0},{4,2},{6,4},{7,6},{5,7},{3,5},{1,3},{0,1},{10,8},{12,10},{14... | collective-permute-start | bytes 589832 | tf_op jit(solution)/shard_map/ppermute | solution.py:229
  120.5 50.0 %copy-start.4 = (bf16[96,1024]{1,0:T(8,128)(2,1)}, bf16[96,1024]{1,0:T(8,128)(2,1)S(1)}, u32[]{:S(2)}) copy-start(bf16[96,1024]{1,0:T(8,128)(2,1)S(1)} %collective-permute-done.24.rest_24_) | copy-start | bytes 589828
  121.0 49.4 %copy-start.5 = (bf16[96,1024]{1,0:T(8,128)(2,1)}, bf16[96,1024]{1,0:T(8,128)(2,1)S(1)}, u32[]{:S(2)}) copy-start(bf16[96,1024]{1,0:T(8,128)(2,1)S(1)} %collective-permute-done.25.rest_25_) | copy-start | bytes 589828
  122.1 7.4 %collective-permute-start.28 = (bf16[96,1024]{1,0:T(8,128)(2,1)S(1)}, bf16[96,1024]{1,0:T(8,128)(2,1)S(1)}, u32[]{:S(2)}, u32[]{:S(2)}) collective-permute-start(bf16[96,1024]{1,0:T(8,128)(2,1)S(1)} %get-tuple-element.225), channel_id=1, source_target_pairs={{0,2},{2,4},{4,6},{6,7},{7,5},{5,3},{3,1},{1,0},{8,10},{10,12},{12... | collective-permute-start | bytes 589832 | tf_op jit(solution)/shard_map/ppermute | solution.py:229
  124.2 6.4 %collective-permute-start.29 = (bf16[96,1024]{1,0:T(8,128)(2,1)S(1)}, bf16[96,1024]{1,0:T(8,128)(2,1)S(1)}, u32[]{:S(2)}, u32[]{:S(2)}) collective-permute-start(bf16[96,1024]{1,0:T(8,128)(2,1)S(1)} %get-tuple-element.226), channel_id=1, source_target_pairs={{2,0},{4,2},{6,4},{7,6},{5,7},{3,5},{1,3},{0,1},{10,8},{12,10},{14... | collective-permute-start | bytes 589832 | tf_op jit(solution)/shard_map/ppermute | solution.py:229
  124.2 47.3 %copy-start.6 = (bf16[96,1024]{1,0:T(8,128)(2,1)}, bf16[96,1024]{1,0:T(8,128)(2,1)S(1)}, u32[]{:S(2)}) copy-start(bf16[96,1024]{1,0:T(8,128)(2,1)S(1)} %collective-permute-done.26.rest_26_) | copy-start | bytes 589828
  126.2 45.3 %copy-start.7 = (bf16[96,1024]{1,0:T(8,128)(2,1)}, bf16[96,1024]{1,0:T(8,128)(2,1)S(1)}, u32[]{:S(2)}) copy-start(bf16[96,1024]{1,0:T(8,128)(2,1)S(1)} %collective-permute-done.27.rest_27_) | copy-start | bytes 589828
  127.2 6.5 %collective-permute-start.30 = (bf16[96,1024]{1,0:T(8,128)(2,1)S(1)}, bf16[96,1024]{1,0:T(8,128)(2,1)S(1)}, u32[]{:S(2)}, u32[]{:S(2)}) collective-permute-start(bf16[96,1024]{1,0:T(8,128)(2,1)S(1)} %get-tuple-element.229), channel_id=1, source_target_pairs={{0,2},{2,4},{4,6},{6,7},{7,5},{5,3},{3,1},{1,0},{8,10},{10,12},{12... | collective-permute-start | bytes 589832 | tf_op jit(solution)/shard_map/ppermute | solution.py:229
  129.5 5.8 %collective-permute-start.31 = (bf16[96,1024]{1,0:T(8,128)(2,1)S(1)}, bf16[96,1024]{1,0:T(8,128)(2,1)S(1)}, u32[]{:S(2)}, u32[]{:S(2)}) collective-permute-start(bf16[96,1024]{1,0:T(8,128)(2,1)S(1)} %get-tuple-element.230), channel_id=1, source_target_pairs={{2,0},{4,2},{6,4},{7,6},{5,7},{3,5},{1,3},{0,1},{10,8},{12,10},{14... | collective-permute-start | bytes 589832 | tf_op jit(solution)/shard_map/ppermute | solution.py:229
  129.5 42.0 %copy-start.8 = (bf16[96,1024]{1,0:T(8,128)(2,1)}, bf16[96,1024]{1,0:T(8,128)(2,1)S(1)}, u32[]{:S(2)}) copy-start(bf16[96,1024]{1,0:T(8,128)(2,1)S(1)} %collective-permute-done.28.rest_28_) | copy-start | bytes 589828
  131.7 6.8 %collective-permute-start.32 = (bf16[96,1024]{1,0:T(8,128)(2,1)S(1)}, bf16[96,1024]{1,0:T(8,128)(2,1)S(1)}, u32[]{:S(2)}, u32[]{:S(2)}) collective-permute-start(bf16[96,1024]{1,0:T(8,128)(2,1)S(1)} %get-tuple-element.233), channel_id=1, source_target_pairs={{0,2},{2,4},{4,6},{6,7},{7,5},{5,3},{3,1},{1,0},{8,10},{10,12},{12... | collective-permute-start | bytes 589832 | tf_op jit(solution)/shard_map/ppermute | solution.py:229
  133.7 6.7 %collective-permute-start.33 = (bf16[96,1024]{1,0:T(8,128)(2,1)S(1)}, bf16[96,1024]{1,0:T(8,128)(2,1)S(1)}, u32[]{:S(2)}, u32[]{:S(2)}) collective-permute-start(bf16[96,1024]{1,0:T(8,128)(2,1)S(1)} %get-tuple-element.234), channel_id=1, source_target_pairs={{2,0},{4,2},{6,4},{7,6},{5,7},{3,5},{1,3},{0,1},{10,8},{12,10},{14... | collective-permute-start | bytes 589832 | tf_op jit(solution)/shard_map/ppermute | solution.py:229
  136.3 7.3 %collective-permute-start.34 = (bf16[96,1024]{1,0:T(8,128)(2,1)S(1)}, bf16[96,1024]{1,0:T(8,128)(2,1)S(1)}, u32[]{:S(2)}, u32[]{:S(2)}) collective-permute-start(bf16[96,1024]{1,0:T(8,128)(2,1)S(1)} %get-tuple-element.237), channel_id=1, source_target_pairs={{0,2},{2,4},{4,6},{6,7},{7,5},{5,3},{3,1},{1,0},{8,10},{10,12},{12... | collective-permute-start | bytes 589832 | tf_op jit(solution)/shard_map/ppermute | solution.py:229
  138.2 6.9 %collective-permute-start.35 = (bf16[96,1024]{1,0:T(8,128)(2,1)S(1)}, bf16[96,1024]{1,0:T(8,128)(2,1)S(1)}, u32[]{:S(2)}, u32[]{:S(2)}) collective-permute-start(bf16[96,1024]{1,0:T(8,128)(2,1)S(1)} %get-tuple-element.238), channel_id=1, source_target_pairs={{2,0},{4,2},{6,4},{7,6},{5,7},{3,5},{1,3},{0,1},{10,8},{12,10},{14... | collective-permute-start | bytes 589832 | tf_op jit(solution)/shard_map/ppermute | solution.py:229
  141.5 6.9 %collective-permute-start.36 = (bf16[96,1024]{1,0:T(8,128)(2,1)S(1)}, bf16[96,1024]{1,0:T(8,128)(2,1)S(1)}, u32[]{:S(2)}, u32[]{:S(2)}) collective-permute-start(bf16[96,1024]{1,0:T(8,128)(2,1)S(1)} %get-tuple-element.241), channel_id=1, source_target_pairs={{0,2},{2,4},{4,6},{6,7},{7,5},{5,3},{3,1},{1,0},{8,10},{10,12},{12... | collective-permute-start | bytes 589832 | tf_op jit(solution)/shard_map/ppermute | solution.py:229
  143.0 7.8 %collective-permute-start.37 = (bf16[96,1024]{1,0:T(8,128)(2,1)S(1)}, bf16[96,1024]{1,0:T(8,128)(2,1)S(1)}, u32[]{:S(2)}, u32[]{:S(2)}) collective-permute-start(bf16[96,1024]{1,0:T(8,128)(2,1)S(1)} %get-tuple-element.242), channel_id=1, source_target_pairs={{2,0},{4,2},{6,4},{7,6},{5,7},{3,5},{1,3},{0,1},{10,8},{12,10},{14... | collective-permute-start | bytes 589832 | tf_op jit(solution)/shard_map/ppermute | solution.py:229
  145.1 7.9 %collective-permute-start.38 = (bf16[96,1024]{1,0:T(8,128)(2,1)S(1)}, bf16[96,1024]{1,0:T(8,128)(2,1)}, u32[]{:S(2)}, u32[]{:S(2)}) collective-permute-start(bf16[96,1024]{1,0:T(8,128)(2,1)S(1)} %collective-permute-done.34.rest_34_), channel_id=1, source_target_pairs={{0,2},{2,4},{4,6},{6,7},{7,5},{5,3},{3,1},{1,0},{8,10},{10,12},{12... | collective-permute-start | bytes 589832 | tf_op jit(solution)/shard_map/ppermute | solution.py:229
  146.2 9.0 %collective-permute-start.39 = (bf16[96,1024]{1,0:T(8,128)(2,1)S(1)}, bf16[96,1024]{1,0:T(8,128)(2,1)}, u32[]{:S(2)}, u32[]{:S(2)}) collective-permute-start(bf16[96,1024]{1,0:T(8,128)(2,1)S(1)} %collective-permute-done.35.rest_35_), channel_id=1, source_target_pairs={{2,0},{4,2},{6,4},{7,6},{5,7},{3,5},{1,3},{0,1},{10,8},{12,10},{14... | collective-permute-start | bytes 589832 | tf_op jit(solution)/shard_map/ppermute | solution.py:229
  150.9 6.6 %collective-permute-start.40 = (bf16[96,1024]{1,0:T(8,128)(2,1)S(1)}, bf16[96,1024]{1,0:T(8,128)(2,1)}, u32[]{:S(2)}, u32[]{:S(2)}) collective-permute-start(bf16[96,1024]{1,0:T(8,128)(2,1)S(1)} %collective-permute-done.36.rest_36_), channel_id=1, source_target_pairs={{0,2},{2,4},{4,6},{6,7},{7,5},{5,3},{3,1},{1,0},{8,10},{10,12},{12... | collective-permute-start | bytes 589832 | tf_op jit(solution)/shard_map/ppermute | solution.py:229
  151.4 8.0 %collective-permute-start.41 = (bf16[96,1024]{1,0:T(8,128)(2,1)S(1)}, bf16[96,1024]{1,0:T(8,128)(2,1)}, u32[]{:S(2)}, u32[]{:S(2)}) collective-permute-start(bf16[96,1024]{1,0:T(8,128)(2,1)S(1)} %collective-permute-done.37.rest_37_), channel_id=1, source_target_pairs={{2,0},{4,2},{6,4},{7,6},{5,7},{3,5},{1,3},{0,1},{10,8},{12,10},{14... | collective-permute-start | bytes 589832 | tf_op jit(solution)/shard_map/ppermute | solution.py:229
  155.2 7.2 %collective-permute-start.42 = (bf16[96,1024]{1,0:T(8,128)(2,1)}, bf16[96,1024]{1,0:T(8,128)(2,1)}, u32[]{:S(2)}, u32[]{:S(2)}) collective-permute-start(bf16[96,1024]{1,0:T(8,128)(2,1)} %collective-permute-done.38.rest_38_), channel_id=1, source_target_pairs={{0,2},{2,4},{4,6},{6,7},{7,5},{5,3},{3,1},{1,0},{8,10},{10,12},{12... | collective-permute-start | bytes 589832 | tf_op jit(solution)/shard_map/ppermute | solution.py:229
  155.7 8.2 %collective-permute-start.43 = (bf16[96,1024]{1,0:T(8,128)(2,1)}, bf16[96,1024]{1,0:T(8,128)(2,1)}, u32[]{:S(2)}, u32[]{:S(2)}) collective-permute-start(bf16[96,1024]{1,0:T(8,128)(2,1)} %collective-permute-done.39.rest_39_), channel_id=1, source_target_pairs={{2,0},{4,2},{6,4},{7,6},{5,7},{3,5},{1,3},{0,1},{10,8},{12,10},{14... | collective-permute-start | bytes 589832 | tf_op jit(solution)/shard_map/ppermute | solution.py:229
  159.4 6.8 %collective-permute-start.44 = (bf16[96,1024]{1,0:T(8,128)(2,1)}, bf16[96,1024]{1,0:T(8,128)(2,1)}, u32[]{:S(2)}, u32[]{:S(2)}) collective-permute-start(bf16[96,1024]{1,0:T(8,128)(2,1)} %collective-permute-done.40.rest_40_), channel_id=1, source_target_pairs={{0,2},{2,4},{4,6},{6,7},{7,5},{5,3},{3,1},{1,0},{8,10},{10,12},{12... | collective-permute-start | bytes 589832 | tf_op jit(solution)/shard_map/ppermute | solution.py:229
  159.9 8.2 %collective-permute-start.45 = (bf16[96,1024]{1,0:T(8,128)(2,1)}, bf16[96,1024]{1,0:T(8,128)(2,1)}, u32[]{:S(2)}, u32[]{:S(2)}) collective-permute-start(bf16[96,1024]{1,0:T(8,128)(2,1)} %collective-permute-done.41.rest_41_), channel_id=1, source_target_pairs={{2,0},{4,2},{6,4},{7,6},{5,7},{3,5},{1,3},{0,1},{10,8},{12,10},{14... | collective-permute-start | bytes 589832 | tf_op jit(solution)/shard_map/ppermute | solution.py:229
  163.9 7.7 %collective-permute-start.46 = (bf16[96,1024]{1,0:T(8,128)(2,1)}, bf16[96,1024]{1,0:T(8,128)(2,1)S(1)}, u32[]{:S(2)}, u32[]{:S(2)}) collective-permute-start(bf16[96,1024]{1,0:T(8,128)(2,1)} %collective-permute-done.42.rest_42_), channel_id=1, source_target_pairs={{0,2},{2,4},{4,6},{6,7},{7,5},{5,3},{3,1},{1,0},{8,10},{10,12},{12... | collective-permute-start | bytes 589832 | tf_op jit(solution)/shard_map/ppermute | solution.py:229
  164.5 7.1 %collective-permute-start.47 = (bf16[96,1024]{1,0:T(8,128)(2,1)}, bf16[96,1024]{1,0:T(8,128)(2,1)S(1)}, u32[]{:S(2)}, u32[]{:S(2)}) collective-permute-start(bf16[96,1024]{1,0:T(8,128)(2,1)} %collective-permute-done.43.rest_43_), channel_id=1, source_target_pairs={{2,0},{4,2},{6,4},{7,6},{5,7},{3,5},{1,3},{0,1},{10,8},{12,10},{14... | collective-permute-start | bytes 589832 | tf_op jit(solution)/shard_map/ppermute | solution.py:229
  168.1 6.0 %collective-permute-start.48 = (bf16[96,1024]{1,0:T(8,128)(2,1)}, bf16[96,1024]{1,0:T(8,128)(2,1)}, u32[]{:S(2)}, u32[]{:S(2)}) collective-permute-start(bf16[96,1024]{1,0:T(8,128)(2,1)} %collective-permute-done.44.rest_44_), channel_id=1, source_target_pairs={{0,2},{2,4},{4,6},{6,7},{7,5},{5,3},{3,1},{1,0},{8,10},{10,12},{12... | collective-permute-start | bytes 589832 | tf_op jit(solution)/shard_map/ppermute | solution.py:229
  168.7 6.0 %collective-permute-start.49 = (bf16[96,1024]{1,0:T(8,128)(2,1)}, bf16[96,1024]{1,0:T(8,128)(2,1)}, u32[]{:S(2)}, u32[]{:S(2)}) collective-permute-start(bf16[96,1024]{1,0:T(8,128)(2,1)} %collective-permute-done.45.rest_45_), channel_id=1, source_target_pairs={{2,0},{4,2},{6,4},{7,6},{5,7},{3,5},{1,3},{0,1},{10,8},{12,10},{14... | collective-permute-start | bytes 589832 | tf_op jit(solution)/shard_map/ppermute | solution.py:229
  (36 other events, 550.9 us)

commit v5 on v4

--- a/solution.py
+++ b/solution.py
@@ -36,23 +36,30 @@
     return (jax.nn.silu(pre[:, :hidden_units]) * pre[:, hidden_units:]).astype(jnp.bfloat16)
 
 
-def both_ways(n, chunks, lag):
-    return min(chunks, (n - 1 - n // 2) * lag // 2)
-
-
-def order_of(n, chunks, lag):
-    single = chunks - both_ways(n, chunks, lag)
+def plan(n, chunks, lag):
+    most = (n - 2) * lag
+    single = chunks - most // 2
+    ways = [[(way, c) for c in range(single)] + [None] * most for way in range(2)]
+    meets = {}
     shared = [(lane, c) for c in range(single, chunks) for lane in range(2)]
-    return [[(way, c) for c in range(single)] + shared for way in range(2)]
+    for k in range(1, n - 1):
+        for i in range(lag):
+            turns = (single + (n - 2 - k) * lag + i, single + (k - 1) * lag + i)
+            chunk = shared[min(len(meets), len(shared) - 1)]
+            meets.setdefault(chunk, (k, turns))
+            for way in range(2):
+                ways[way][turns[way]] = chunk
+    return single, ways, meets
 
 
 def arrivals(n, chunks, lag, h):
-    single = chunks - both_ways(n, chunks, lag)
-    nearer = 0 if h <= n // 2 else 1
-    for way, turns in enumerate(order_of(n, chunks, lag)):
-        for turn, (lane, c) in enumerate(turns):
-            if c < single or way == nearer:
-                yield lane, c, way, turn + lag * ((h, n - h)[way] - 1)
+    single, _, meets = plan(n, chunks, lag)
+    for way in range(2):
+        for c in range(single):
+            yield way, c, way, c + lag * ((h, n - h)[way] - 1)
+    for (lane, c), (k, turns) in meets.items():
+        way = 0 if h <= k else 1
+        yield lane, c, way, turns[way] + lag * ((h, n - h)[way] - 1)
 
 
 def hot_kernel(n, lag, hops, x, weight, gate_up, down, *rest):
@@ -197,7 +204,7 @@
         [(order[(i + 1) % n], order[i]) for i in range(n)],
     )
     weight = res_weight[:, None]
-    turns = order_of(n, chunks, lag)
+    _, turns, _ = plan(n, chunks, lag)
     sends = len(turns[0])
     steps = 1 + max(t for h in range(1, n) for _, _, _, t in arrivals(n, chunks, lag, h))
     came, last = [], None
@@ -207,11 +214,11 @@
             got = came[t - lag]
             if t == lag + 1:
                 got, hops, weight = join(got, hops, weight)
-            elif t == steps // 3:
+            elif t == steps * 3 // 8:
                 got, cold = join(got, cold)
                 pre = jnp.dot(cold, gate_up, preferred_element_type=jnp.float32)
                 cold = jnp.dot(swiglu(pre, hidden_units), down, preferred_element_type=jnp.float32).astype(jnp.bfloat16)
-            elif t == steps // 3 + 1:
+            elif t == steps * 3 // 8 + 1:
                 got, cold = join(got, cold)
                 cold = lax.all_to_all(cold, ("ep", "shadow"), 0, 0, tiled=True)
             elif t == steps - 2:

time: 186 us -> 176 us (0.946)
  waiting for transfers between devices: 55.2 us -> 42.3 us
  starting transfers between devices: 77.6 us -> 70.3 us
  other arithmetic: 19.5 us -> 26.2 us
  local copies, waits for them, and re-layouts: 9.04 us -> 12.2 us
    ppermute x50 -> x44, waiting for transfers between devices: 55.2 us -> 42.3 us  [body(): lax.ppermute(mine[i], 'shadow', ways[i])]
    ppermute x50 -> x44, starting transfers between devices: 66.5 us -> 59.3 us  [body(): lax.ppermute(mine[i], 'shadow', ways[i])]
    select_n x17 -> x23, other arithmetic: 18.9 us -> 25.6 us  [body(): jnp.where(me == root, m, g)]
  transfers between devices with their start and end apart: 52 -> 46, of which waited for: 25 -> 20; matrix products, arithmetic and copies ran while one was open for 18% -> 24% of each run, Pallas kernels for 0% -> 0%
where the time goes in v5:
time: 176 us; the launch traced here: 175 us
  starting transfers between devices  70.3 us (40%)
  waiting for transfers between devices  42.3 us (24%)
  other arithmetic  26.2 us (15%)
  local copies, waits for them, and re-layouts  12.2 us (7%)
  Pallas kernels  10.9 us (6%)
  matrix products  8.27 us (5%)
  between operations  5.24 us (3%)
    ppermute x44, starting transfers between devices, body(): lax.ppermute(mine[i], 'shadow', ways[i])  59.3 us
    ppermute x44, waiting for transfers between devices, body(): lax.ppermute(mine[i], 'shadow', ways[i])  42.3 us
    select_n x23, other arithmetic, body(): jnp.where(me == root, m, g)  25.6 us
    pallas_call x1, Pallas kernels, hot_expert(): pl.pallas_call(functools.partial(hot_kernel, n, lag), grid=(BLOCKS,), out...  10.9 us
    all_to_all x1, starting transfers between devices, body(): cold = lax.all_to_all(outgoing, ('ep', 'shadow'), 0, 0, tiled=True)  6.37 us
    all_to_all x1, starting transfers between devices, body(): cold = lax.all_to_all(cold, ('ep', 'shadow'), 0, 0, tiled=True)  4.67 us
    slice x3, local copies, waits for them, and re-layouts, cut(): out.append(part[low:high])  4.45 us
  transfers between devices with their start and end apart: 46, of which 20 were waited for; matrix products, arithmetic and copies ran while one was open for 24% of the time, Pallas kernels for 0%

profile of v5, /device:TPU:0, one launch (start us, length us, event | category | flops | bytes accessed | tf_op | source)
XLA Modules:
  0.0 175.5 jit_solution(17281652646449122821)
XLA Ops:
  0.6 2.2 %slice_bitcast_fusion = (bf16[96,1024]{1,0:T(8,128)(2,1)}, bf16[96,1024]{1,0:T(8,128)(2,1)}, bf16[96,1024]{1,0:T(8,128)(2,1)}, bf16[96,1024]{1,0:T(8,128)(2,1)}) fusion(bf16[1,2048,1024]{2,1,0:T(8,128)(2,1)} %param.15), kind=kLoop, calls=%fused_computation.26 | loop fusion | bytes 1572864 | tf_op jit(solution)/shard_map/slice | solution.py:158
  2.8 3.1 %collective-permute-start = (bf16[96,1024]{1,0:T(8,128)(2,1)}, bf16[96,1024]{1,0:T(8,128)(2,1)}, u32[]{:S(2)}, u32[]{:S(2)}) collective-permute-start(bf16[96,1024]{1,0:T(8,128)(2,1)} %get-tuple-element.144), channel_id=1, source_target_pairs={{0,2},{2,4},{4,6},{6,7},{7,5},{5,3},{3,1},{1,0},{8,10},{10,12},{12... | collective-permute-start | bytes 589832 | tf_op jit(solution)/shard_map/ppermute | solution.py:236
  5.9 2.0 %collective-permute-start.2 = (bf16[96,1024]{1,0:T(8,128)(2,1)}, bf16[96,1024]{1,0:T(8,128)(2,1)}, u32[]{:S(2)}, u32[]{:S(2)}) collective-permute-start(bf16[96,1024]{1,0:T(8,128)(2,1)} %get-tuple-element.148), channel_id=1, source_target_pairs={{0,2},{2,4},{4,6},{6,7},{7,5},{5,3},{3,1},{1,0},{8,10},{10,12},{12... | collective-permute-start | bytes 589832 | tf_op jit(solution)/shard_map/ppermute | solution.py:236
  9.0 1.5 convolution_convert_fusion.1
  10.5 6.4 %all-to-all-start = ((bf16[16,16,2048]{2,1,0:T(8,128)(2,1)}), bf16[16,16,2048]{2,1,0:T(8,128)(2,1)S(1)}, u32[]{:S(2)}, u32[]{:S(2)}) async-start(bf16[16,16,2048]{2,1,0:T(8,128)(2,1)} %bitcast.25), calls=%async_computation | async-start | bytes 2097152 | tf_op jit(solution)/shard_map/all_to_all | solution.py:189
  23.9 1.6 slice_bitcast_fusion.4
  25.5 1.3 slice_bitcast_fusion.7
  26.9 1.7 copy.11.weight
  28.5 1.3 bitcast_select_fusion.14
  29.8 2.0 %collective-permute-start.4 = (bf16[96,1024]{1,0:T(8,128)(2,1)S(1)}, bf16[96,1024]{1,0:T(8,128)(2,1)S(1)}, u32[]{:S(2)}, u32[]{:S(2)}) collective-permute-start(bf16[96,1024]{1,0:T(8,128)(2,1)S(1)} %get-tuple-element.152), channel_id=1, source_target_pairs={{0,2},{2,4},{4,6},{6,7},{7,5},{5,3},{3,1},{1,0},{8,10},{10,12},{12... | collective-permute-start | bytes 589832 | tf_op jit(solution)/shard_map/ppermute | solution.py:236
  31.9 1.3 bitcast_select_fusion.12
  33.1 2.0 %collective-permute-start.6 = (bf16[96,1024]{1,0:T(8,128)(2,1)S(1)}, bf16[96,1024]{1,0:T(8,128)(2,1)S(1)}, u32[]{:S(2)}, u32[]{:S(2)}) collective-permute-start(bf16[96,1024]{1,0:T(8,128)(2,1)S(1)} %get-tuple-element.158), channel_id=1, source_target_pairs={{0,2},{2,4},{4,6},{6,7},{7,5},{5,3},{3,1},{1,0},{8,10},{10,12},{12... | collective-permute-start | bytes 589832 | tf_op jit(solution)/shard_map/ppermute | solution.py:236
  35.2 5.0 %collective-permute-done.4.rest_4_ = bf16[96,1024]{1,0:T(8,128)(2,1)S(1)} collective-permute-done((bf16[96,1024]{1,0:T(8,128)(2,1)S(1)}, bf16[96,1024]{1,0:T(8,128)(2,1)S(1)}, u32[]{:S(2)}, u32[]{:S(2)}) %collective-permute-start.4) | collective-permute-done | bytes 196640 | tf_op jit(solution)/shard_map/ppermute | solution.py:236
  40.2 3.5 %collective-permute-done.5.rest_5_ = bf16[96,1024]{1,0:T(8,128)(2,1)S(1)} collective-permute-done((bf16[96,1024]{1,0:T(8,128)(2,1)S(1)}, bf16[96,1024]{1,0:T(8,128)(2,1)S(1)}, u32[]{:S(2)}, u32[]{:S(2)}) %collective-permute-start.5) | collective-permute-done | bytes 196640 | tf_op jit(solution)/shard_map/ppermute | solution.py:236
  43.7 1.2 bitcast_select_fusion.10
  44.9 5.0 %collective-permute-start.8 = (bf16[96,1024]{1,0:T(8,128)(2,1)S(1)}, bf16[96,1024]{1,0:T(8,128)(2,1)S(1)}, u32[]{:S(2)}, u32[]{:S(2)}) collective-permute-start(bf16[96,1024]{1,0:T(8,128)(2,1)S(1)} %get-tuple-element.162), channel_id=1, source_target_pairs={{0,2},{2,4},{4,6},{6,7},{7,5},{5,3},{3,1},{1,0},{8,10},{10,12},{12... | collective-permute-start | bytes 589832 | tf_op jit(solution)/shard_map/ppermute | solution.py:236
  49.9 1.2 bitcast_select_fusion.8
  51.1 2.5 %collective-permute-start.10 = (bf16[96,1024]{1,0:T(8,128)(2,1)S(1)}, bf16[96,1024]{1,0:T(8,128)(2,1)S(1)}, u32[]{:S(2)}, u32[]{:S(2)}) collective-permute-start(bf16[96,1024]{1,0:T(8,128)(2,1)S(1)} %get-tuple-element.166), channel_id=1, source_target_pairs={{0,2},{2,4},{4,6},{6,7},{7,5},{5,3},{3,1},{1,0},{8,10},{10,12},{12... | collective-permute-start | bytes 589832 | tf_op jit(solution)/shard_map/ppermute | solution.py:236
  53.6 1.9 %collective-permute-done.9.rest_9_ = bf16[96,1024]{1,0:T(8,128)(2,1)S(1)} collective-permute-done((bf16[96,1024]{1,0:T(8,128)(2,1)S(1)}, bf16[96,1024]{1,0:T(8,128)(2,1)S(1)}, u32[]{:S(2)}, u32[]{:S(2)}) %collective-permute-start.9) | collective-permute-done | bytes 196640 | tf_op jit(solution)/shard_map/ppermute | solution.py:236
  55.6 1.2 bitcast_select_fusion.6
  56.7 1.1 collective-permute-start.12
  58.8 1.7 collective-permute-done.11.rest_11_
  60.5 1.9 %bitcast_select_fusion.4 = (bf16[96,1024]{1,0:T(8,128)(2,1)}, bf16[96,1024]{1,0:T(8,128)(2,1)}) fusion(bf16[96,1024]{1,0:T(8,128)(2,1)S(1)} %collective-permute-done.11.rest_11_, bf16[1,2048,1024]{2,1,0:T(8,128)(2,1)} %param.15, pred[]{:T(512)S(6)} %eq.21, bf16[96,1024]{1,0:T(8,128)(2,1)S(1)} %collective-permute-done.10.rest_10_), kind=kLoop, calls=%fused_computation.14 | loop fusion | flops 196608 | bytes 1179649 | tf_op jit(solution)/shard_map/jit(_where)/select_n | solution.py:234
  63.4 1.0 collective-permute-start.15
  65.2 2.0 %bitcast_select_fusion.2 = (bf16[96,1024]{1,0:T(8,128)(2,1)}, bf16[96,1024]{1,0:T(8,128)(2,1)}) fusion(bf16[96,1024]{1,0:T(8,128)(2,1)} %collective-permute-done.13.rest_13_, bf16[1,2048,1024]{2,1,0:T(8,128)(2,1)} %param.15, pred[]{:T(512)S(6)} %eq.21, bf16[96,1024]{1,0:T(8,128)(2,1)} %copy-done.13), kind=kLoop, calls=%fused_computation.12 | loop fusion | flops 196608 | bytes 1179649 | tf_op jit(solution)/shard_map/jit(_where)/select_n | solution.py:234
  68.2 1.0 collective-permute-start.17
  69.2 3.4 %fusion.31 = f32[256,1024]{1,0:T(8,128)S(1)} fusion(bf16[256,2048]{1,0:T(8,128)(2,1)S(1)} %bitcast.87, bf16[1,2048,1024]{2,1,0:T(8,128)(2,1)} %param.15), kind=kOutput, calls=%fused_computation.97 | convolution fusion | flops 1073741824 | bytes 6291456 | tf_op jit(solution)/shard_map/dot_general | solution.py:219
  72.7 1.7 convolution_convert_fusion
  74.4 4.7 %all-to-all-start.1 = ((bf16[16,16,2048]{2,1,0:T(8,128)(2,1)}), bf16[16,16,2048]{2,1,0:T(8,128)(2,1)S(1)}, u32[]{:S(2)}, u32[]{:S(2)}) async-start(bf16[16,16,2048]{2,1,0:T(8,128)(2,1)} %bitcast.88), calls=%async_computation.1 | async-start | bytes 2097152 | tf_op jit(solution)/shard_map/all_to_all | solution.py:223
  79.1 1.3 bitcast_select_fusion
  80.4 2.0 %collective-permute-start.18 = (bf16[96,1024]{1,0:T(8,128)(2,1)S(1)}, bf16[96,1024]{1,0:T(8,128)(2,1)S(1)}, u32[]{:S(2)}, u32[]{:S(2)}) collective-permute-start(bf16[96,1024]{1,0:T(8,128)(2,1)S(1)} %get-tuple-element.187), channel_id=1, source_target_pairs={{0,2},{2,4},{4,6},{6,7},{7,5},{5,3},{3,1},{1,0},{8,10},{10,12},{12... | collective-permute-start | bytes 589832 | tf_op jit(solution)/shard_map/ppermute | solution.py:236
  83.4 1.1 broadcast_select_fusion.22
  84.5 2.0 %collective-permute-start.20 = (bf16[96,1024]{1,0:T(8,128)(2,1)S(1)}, bf16[96,1024]{1,0:T(8,128)(2,1)S(1)}, u32[]{:S(2)}, u32[]{:S(2)}) collective-permute-start(bf16[96,1024]{1,0:T(8,128)(2,1)S(1)} %broadcast_select_fusion.23), channel_id=1, source_target_pairs={{0,2},{2,4},{4,6},{6,7},{7,5},{5,3},{3,1},{1,0},{8,10},{10,12},{12... | collective-permute-start | bytes 589832 | tf_op jit(solution)/shard_map/ppermute | solution.py:236
  86.6 15.1 %collective-permute-done.18.rest_18_ = bf16[96,1024]{1,0:T(8,128)(2,1)S(1)} collective-permute-done((bf16[96,1024]{1,0:T(8,128)(2,1)S(1)}, bf16[96,1024]{1,0:T(8,128)(2,1)S(1)}, u32[]{:S(2)}, u32[]{:S(2)}) %collective-permute-start.18) | collective-permute-done | bytes 196640 | tf_op jit(solution)/shard_map/ppermute | solution.py:236
  102.5 8.5 %collective-permute-start.22 = (bf16[96,1024]{1,0:T(8,128)(2,1)S(1)}, bf16[96,1024]{1,0:T(8,128)(2,1)S(1)}, u32[]{:S(2)}, u32[]{:S(2)}) collective-permute-start(bf16[96,1024]{1,0:T(8,128)(2,1)S(1)} %broadcast_select_fusion.21), channel_id=1, source_target_pairs={{0,2},{2,4},{4,6},{6,7},{7,5},{5,3},{3,1},{1,0},{8,10},{10,12},{12... | collective-permute-start | bytes 589832 | tf_op jit(solution)/shard_map/ppermute | solution.py:236
  111.1 4.1 %collective-permute-start.24 = (bf16[96,1024]{1,0:T(8,128)(2,1)S(1)}, bf16[96,1024]{1,0:T(8,128)(2,1)S(1)}, u32[]{:S(2)}, u32[]{:S(2)}) collective-permute-start(bf16[96,1024]{1,0:T(8,128)(2,1)S(1)} %get-tuple-element.199), channel_id=1, source_target_pairs={{0,2},{2,4},{4,6},{6,7},{7,5},{5,3},{3,1},{1,0},{8,10},{10,12},{12... | collective-permute-start | bytes 589832 | tf_op jit(solution)/shard_map/ppermute | solution.py:236
  115.2 1.5 collective-permute-done.23.rest_23_
  116.7 1.2 broadcast_select_fusion.16
  117.9 2.6 %collective-permute-start.26 = (bf16[96,1024]{1,0:T(8,128)(2,1)S(1)}, bf16[96,1024]{1,0:T(8,128)(2,1)S(1)}, u32[]{:S(2)}, u32[]{:S(2)}) collective-permute-start(bf16[96,1024]{1,0:T(8,128)(2,1)S(1)} %get-tuple-element.203), channel_id=1, source_target_pairs={{0,2},{2,4},{4,6},{6,7},{7,5},{5,3},{3,1},{1,0},{8,10},{10,12},{12... | collective-permute-start | bytes 589832 | tf_op jit(solution)/shard_map/ppermute | solution.py:236
  120.9 1.2 broadcast_select_fusion.14
  122.1 2.2 %collective-permute-start.28 = (bf16[96,1024]{1,0:T(8,128)(2,1)S(1)}, bf16[96,1024]{1,0:T(8,128)(2,1)S(1)}, u32[]{:S(2)}, u32[]{:S(2)}) collective-permute-start(bf16[96,1024]{1,0:T(8,128)(2,1)S(1)} %get-tuple-element.207), channel_id=1, source_target_pairs={{0,2},{2,4},{4,6},{6,7},{7,5},{5,3},{3,1},{1,0},{8,10},{10,12},{12... | collective-permute-start | bytes 589832 | tf_op jit(solution)/shard_map/ppermute | solution.py:236
  124.3 1.9 %collective-permute-done.27.rest_27_ = bf16[96,1024]{1,0:T(8,128)(2,1)S(1)} collective-permute-done((bf16[96,1024]{1,0:T(8,128)(2,1)S(1)}, bf16[96,1024]{1,0:T(8,128)(2,1)S(1)}, u32[]{:S(2)}, u32[]{:S(2)}) %collective-permute-start.27) | collective-permute-done | bytes 196640 | tf_op jit(solution)/shard_map/ppermute | solution.py:236
  126.2 1.2 broadcast_select_fusion.12
  127.4 1.1 collective-permute-start.30
  129.5 1.7 collective-permute-done.29.rest_29_
  131.1 1.2 broadcast_select_fusion.10
  132.3 1.0 collective-permute-start.32
  133.3 1.0 collective-permute-start.33
  135.3 1.2 broadcast_select_fusion.8
  136.5 1.0 collective-permute-start.34
  137.5 1.1 collective-permute-start.35
  140.1 1.2 broadcast_select_fusion.6
  141.9 1.4 collective-permute-start.37
  143.8 1.1 collective-permute-done.35.rest_35_
  144.9 1.9 %broadcast_select_fusion.4 = (bf16[96,1024]{1,0:T(8,128)(2,1)}, bf16[96,1024]{1,0:T(8,128)(2,1)}) fusion(bf16[96,1024]{1,0:T(8,128)(2,1)S(1)} %collective-permute-done.35.rest_35_, pred[]{:T(512)S(6)} %eq.21, bf16[512,2048]{1,0:T(8,128)(2,1)} %bitcast.76, bf16[96,1024]{1,0:T(8,128)(2,1)S(1)} %collective-permute-done.34.rest_34_), kind=kLoop, calls=%fused_computation.34 | loop fusion | flops 196608 | bytes 1179649 | tf_op jit(solution)/shard_map/jit(_where)/select_n | solution.py:234
  147.4 1.4 collective-permute-start.39
  150.6 1.1 broadcast_select_fusion.3
  151.7 2.4 %collective-permute-start.40 = (bf16[96,1024]{1,0:T(8,128)(2,1)S(1)}, bf16[96,1024]{1,0:T(8,128)(2,1)S(1)}, u32[]{:S(2)}, u32[]{:S(2)}) collective-permute-start(bf16[96,1024]{1,0:T(8,128)(2,1)S(1)} %broadcast_select_fusion.3), channel_id=1, source_target_pairs={{0,2},{2,4},{4,6},{6,7},{7,5},{5,3},{3,1},{1,0},{8,10},{10,12},{12... | collective-permute-start | bytes 589832 | tf_op jit(solution)/shard_map/ppermute | solution.py:236
  155.1 1.2 broadcast_select_fusion
  156.3 1.7 collective-permute-start.42
  158.8 1.1 fusion
  159.9 2.1 %collective-permute-done.42.rest_42_ = bf16[96,1024]{1,0:T(8,128)(2,1)S(1)} collective-permute-done((bf16[96,1024]{1,0:T(8,128)(2,1)S(1)}, bf16[96,1024]{1,0:T(8,128)(2,1)S(1)}, u32[]{:S(2)}, u32[]{:S(2)}) %collective-permute-start.42) | collective-permute-done | bytes 196640 | tf_op jit(solution)/shard_map/ppermute | solution.py:236
  162.0 1.7 collective-permute-done.43.rest_43_
  164.4 10.9 %shard_map.104 = bf16[768,2048]{1,0:T(8,128)(2,1)} custom-call(s32[2]{0:T(128)} %pad_add_fusion.hops, bf16[768,2048]{1,0:T(8,128)(2,1)} %x.1, f32[768,1]{1,0:T(8,128)} %copy.11.weight, bf16[2048,1024]{1,0:T(8,128)(2,1)} %bitcast.84, bf16[512,2048]{1,0:T(8,128)(2,1)} %bitcast.77, bf16[96,1024]{1,0:T(8,128)(2,1)} %collective-permute-done.2.rest_0_, ...), custom_call_target="tpu_custom_call" | custom-call | flops 4831838208 | bytes 20971520 | tf_op jit(solution)/shard_map/pallas_call | solution.py:123
  (174 shorter events, 19.8 us)
Async XLA Ops:
  2.8 16.6 %copy-start.48 = (s32[8]{0:T(128)S(1)}, s32[8]{0:T(128)}, u32[]{:S(2)}) copy-start(s32[8]{0:T(128)} %constant.70.clone) | copy-start | bytes 100
  2.8 18.5 %copy-start.1 = (bf16[1,512,2048]{2,1,0:T(8,128)(2,1)S(1)}, bf16[1,512,2048]{2,1,0:T(8,128)(2,1)}, u32[]{:S(2)}) copy-start(bf16[1,512,2048]{2,1,0:T(8,128)(2,1)} %param.16) | copy-start | bytes 6291460
  2.8 20.5 %copy-start.47 = (f32[768]{0:T(1024)S(1)}, f32[768]{0:T(1024)}, u32[]{:S(2)}) copy-start(f32[768]{0:T(1024)} %param.11) | copy-start | bytes 9220
  2.8 24.0 %collective-permute-start = (bf16[96,1024]{1,0:T(8,128)(2,1)}, bf16[96,1024]{1,0:T(8,128)(2,1)}, u32[]{:S(2)}, u32[]{:S(2)}) collective-permute-start(bf16[96,1024]{1,0:T(8,128)(2,1)} %get-tuple-element.144), channel_id=1, source_target_pairs={{0,2},{2,4},{4,6},{6,7},{7,5},{5,3},{3,1},{1,0},{8,10},{10,12},{12... | collective-permute-start | bytes 589832 | tf_op jit(solution)/shard_map/ppermute | solution.py:236
  5.9 21.0 %collective-permute-start.1 = (bf16[96,1024]{1,0:T(8,128)(2,1)}, bf16[96,1024]{1,0:T(8,128)(2,1)}, u32[]{:S(2)}, u32[]{:S(2)}) collective-permute-start(bf16[96,1024]{1,0:T(8,128)(2,1)} %get-tuple-element.145), channel_id=1, source_target_pairs={{2,0},{4,2},{6,4},{7,6},{5,7},{3,5},{1,3},{0,1},{10,8},{12,10},{14... | collective-permute-start | bytes 589832 | tf_op jit(solution)/shard_map/ppermute | solution.py:236
  5.9 21.0 %collective-permute-start.2 = (bf16[96,1024]{1,0:T(8,128)(2,1)}, bf16[96,1024]{1,0:T(8,128)(2,1)}, u32[]{:S(2)}, u32[]{:S(2)}) collective-permute-start(bf16[96,1024]{1,0:T(8,128)(2,1)} %get-tuple-element.148), channel_id=1, source_target_pairs={{0,2},{2,4},{4,6},{6,7},{7,5},{5,3},{3,1},{1,0},{8,10},{10,12},{12... | collective-permute-start | bytes 589832 | tf_op jit(solution)/shard_map/ppermute | solution.py:236
  7.9 19.0 %collective-permute-start.3 = (bf16[96,1024]{1,0:T(8,128)(2,1)}, bf16[96,1024]{1,0:T(8,128)(2,1)}, u32[]{:S(2)}, u32[]{:S(2)}) collective-permute-start(bf16[96,1024]{1,0:T(8,128)(2,1)} %get-tuple-element.149), channel_id=1, source_target_pairs={{2,0},{4,2},{6,4},{7,6},{5,7},{3,5},{1,3},{0,1},{10,8},{12,10},{14... | collective-permute-start | bytes 589832 | tf_op jit(solution)/shard_map/ppermute | solution.py:236
  7.9 15.3 %copy-start.43 = (pred[256]{0:T(512)(128)(4,1)}, pred[256]{0:T(512)(128)(4,1)S(1)}, u32[]{:S(2)}) copy-start(pred[256]{0:T(512)(128)(4,1)S(1)} %compare_and_fusion.1) | copy-start | bytes 772
  8.0 15.3 %copy-start.35 = (s32[256]{0:T(256)}, s32[256]{0:T(256)S(1)}, u32[]{:S(2)}) copy-start(s32[256]{0:T(256)S(1)} %broadcast_add_fusion) | copy-start | bytes 3076
  10.5 54.7 %all-to-all-start = ((bf16[16,16,2048]{2,1,0:T(8,128)(2,1)}), bf16[16,16,2048]{2,1,0:T(8,128)(2,1)S(1)}, u32[]{:S(2)}, u32[]{:S(2)}) async-start(bf16[16,16,2048]{2,1,0:T(8,128)(2,1)} %bitcast.25), calls=%async_computation | async-start | bytes 2097152 | tf_op jit(solution)/shard_map/all_to_all | solution.py:189
  29.8 10.4 %collective-permute-start.4 = (bf16[96,1024]{1,0:T(8,128)(2,1)S(1)}, bf16[96,1024]{1,0:T(8,128)(2,1)S(1)}, u32[]{:S(2)}, u32[]{:S(2)}) collective-permute-start(bf16[96,1024]{1,0:T(8,128)(2,1)S(1)} %get-tuple-element.152), channel_id=1, source_target_pairs={{0,2},{2,4},{4,6},{6,7},{7,5},{5,3},{3,1},{1,0},{8,10},{10,12},{12... | collective-permute-start | bytes 589832 | tf_op jit(solution)/shard_map/ppermute | solution.py:236
  31.8 11.9 %collective-permute-start.5 = (bf16[96,1024]{1,0:T(8,128)(2,1)S(1)}, bf16[96,1024]{1,0:T(8,128)(2,1)S(1)}, u32[]{:S(2)}, u32[]{:S(2)}) collective-permute-start(bf16[96,1024]{1,0:T(8,128)(2,1)S(1)} %get-tuple-element.153), channel_id=1, source_target_pairs={{2,0},{4,2},{6,4},{7,6},{5,7},{3,5},{1,3},{0,1},{10,8},{12,10},{14... | collective-permute-start | bytes 589832 | tf_op jit(solution)/shard_map/ppermute | solution.py:236
  33.1 16.7 %collective-permute-start.6 = (bf16[96,1024]{1,0:T(8,128)(2,1)S(1)}, bf16[96,1024]{1,0:T(8,128)(2,1)S(1)}, u32[]{:S(2)}, u32[]{:S(2)}) collective-permute-start(bf16[96,1024]{1,0:T(8,128)(2,1)S(1)} %get-tuple-element.158), channel_id=1, source_target_pairs={{0,2},{2,4},{4,6},{6,7},{7,5},{5,3},{3,1},{1,0},{8,10},{10,12},{12... | collective-permute-start | bytes 589832 | tf_op jit(solution)/shard_map/ppermute | solution.py:236
  35.1 14.8 %collective-permute-start.7 = (bf16[96,1024]{1,0:T(8,128)(2,1)S(1)}, bf16[96,1024]{1,0:T(8,128)(2,1)S(1)}, u32[]{:S(2)}, u32[]{:S(2)}) collective-permute-start(bf16[96,1024]{1,0:T(8,128)(2,1)S(1)} %get-tuple-element.159), channel_id=1, source_target_pairs={{2,0},{4,2},{6,4},{7,6},{5,7},{3,5},{1,3},{0,1},{10,8},{12,10},{14... | collective-permute-start | bytes 589832 | tf_op jit(solution)/shard_map/ppermute | solution.py:236
  40.2 22.2 %copy-start.5 = (bf16[96,1024]{1,0:T(8,128)(2,1)}, bf16[96,1024]{1,0:T(8,128)(2,1)S(1)}, u32[]{:S(2)}) copy-start(bf16[96,1024]{1,0:T(8,128)(2,1)S(1)} %collective-permute-done.4.rest_4_) | copy-start | bytes 589828
  43.7 18.7 %copy-start.6 = (bf16[96,1024]{1,0:T(8,128)(2,1)}, bf16[96,1024]{1,0:T(8,128)(2,1)S(1)}, u32[]{:S(2)}) copy-start(bf16[96,1024]{1,0:T(8,128)(2,1)S(1)} %collective-permute-done.5.rest_5_) | copy-start | bytes 589828
  44.9 8.8 %collective-permute-start.8 = (bf16[96,1024]{1,0:T(8,128)(2,1)S(1)}, bf16[96,1024]{1,0:T(8,128)(2,1)S(1)}, u32[]{:S(2)}, u32[]{:S(2)}) collective-permute-start(bf16[96,1024]{1,0:T(8,128)(2,1)S(1)} %get-tuple-element.162), channel_id=1, source_target_pairs={{0,2},{2,4},{4,6},{6,7},{7,5},{5,3},{3,1},{1,0},{8,10},{10,12},{12... | collective-permute-start | bytes 589832 | tf_op jit(solution)/shard_map/ppermute | solution.py:236
  49.9 5.7 %collective-permute-start.9 = (bf16[96,1024]{1,0:T(8,128)(2,1)S(1)}, bf16[96,1024]{1,0:T(8,128)(2,1)S(1)}, u32[]{:S(2)}, u32[]{:S(2)}) collective-permute-start(bf16[96,1024]{1,0:T(8,128)(2,1)S(1)} %get-tuple-element.163), channel_id=1, source_target_pairs={{2,0},{4,2},{6,4},{7,6},{5,7},{3,5},{1,3},{0,1},{10,8},{12,10},{14... | collective-permute-start | bytes 589832 | tf_op jit(solution)/shard_map/ppermute | solution.py:236
  51.1 7.7 %collective-permute-start.10 = (bf16[96,1024]{1,0:T(8,128)(2,1)S(1)}, bf16[96,1024]{1,0:T(8,128)(2,1)S(1)}, u32[]{:S(2)}, u32[]{:S(2)}) collective-permute-start(bf16[96,1024]{1,0:T(8,128)(2,1)S(1)} %get-tuple-element.166), channel_id=1, source_target_pairs={{0,2},{2,4},{4,6},{6,7},{7,5},{5,3},{3,1},{1,0},{8,10},{10,12},{12... | collective-permute-start | bytes 589832 | tf_op jit(solution)/shard_map/ppermute | solution.py:236
  53.6 6.9 %collective-permute-start.11 = (bf16[96,1024]{1,0:T(8,128)(2,1)S(1)}, bf16[96,1024]{1,0:T(8,128)(2,1)S(1)}, u32[]{:S(2)}, u32[]{:S(2)}) collective-permute-start(bf16[96,1024]{1,0:T(8,128)(2,1)S(1)} %get-tuple-element.167), channel_id=1, source_target_pairs={{2,0},{4,2},{6,4},{7,6},{5,7},{3,5},{1,3},{0,1},{10,8},{12,10},{14... | collective-permute-start | bytes 589832 | tf_op jit(solution)/shard_map/ppermute | solution.py:236
  56.7 7.7 %collective-permute-start.12 = (bf16[96,1024]{1,0:T(8,128)(2,1)S(1)}, bf16[96,1024]{1,0:T(8,128)(2,1)S(1)}, u32[]{:S(2)}, u32[]{:S(2)}) collective-permute-start(bf16[96,1024]{1,0:T(8,128)(2,1)S(1)} %get-tuple-element.170), channel_id=1, source_target_pairs={{0,2},{2,4},{4,6},{6,7},{7,5},{5,3},{3,1},{1,0},{8,10},{10,12},{12... | collective-permute-start | bytes 589832 | tf_op jit(solution)/shard_map/ppermute | solution.py:236
  57.8 7.3 %collective-permute-start.13 = (bf16[96,1024]{1,0:T(8,128)(2,1)S(1)}, bf16[96,1024]{1,0:T(8,128)(2,1)}, u32[]{:S(2)}, u32[]{:S(2)}) collective-permute-start(bf16[96,1024]{1,0:T(8,128)(2,1)S(1)} %get-tuple-element.171), channel_id=1, source_target_pairs={{2,0},{4,2},{6,4},{7,6},{5,7},{3,5},{1,3},{0,1},{10,8},{12,10},{14... | collective-permute-start | bytes 589832 | tf_op jit(solution)/shard_map/ppermute | solution.py:236
  62.4 12.0 %collective-permute-start.14 = (bf16[96,1024]{1,0:T(8,128)(2,1)}, bf16[96,1024]{1,0:T(8,128)(2,1)}, u32[]{:S(2)}, u32[]{:S(2)}) collective-permute-start(bf16[96,1024]{1,0:T(8,128)(2,1)} %get-tuple-element.174), channel_id=1, source_target_pairs={{0,2},{2,4},{4,6},{6,7},{7,5},{5,3},{3,1},{1,0},{8,10},{10,12},{12... | collective-permute-start | bytes 589832 | tf_op jit(solution)/shard_map/ppermute | solution.py:236
  63.4 11.0 %collective-permute-start.15 = (bf16[96,1024]{1,0:T(8,128)(2,1)}, bf16[96,1024]{1,0:T(8,128)(2,1)}, u32[]{:S(2)}, u32[]{:S(2)}) collective-permute-start(bf16[96,1024]{1,0:T(8,128)(2,1)} %get-tuple-element.175), channel_id=1, source_target_pairs={{2,0},{4,2},{6,4},{7,6},{5,7},{3,5},{1,3},{0,1},{10,8},{12,10},{14... | collective-permute-start | bytes 589832 | tf_op jit(solution)/shard_map/ppermute | solution.py:236
  67.2 15.3 %collective-permute-start.16 = (bf16[96,1024]{1,0:T(8,128)(2,1)}, bf16[96,1024]{1,0:T(8,128)(2,1)}, u32[]{:S(2)}, u32[]{:S(2)}) collective-permute-start(bf16[96,1024]{1,0:T(8,128)(2,1)} %get-tuple-element.180), channel_id=1, source_target_pairs={{0,2},{2,4},{4,6},{6,7},{7,5},{5,3},{3,1},{1,0},{8,10},{10,12},{12... | collective-permute-start | bytes 589832 | tf_op jit(solution)/shard_map/ppermute | solution.py:236
  68.2 14.3 %collective-permute-start.17 = (bf16[96,1024]{1,0:T(8,128)(2,1)}, bf16[96,1024]{1,0:T(8,128)(2,1)}, u32[]{:S(2)}, u32[]{:S(2)}) collective-permute-start(bf16[96,1024]{1,0:T(8,128)(2,1)} %get-tuple-element.181), channel_id=1, source_target_pairs={{2,0},{4,2},{6,4},{7,6},{5,7},{3,5},{1,3},{0,1},{10,8},{12,10},{14... | collective-permute-start | bytes 589832 | tf_op jit(solution)/shard_map/ppermute | solution.py:236
  74.4 75.2 %all-to-all-start.1 = ((bf16[16,16,2048]{2,1,0:T(8,128)(2,1)}), bf16[16,16,2048]{2,1,0:T(8,128)(2,1)S(1)}, u32[]{:S(2)}, u32[]{:S(2)}) async-start(bf16[16,16,2048]{2,1,0:T(8,128)(2,1)} %bitcast.88), calls=%async_computation.1 | async-start | bytes 2097152 | tf_op jit(solution)/shard_map/all_to_all | solution.py:223
  79.1 23.3 %copy-start.30 = (bf16[32,1024]{1,0:T(8,128)(2,1)S(1)}, bf16[32,1024]{1,0:T(8,128)(2,1)}, u32[]{:S(2)}) copy-start(bf16[32,1024]{1,0:T(8,128)(2,1)} %get-tuple-element.324) | copy-start | bytes 196612
  80.4 21.3 %collective-permute-start.18 = (bf16[96,1024]{1,0:T(8,128)(2,1)S(1)}, bf16[96,1024]{1,0:T(8,128)(2,1)S(1)}, u32[]{:S(2)}, u32[]{:S(2)}) collective-permute-start(bf16[96,1024]{1,0:T(8,128)(2,1)S(1)} %get-tuple-element.187), channel_id=1, source_target_pairs={{0,2},{2,4},{4,6},{6,7},{7,5},{5,3},{3,1},{1,0},{8,10},{10,12},{12... | collective-permute-start | bytes 589832 | tf_op jit(solution)/shard_map/ppermute | solution.py:236
  82.4 20.0 %collective-permute-start.19 = (bf16[96,1024]{1,0:T(8,128)(2,1)S(1)}, bf16[96,1024]{1,0:T(8,128)(2,1)S(1)}, u32[]{:S(2)}, u32[]{:S(2)}) collective-permute-start(bf16[96,1024]{1,0:T(8,128)(2,1)S(1)} %get-tuple-element.188), channel_id=1, source_target_pairs={{2,0},{4,2},{6,4},{7,6},{5,7},{3,5},{1,3},{0,1},{10,8},{12,10},{14... | collective-permute-start | bytes 589832 | tf_op jit(solution)/shard_map/ppermute | solution.py:236
  84.5 26.5 %collective-permute-start.20 = (bf16[96,1024]{1,0:T(8,128)(2,1)S(1)}, bf16[96,1024]{1,0:T(8,128)(2,1)S(1)}, u32[]{:S(2)}, u32[]{:S(2)}) collective-permute-start(bf16[96,1024]{1,0:T(8,128)(2,1)S(1)} %broadcast_select_fusion.23), channel_id=1, source_target_pairs={{0,2},{2,4},{4,6},{6,7},{7,5},{5,3},{3,1},{1,0},{8,10},{10,12},{12... | collective-permute-start | bytes 589832 | tf_op jit(solution)/shard_map/ppermute | solution.py:236
  86.5 24.5 %collective-permute-start.21 = (bf16[96,1024]{1,0:T(8,128)(2,1)S(1)}, bf16[96,1024]{1,0:T(8,128)(2,1)S(1)}, u32[]{:S(2)}, u32[]{:S(2)}) collective-permute-start(bf16[96,1024]{1,0:T(8,128)(2,1)S(1)} %broadcast_select_fusion.22), channel_id=1, source_target_pairs={{2,0},{4,2},{6,4},{7,6},{5,7},{3,5},{1,3},{0,1},{10,8},{12,10},{14... | collective-permute-start | bytes 589832 | tf_op jit(solution)/shard_map/ppermute | solution.py:236
  101.7 20.4 %copy-start.2 = (bf16[96,1024]{1,0:T(8,128)(2,1)}, bf16[96,1024]{1,0:T(8,128)(2,1)S(1)}, u32[]{:S(2)}) copy-start(bf16[96,1024]{1,0:T(8,128)(2,1)S(1)} %collective-permute-done.18.rest_18_) | copy-start | bytes 589828
  102.4 19.7 %copy-start.3 = (bf16[96,1024]{1,0:T(8,128)(2,1)}, bf16[96,1024]{1,0:T(8,128)(2,1)S(1)}, u32[]{:S(2)}) copy-start(bf16[96,1024]{1,0:T(8,128)(2,1)S(1)} %collective-permute-done.19.rest_19_) | copy-start | bytes 589828
  102.5 12.7 %collective-permute-start.22 = (bf16[96,1024]{1,0:T(8,128)(2,1)S(1)}, bf16[96,1024]{1,0:T(8,128)(2,1)S(1)}, u32[]{:S(2)}, u32[]{:S(2)}) collective-permute-start(bf16[96,1024]{1,0:T(8,128)(2,1)S(1)} %broadcast_select_fusion.21), channel_id=1, source_target_pairs={{0,2},{2,4},{4,6},{6,7},{7,5},{5,3},{3,1},{1,0},{8,10},{10,12},{12... | collective-permute-start | bytes 589832 | tf_op jit(solution)/shard_map/ppermute | solution.py:236
  111.0 5.7 %collective-permute-start.23 = (bf16[96,1024]{1,0:T(8,128)(2,1)S(1)}, bf16[96,1024]{1,0:T(8,128)(2,1)S(1)}, u32[]{:S(2)}, u32[]{:S(2)}) collective-permute-start(bf16[96,1024]{1,0:T(8,128)(2,1)S(1)} %broadcast_select_fusion.20), channel_id=1, source_target_pairs={{2,0},{4,2},{6,4},{7,6},{5,7},{3,5},{1,3},{0,1},{10,8},{12,10},{14... | collective-permute-start | bytes 589832 | tf_op jit(solution)/shard_map/ppermute | solution.py:236
  111.0 16.3 %copy-start.14 = (bf16[96,1024]{1,0:T(8,128)(2,1)}, bf16[96,1024]{1,0:T(8,128)(2,1)S(1)}, u32[]{:S(2)}) copy-start(bf16[96,1024]{1,0:T(8,128)(2,1)S(1)} %collective-permute-done.20.rest_20_) | copy-start | bytes 589828
  111.0 16.3 %copy-start.15 = (bf16[96,1024]{1,0:T(8,128)(2,1)}, bf16[96,1024]{1,0:T(8,128)(2,1)S(1)}, u32[]{:S(2)}) copy-start(bf16[96,1024]{1,0:T(8,128)(2,1)S(1)} %collective-permute-done.21.rest_21_) | copy-start | bytes 589828
  111.1 9.4 %collective-permute-start.24 = (bf16[96,1024]{1,0:T(8,128)(2,1)S(1)}, bf16[96,1024]{1,0:T(8,128)(2,1)S(1)}, u32[]{:S(2)}, u32[]{:S(2)}) collective-permute-start(bf16[96,1024]{1,0:T(8,128)(2,1)S(1)} %get-tuple-element.199), channel_id=1, source_target_pairs={{0,2},{2,4},{4,6},{6,7},{7,5},{5,3},{3,1},{1,0},{8,10},{10,12},{12... | collective-permute-start | bytes 589832 | tf_op jit(solution)/shard_map/ppermute | solution.py:236
  115.2 5.7 %collective-permute-start.25 = (bf16[96,1024]{1,0:T(8,128)(2,1)S(1)}, bf16[96,1024]{1,0:T(8,128)(2,1)S(1)}, u32[]{:S(2)}, u32[]{:S(2)}) collective-permute-start(bf16[96,1024]{1,0:T(8,128)(2,1)S(1)} %get-tuple-element.200), channel_id=1, source_target_pairs={{2,0},{4,2},{6,4},{7,6},{5,7},{3,5},{1,3},{0,1},{10,8},{12,10},{14... | collective-permute-start | bytes 589832 | tf_op jit(solution)/shard_map/ppermute | solution.py:236
  115.2 17.1 %copy-start.16 = (bf16[96,1024]{1,0:T(8,128)(2,1)}, bf16[96,1024]{1,0:T(8,128)(2,1)S(1)}, u32[]{:S(2)}) copy-start(bf16[96,1024]{1,0:T(8,128)(2,1)S(1)} %collective-permute-done.22.rest_22_) | copy-start | bytes 589828
  116.7 15.6 %copy-start.17 = (bf16[96,1024]{1,0:T(8,128)(2,1)}, bf16[96,1024]{1,0:T(8,128)(2,1)S(1)}, u32[]{:S(2)}) copy-start(bf16[96,1024]{1,0:T(8,128)(2,1)S(1)} %collective-permute-done.23.rest_23_) | copy-start | bytes 589828
  117.9 6.4 %collective-permute-start.26 = (bf16[96,1024]{1,0:T(8,128)(2,1)S(1)}, bf16[96,1024]{1,0:T(8,128)(2,1)S(1)}, u32[]{:S(2)}, u32[]{:S(2)}) collective-permute-start(bf16[96,1024]{1,0:T(8,128)(2,1)S(1)} %get-tuple-element.203), channel_id=1, source_target_pairs={{0,2},{2,4},{4,6},{6,7},{7,5},{5,3},{3,1},{1,0},{8,10},{10,12},{12... | collective-permute-start | bytes 589832 | tf_op jit(solution)/shard_map/ppermute | solution.py:236
  120.5 5.7 %collective-permute-start.27 = (bf16[96,1024]{1,0:T(8,128)(2,1)S(1)}, bf16[96,1024]{1,0:T(8,128)(2,1)S(1)}, u32[]{:S(2)}, u32[]{:S(2)}) collective-permute-start(bf16[96,1024]{1,0:T(8,128)(2,1)S(1)} %get-tuple-element.204), channel_id=1, source_target_pairs={{2,0},{4,2},{6,4},{7,6},{5,7},{3,5},{1,3},{0,1},{10,8},{12,10},{14... | collective-permute-start | bytes 589832 | tf_op jit(solution)/shard_map/ppermute | solution.py:236
  120.5 16.0 %copy-start.18 = (bf16[96,1024]{1,0:T(8,128)(2,1)}, bf16[96,1024]{1,0:T(8,128)(2,1)S(1)}, u32[]{:S(2)}) copy-start(bf16[96,1024]{1,0:T(8,128)(2,1)S(1)} %collective-permute-done.24.rest_24_) | copy-start | bytes 589828
  120.9 15.6 %copy-start.19 = (bf16[96,1024]{1,0:T(8,128)(2,1)}, bf16[96,1024]{1,0:T(8,128)(2,1)S(1)}, u32[]{:S(2)}) copy-start(bf16[96,1024]{1,0:T(8,128)(2,1)S(1)} %collective-permute-done.25.rest_25_) | copy-start | bytes 589828
  122.1 7.4 %collective-permute-start.28 = (bf16[96,1024]{1,0:T(8,128)(2,1)S(1)}, bf16[96,1024]{1,0:T(8,128)(2,1)S(1)}, u32[]{:S(2)}, u32[]{:S(2)}) collective-permute-start(bf16[96,1024]{1,0:T(8,128)(2,1)S(1)} %get-tuple-element.207), channel_id=1, source_target_pairs={{0,2},{2,4},{4,6},{6,7},{7,5},{5,3},{3,1},{1,0},{8,10},{10,12},{12... | collective-permute-start | bytes 589832 | tf_op jit(solution)/shard_map/ppermute | solution.py:236
  124.3 6.9 %collective-permute-start.29 = (bf16[96,1024]{1,0:T(8,128)(2,1)S(1)}, bf16[96,1024]{1,0:T(8,128)(2,1)S(1)}, u32[]{:S(2)}, u32[]{:S(2)}) collective-permute-start(bf16[96,1024]{1,0:T(8,128)(2,1)S(1)} %get-tuple-element.208), channel_id=1, source_target_pairs={{2,0},{4,2},{6,4},{7,6},{5,7},{3,5},{1,3},{0,1},{10,8},{12,10},{14... | collective-permute-start | bytes 589832 | tf_op jit(solution)/shard_map/ppermute | solution.py:236
  124.3 17.0 %copy-start.20 = (bf16[96,1024]{1,0:T(8,128)(2,1)}, bf16[96,1024]{1,0:T(8,128)(2,1)S(1)}, u32[]{:S(2)}) copy-start(bf16[96,1024]{1,0:T(8,128)(2,1)S(1)} %collective-permute-done.26.rest_26_) | copy-start | bytes 589828
  127.4 7.0 %collective-permute-start.30 = (bf16[96,1024]{1,0:T(8,128)(2,1)S(1)}, bf16[96,1024]{1,0:T(8,128)(2,1)S(1)}, u32[]{:S(2)}, u32[]{:S(2)}) collective-permute-start(bf16[96,1024]{1,0:T(8,128)(2,1)S(1)} %get-tuple-element.211), channel_id=1, source_target_pairs={{0,2},{2,4},{4,6},{6,7},{7,5},{5,3},{3,1},{1,0},{8,10},{10,12},{12... | collective-permute-start | bytes 589832 | tf_op jit(solution)/shard_map/ppermute | solution.py:236
  128.5 6.8 %collective-permute-start.31 = (bf16[96,1024]{1,0:T(8,128)(2,1)S(1)}, bf16[96,1024]{1,0:T(8,128)(2,1)S(1)}, u32[]{:S(2)}, u32[]{:S(2)}) collective-permute-start(bf16[96,1024]{1,0:T(8,128)(2,1)S(1)} %get-tuple-element.212), channel_id=1, source_target_pairs={{2,0},{4,2},{6,4},{7,6},{5,7},{3,5},{1,3},{0,1},{10,8},{12,10},{14... | collective-permute-start | bytes 589832 | tf_op jit(solution)/shard_map/ppermute | solution.py:236
  131.1 15.7 %copy-start.23 = (bf16[96,1024]{1,0:T(8,128)(2,1)}, bf16[96,1024]{1,0:T(8,128)(2,1)S(1)}, u32[]{:S(2)}) copy-start(bf16[96,1024]{1,0:T(8,128)(2,1)S(1)} %collective-permute-done.29.rest_29_) | copy-start | bytes 589828
  132.3 6.9 %collective-permute-start.32 = (bf16[96,1024]{1,0:T(8,128)(2,1)S(1)}, bf16[96,1024]{1,0:T(8,128)(2,1)S(1)}, u32[]{:S(2)}, u32[]{:S(2)}) collective-permute-start(bf16[96,1024]{1,0:T(8,128)(2,1)S(1)} %get-tuple-element.215), channel_id=1, source_target_pairs={{0,2},{2,4},{4,6},{6,7},{7,5},{5,3},{3,1},{1,0},{8,10},{10,12},{12... | collective-permute-start | bytes 589832 | tf_op jit(solution)/shard_map/ppermute | solution.py:236
  133.3 6.8 %collective-permute-start.33 = (bf16[96,1024]{1,0:T(8,128)(2,1)S(1)}, bf16[96,1024]{1,0:T(8,128)(2,1)S(1)}, u32[]{:S(2)}, u32[]{:S(2)}) collective-permute-start(bf16[96,1024]{1,0:T(8,128)(2,1)S(1)} %get-tuple-element.216), channel_id=1, source_target_pairs={{2,0},{4,2},{6,4},{7,6},{5,7},{3,5},{1,3},{0,1},{10,8},{12,10},{14... | collective-permute-start | bytes 589832 | tf_op jit(solution)/shard_map/ppermute | solution.py:236
  136.5 7.3 %collective-permute-start.34 = (bf16[96,1024]{1,0:T(8,128)(2,1)S(1)}, bf16[96,1024]{1,0:T(8,128)(2,1)S(1)}, u32[]{:S(2)}, u32[]{:S(2)}) collective-permute-start(bf16[96,1024]{1,0:T(8,128)(2,1)S(1)} %get-tuple-element.219), channel_id=1, source_target_pairs={{0,2},{2,4},{4,6},{6,7},{7,5},{5,3},{3,1},{1,0},{8,10},{10,12},{12... | collective-permute-start | bytes 589832 | tf_op jit(solution)/shard_map/ppermute | solution.py:236
  137.5 7.4 %collective-permute-start.35 = (bf16[96,1024]{1,0:T(8,128)(2,1)S(1)}, bf16[96,1024]{1,0:T(8,128)(2,1)S(1)}, u32[]{:S(2)}, u32[]{:S(2)}) collective-permute-start(bf16[96,1024]{1,0:T(8,128)(2,1)S(1)} %get-tuple-element.220), channel_id=1, source_target_pairs={{2,0},{4,2},{6,4},{7,6},{5,7},{3,5},{1,3},{0,1},{10,8},{12,10},{14... | collective-permute-start | bytes 589832 | tf_op jit(solution)/shard_map/ppermute | solution.py:236
  141.3 7.5 %collective-permute-start.36 = (bf16[96,1024]{1,0:T(8,128)(2,1)S(1)}, bf16[96,1024]{1,0:T(8,128)(2,1)S(1)}, u32[]{:S(2)}, u32[]{:S(2)}) collective-permute-start(bf16[96,1024]{1,0:T(8,128)(2,1)S(1)} %get-tuple-element.223), channel_id=1, source_target_pairs={{0,2},{2,4},{4,6},{6,7},{7,5},{5,3},{3,1},{1,0},{8,10},{10,12},{12... | collective-permute-start | bytes 589832 | tf_op jit(solution)/shard_map/ppermute | solution.py:236
  141.9 7.6 %collective-permute-start.37 = (bf16[96,1024]{1,0:T(8,128)(2,1)S(1)}, bf16[96,1024]{1,0:T(8,128)(2,1)}, u32[]{:S(2)}, u32[]{:S(2)}) collective-permute-start(bf16[96,1024]{1,0:T(8,128)(2,1)S(1)} %get-tuple-element.224), channel_id=1, source_target_pairs={{2,0},{4,2},{6,4},{7,6},{5,7},{3,5},{1,3},{0,1},{10,8},{12,10},{14... | collective-permute-start | bytes 589832 | tf_op jit(solution)/shard_map/ppermute | solution.py:236
  146.8 8.0 %collective-permute-start.38 = (bf16[96,1024]{1,0:T(8,128)(2,1)}, bf16[96,1024]{1,0:T(8,128)(2,1)}, u32[]{:S(2)}, u32[]{:S(2)}) collective-permute-start(bf16[96,1024]{1,0:T(8,128)(2,1)} %get-tuple-element.227), channel_id=1, source_target_pairs={{0,2},{2,4},{4,6},{6,7},{7,5},{5,3},{3,1},{1,0},{8,10},{10,12},{12... | collective-permute-start | bytes 589832 | tf_op jit(solution)/shard_map/ppermute | solution.py:236
  147.4 7.7 %collective-permute-start.39 = (bf16[96,1024]{1,0:T(8,128)(2,1)}, bf16[96,1024]{1,0:T(8,128)(2,1)}, u32[]{:S(2)}, u32[]{:S(2)}) collective-permute-start(bf16[96,1024]{1,0:T(8,128)(2,1)} %get-tuple-element.228), channel_id=1, source_target_pairs={{2,0},{4,2},{6,4},{7,6},{5,7},{3,5},{1,3},{0,1},{10,8},{12,10},{14... | collective-permute-start | bytes 589832 | tf_op jit(solution)/shard_map/ppermute | solution.py:236
  151.7 8.1 %collective-permute-start.40 = (bf16[96,1024]{1,0:T(8,128)(2,1)S(1)}, bf16[96,1024]{1,0:T(8,128)(2,1)S(1)}, u32[]{:S(2)}, u32[]{:S(2)}) collective-permute-start(bf16[96,1024]{1,0:T(8,128)(2,1)S(1)} %broadcast_select_fusion.3), channel_id=1, source_target_pairs={{0,2},{2,4},{4,6},{6,7},{7,5},{5,3},{3,1},{1,0},{8,10},{10,12},{12... | collective-permute-start | bytes 589832 | tf_op jit(solution)/shard_map/ppermute | solution.py:236
  154.1 5.8 %collective-permute-start.41 = (bf16[96,1024]{1,0:T(8,128)(2,1)S(1)}, bf16[96,1024]{1,0:T(8,128)(2,1)S(1)}, u32[]{:S(2)}, u32[]{:S(2)}) collective-permute-start(bf16[96,1024]{1,0:T(8,128)(2,1)S(1)} %broadcast_select_fusion.2), channel_id=1, source_target_pairs={{2,0},{4,2},{6,4},{7,6},{5,7},{3,5},{1,3},{0,1},{10,8},{12,10},{14... | collective-permute-start | bytes 589832 | tf_op jit(solution)/shard_map/ppermute | solution.py:236
  156.3 5.7 %collective-permute-start.42 = (bf16[96,1024]{1,0:T(8,128)(2,1)S(1)}, bf16[96,1024]{1,0:T(8,128)(2,1)S(1)}, u32[]{:S(2)}, u32[]{:S(2)}) collective-permute-start(bf16[96,1024]{1,0:T(8,128)(2,1)S(1)} %get-tuple-element.238), channel_id=1, source_target_pairs={{0,2},{2,4},{4,6},{6,7},{7,5},{5,3},{3,1},{1,0},{8,10},{10,12},{12... | collective-permute-start | bytes 589832 | tf_op jit(solution)/shard_map/ppermute | solution.py:236
  158.0 5.7 %collective-permute-start.43 = (bf16[96,1024]{1,0:T(8,128)(2,1)S(1)}, bf16[96,1024]{1,0:T(8,128)(2,1)S(1)}, u32[]{:S(2)}, u32[]{:S(2)}) collective-permute-start(bf16[96,1024]{1,0:T(8,128)(2,1)S(1)} %get-tuple-element.239), channel_id=1, source_target_pairs={{2,0},{4,2},{6,4},{7,6},{5,7},{3,5},{1,3},{0,1},{10,8},{12,10},{14... | collective-permute-start | bytes 589832 | tf_op jit(solution)/shard_map/ppermute | solution.py:236
  (32 other events, 280.8 us)
